TPU v7x, 32 devices: a whole 2x2x4 slice. The times are simulated.
32 devices in a mesh: ch: 8 (over z, x), tok: 4 (over y, core).
Axes of the slice: x: 2, y: 2, z: 4, core: 2. Of those that a mesh axis runs over, the one named last changes fastest.
Arguments:
- inputs: bfloat16 [4, 768, 4096], P(None, 'ch', 'tok'), may hold values from -6 to 6
- out_grad: bfloat16 [4, 768, 4096], P(None, 'ch', 'tok'), may hold values from -6 to 6
- seq_lengths: int32 [4], replicated, may hold values from 2560 to 4096, as said below
- ema_alpha: float32 [768, 16], P('ch'), may hold values from -0.85 to 0.85
- ema_delta: float32 [768, 16], P('ch'), may hold values from -14 to -1.9
- ema_beta: float32 [768, 16], P('ch'), may hold values from -3 to 3
- ema_eta: float32 [768, 16], P('ch'), may hold values from -1.5 to 1.5
- ema_omega: float32 [768], P('ch'), may hold values from -2 to 2
- w_mix: bfloat16 [768, 3200], replicated, may hold values from -0.21875 to 0.21875
- b_mix: float32 [3200], replicated, may hold values from -1.5 to 1.5
- w_value: bfloat16 [768, 1536], replicated, may hold values from -0.21875 to 0.21875
- b_value: float32 [1536], replicated, may hold values from -1.5 to 1.5
- w_out: bfloat16 [1536, 768], replicated, may hold values from -0.3125 to 0.3125
- b_out: float32 [768], replicated, may hold values from -1.5 to 1.5
- qk_scale: float32 [2, 128], replicated, may hold values from 0.25 to 1.75
- qk_shift: float32 [2, 128], replicated, may hold values from -1.5 to 1.5
- ln_gain: float32 [768], replicated, may hold values from 0.5 to 1.5
- ln_bias: float32 [768], replicated, may hold values from -1.5 to 1.5
- w_up: bfloat16 [768, 1536], replicated, may hold values from -0.21875 to 0.21875
- b_up: float32 [1536], replicated, may hold values from -1.5 to 1.5
- w_down: bfloat16 [1536, 768], replicated, may hold values from -0.21875 to 0.21875
- b_down: float32 [768], replicated, may hold values from -1.5 to 1.5
Outputs:
- output: bfloat16 [4, 768, 4096], P(None, 'ch', 'tok')
- input_grad: float32 [4, 768, 4096], P(None, 'ch', 'tok')
- grad_ema_alpha: float32 [768, 16], P('ch')
- grad_ema_delta: float32 [768, 16], P('ch')
- grad_ema_beta: float32 [768, 16], P('ch')
- grad_ema_eta: float32 [768, 16], P('ch')
- grad_ema_omega: float32 [768], P('ch')
- grad_w_mix: float32 [768, 3200], P('ch')
- grad_b_mix: float32 [3200], replicated
- grad_w_value: float32 [768, 1536], P('ch')
- grad_b_value: float32 [1536], replicated
- grad_w_out: float32 [1536, 768], P('ch')
- grad_b_out: float32 [768], replicated
- grad_qk_scale: float32 [2, 128], replicated
- grad_qk_shift: float32 [2, 128], replicated
- grad_ln_gain: float32 [768], replicated
- grad_ln_bias: float32 [768], replicated
- grad_w_up: float32 [768, 1536], P('ch')
- grad_b_up: float32 [1536], replicated
- grad_w_down: float32 [1536, 768], P('ch')
- grad_b_down: float32 [768], replicated
Inputs may be any that keep to these rules, and one draw needn't show every extreme that they name: `seq_lengths`: every sequence but one, chosen by the seed, has 4096 live positions; that one has 2560 or more.
All inputs are finite; a program needn't handle non-finite values.
Results may differ from a plain program's by a relative error of at most 0.025.
The roundings to bfloat16 on the way count: a program that leaves them out, or rounds other values in their place, can miss the bound.
Values may be sent and summed in bfloat16 or wider, within the bound.
No kernel may reach another device: no remote copies, remote signals or barrier semaphores. Data moves between devices by JAX's collectives and lax.ppermute only.
A program may use at most 192 MiB of HBM per device.

v0:
```python
import jax
import jax.numpy as jnp
from jax import lax
from jax.sharding import PartitionSpec as P

GROUP = 128


highest = lax.Precision.HIGHEST


def prefix(shard, axis, combine, identity, reverse):
    size, position = (lax.axis_size(axis), lax.axis_index(axis))
    everything = jax.tree.map(lambda part: lax.all_gather(part, axis), shard)
    start = jax.tree.map(
        lambda part, zero: jnp.broadcast_to(jnp.asarray(zero, part.dtype), part.shape),
        shard,
        identity,
    )

    def lap(k, before):
        at = size - 1 - k if reverse else k
        reached = at > position if reverse else at < position
        new = combine(before, jax.tree.map(lambda part: part[at], everything))
        return jax.tree.map(lambda a, b: jnp.where(reached, a, b), new, before)

    return lax.fori_loop(0, size, lap, start)


def silu_slope(preact):
    sigma = jax.nn.sigmoid(preact)
    return sigma * (1.0 + preact * (1.0 - sigma))


def decay_logs(alpha_logit, delta_logit):
    return jnp.log1p(-jax.nn.sigmoid(alpha_logit) * jax.nn.sigmoid(delta_logit))


def ema_core(seq_f, alpha_logit, delta_logit, beta, eta, omega, state_in):
    nseq_count, channels, local_len = seq_f.shape
    blocks_n = local_len // GROUP
    log_decay = decay_logs(alpha_logit, delta_logit)
    scaled = jax.nn.sigmoid(alpha_logit) * beta
    offsets = jnp.arange(GROUP, dtype=jnp.float32)
    powers = jnp.exp(offsets[None, None, :] * log_decay[:, :, None])
    kernel = jnp.einsum("dj,djt->dt", eta * scaled, powers, precision=highest)
    lag = offsets[:, None] - offsets[None, :]
    onehot = (lag[None] == offsets[:, None, None]).astype(jnp.float32)
    toeplitz = jnp.einsum("dm,mts->dts", kernel, onehot, precision=highest)
    blocks = seq_f.reshape(nseq_count, channels, blocks_n, GROUP)
    inner = jnp.einsum("dts,ndbs->ndbt", toeplitz, blocks, precision=highest)
    state_pow = scaled[:, :, None] * jnp.flip(powers, axis=2)
    running = jnp.einsum("djs,ndbs->ndbj", state_pow, blocks, precision=highest)
    span = 1
    while span < blocks_n:
        factor = jnp.exp(span * GROUP * log_decay)
        moved = jnp.pad(running, ((0, 0), (0, 0), (span, 0), (0, 0)))[:, :, :blocks_n]
        running = running + factor[None, :, None, :] * moved
        span = span * 2
    starts = jnp.pad(running, ((0, 0), (0, 0), (1, 0), (0, 0)))[:, :, :blocks_n]
    group_ids = jnp.arange(blocks_n, dtype=jnp.float32)
    entry = jnp.exp(group_ids[None, :, None] * (GROUP * log_decay)[:, None, :])
    starts = starts + entry[None] * state_in[:, :, None, :]
    carry_pow = eta[:, :, None] * powers * jnp.exp(log_decay)[:, :, None]
    smooth = inner + jnp.einsum("djt,ndbj->ndbt", carry_pow, starts, precision=highest)
    smooth = smooth.reshape(nseq_count, channels, local_len)
    return jax.nn.silu(smooth + omega[None, :, None] * seq_f)


def state_advance(seq_f, alpha_logit, delta_logit, beta, state_in):
    local_len = seq_f.shape[2]
    log_decay = decay_logs(alpha_logit, delta_logit)
    scaled = jax.nn.sigmoid(alpha_logit) * beta
    reverse_pos = jnp.arange(local_len - 1, -1, -1, dtype=jnp.float32)
    weights = scaled[:, :, None] * jnp.exp(reverse_pos[None, None, :] * log_decay[:, :, None])
    fresh = jnp.einsum("djs,nds->ndj", weights, seq_f, precision=highest)
    return jnp.exp(local_len * log_decay)[None] * state_in + fresh


def chain_combine(earlier, later):
    return (earlier[0] * later[0], later[0][None] * earlier[1] + later[1])


def to_rows(columns):
    return jnp.swapaxes(columns, 1, 2).reshape(-1, columns.shape[1])


def from_rows(table, nseq_count):
    return jnp.swapaxes(table.reshape(nseq_count, -1, table.shape[1]), 1, 2)


def local(
    inputs,
    out_grad,
    seq_lengths,
    ema_alpha,
    ema_delta,
    ema_beta,
    ema_eta,
    ema_omega,
    w_mix,
    b_mix,
    w_value,
    b_value,
    w_out,
    b_out,
    qk_scale,
    qk_shift,
    ln_gain,
    ln_bias,
    w_up,
    b_up,
    w_down,
    b_down,
):
    nseq_count, channels, local_len = inputs.shape
    width = w_mix.shape[0]
    zwidth = qk_scale.shape[1]
    vwidth = w_value.shape[1]
    scale = zwidth ** (-0.5)
    tok_index = lax.axis_index("tok")
    seq_f = inputs.astype(jnp.float32)
    log_total = local_len * decay_logs(ema_alpha, ema_delta)
    decay_all = jnp.exp(log_total)
    zero_state = jnp.zeros((nseq_count, channels, ema_alpha.shape[1]), jnp.float32)
    state_dev = state_advance(seq_f, ema_alpha, ema_delta, ema_beta, zero_state)
    state_in = prefix(
        (decay_all, state_dev), "tok", chain_combine, (jnp.ones_like(decay_all), zero_state), False
    )[1]
    activ = ema_core(seq_f, ema_alpha, ema_delta, ema_beta, ema_eta, ema_omega, state_in)
    recv_in, recv_mix = (
        lax.all_to_all(inputs, "ch", split_axis=2, concat_axis=1, tiled=True),
        lax.all_to_all(activ.astype(jnp.bfloat16), "ch", split_axis=2, concat_axis=1, tiled=True),
    )
    tok_in = to_rows(recv_in)
    tok_mix = to_rows(recv_mix)
    row_count = tok_in.shape[0]
    blocks_n = row_count // GROUP
    value_pre = jnp.dot(tok_in, w_value, preferred_element_type=jnp.float32) + b_value
    values = jax.nn.silu(value_pre).astype(jnp.bfloat16)
    mix_pre = jnp.dot(tok_mix, w_mix, preferred_element_type=jnp.float32) + b_mix
    gate_pre = mix_pre[:, :width]
    query_pre = mix_pre[:, width : width + zwidth]
    reset_pre = mix_pre[:, width + zwidth : width + zwidth + vwidth]
    hidden_mix = mix_pre[:, width + zwidth + vwidth :]
    update = jax.nn.sigmoid(gate_pre)
    shared = jax.nn.silu(query_pre)
    queries = (shared * qk_scale[0] + qk_shift[0]).astype(jnp.bfloat16)
    keys_all = (shared * qk_scale[1] + qk_shift[1]).astype(jnp.bfloat16)
    reset = jax.nn.silu(reset_pre)
    query_blk = queries.reshape(blocks_n, GROUP, zwidth)
    key_blk = keys_all.reshape(blocks_n, GROUP, zwidth)
    value_blk = values.reshape(blocks_n, GROUP, vwidth)
    position = jnp.arange(GROUP)
    causal = position[:, None] >= position[None, :]

    def block_scores():
        raw = (
            jnp.einsum("cqz,ckz->cqk", query_blk, key_blk, preferred_element_type=jnp.float32)
            * scale
        )
        return jnp.where(causal[None], raw, -1e30)

    scores = block_scores()
    top_score = jnp.max(scores, axis=-1, keepdims=True)
    log_norm = top_score + jnp.log(jnp.sum(jnp.exp(scores - top_score), axis=-1, keepdims=True))
    probs_bf = jnp.exp(scores - log_norm).astype(jnp.bfloat16)
    attended = jnp.einsum(
        "cqk,ckv->cqv", probs_bf, value_blk, preferred_element_type=jnp.float32
    ).reshape(row_count, vwidth)
    gated = (reset * attended).astype(jnp.bfloat16)
    hidden_pre = hidden_mix + jnp.dot(gated, w_out, preferred_element_type=jnp.float32) + b_out
    hidden = jax.nn.silu(hidden_pre)
    resid = tok_in.astype(jnp.float32)
    blend = update * hidden + (1.0 - update) * resid
    centered = blend - jnp.mean(blend, axis=-1, keepdims=True)
    rstd = lax.rsqrt(jnp.mean(centered * centered, axis=-1, keepdims=True) + 1e-05)
    unit = centered * rstd
    normed = unit * ln_gain + ln_bias
    normed_bf = normed.astype(jnp.bfloat16)
    ffn_pre = jnp.dot(normed_bf, w_up, preferred_element_type=jnp.float32) + b_up
    ffn_hidden = jax.nn.silu(ffn_pre).astype(jnp.bfloat16)
    result = normed + jnp.dot(ffn_hidden, w_down, preferred_element_type=jnp.float32) + b_down
    out_local = lax.all_to_all(
        from_rows(result.astype(jnp.bfloat16), nseq_count),
        "ch",
        split_axis=1,
        concat_axis=2,
        tiled=True,
    )
    seq_pos = tok_index * local_len + jnp.arange(local_len, dtype=jnp.int32)
    live = (seq_pos[None, :] < seq_lengths[:, None])[:, None, :]
    output = jnp.where(live, out_local, jnp.zeros_like(out_local))
    grad_masked = jnp.where(live, out_grad, jnp.zeros_like(out_grad))
    grad_rows = to_rows(lax.all_to_all(grad_masked, "ch", split_axis=2, concat_axis=1, tiled=True))
    grad_f = grad_rows.astype(jnp.float32)
    g_down = jnp.dot(ffn_hidden.T, grad_rows, preferred_element_type=jnp.float32)
    g_bdown = jnp.sum(grad_f, axis=0)
    d_ffn = (
        jnp.dot(grad_rows, w_down.T, preferred_element_type=jnp.float32) * silu_slope(ffn_pre)
    ).astype(jnp.bfloat16)
    g_up = jnp.dot(normed_bf.T, d_ffn, preferred_element_type=jnp.float32)
    g_bup = jnp.sum(d_ffn.astype(jnp.float32), axis=0)
    d_normed = grad_f + jnp.dot(d_ffn, w_up.T, preferred_element_type=jnp.float32)
    g_gain = jnp.sum(d_normed * unit, axis=0)
    g_lnbias = jnp.sum(d_normed, axis=0)
    d_unit = d_normed * ln_gain
    d_blend = rstd * (
        d_unit
        - jnp.mean(d_unit, axis=-1, keepdims=True)
        - unit * jnp.mean(d_unit * unit, axis=-1, keepdims=True)
    )
    d_hidden_pre = (d_blend * update * silu_slope(hidden_pre)).astype(jnp.bfloat16)
    d_update_pre = d_blend * (hidden - resid) * update * (1.0 - update)
    d_direct = d_blend * (1.0 - update)
    g_out = jnp.dot(gated.T, d_hidden_pre, preferred_element_type=jnp.float32)
    g_bout = jnp.sum(d_hidden_pre.astype(jnp.float32), axis=0)
    d_gated = jnp.dot(d_hidden_pre, w_out.T, preferred_element_type=jnp.float32)
    d_reset_pre = d_gated * attended * silu_slope(reset_pre)
    d_attended = (d_gated * reset).astype(jnp.bfloat16).reshape(blocks_n, GROUP, vwidth)
    scores = block_scores()
    probs = jnp.exp(scores - log_norm)
    probs_bf = probs.astype(jnp.bfloat16)
    d_probs = jnp.einsum("cqv,ckv->cqk", d_attended, value_blk, preferred_element_type=jnp.float32)
    d_values = jnp.einsum(
        "cqk,cqv->ckv", probs_bf, d_attended, preferred_element_type=jnp.float32
    ).reshape(row_count, vwidth)
    d_scores = (probs * (d_probs - jnp.sum(d_probs * probs, axis=-1, keepdims=True))).astype(
        jnp.bfloat16
    )
    d_query = (
        jnp.einsum("cqk,ckz->cqz", d_scores, key_blk, preferred_element_type=jnp.float32).reshape(
            row_count, zwidth
        )
        * scale
    )
    d_key = (
        jnp.einsum("cqk,cqz->ckz", d_scores, query_blk, preferred_element_type=jnp.float32).reshape(
            row_count, zwidth
        )
        * scale
    )
    d_value_pre = (d_values * silu_slope(value_pre)).astype(jnp.bfloat16)
    g_value = jnp.dot(tok_in.T, d_value_pre, preferred_element_type=jnp.float32)
    g_bvalue = jnp.sum(d_value_pre.astype(jnp.float32), axis=0)
    d_resid = d_direct + jnp.dot(d_value_pre, w_value.T, preferred_element_type=jnp.float32)
    g_qscale = jnp.stack([jnp.sum(d_query * shared, axis=0), jnp.sum(d_key * shared, axis=0)])
    g_qshift = jnp.stack([jnp.sum(d_query, axis=0), jnp.sum(d_key, axis=0)])
    d_query_pre = (d_query * qk_scale[0] + d_key * qk_scale[1]) * silu_slope(query_pre)
    d_mix_pre = jnp.concatenate(
        [d_update_pre, d_query_pre, d_reset_pre, d_hidden_pre.astype(jnp.float32)], axis=1
    ).astype(jnp.bfloat16)
    g_mix = jnp.dot(tok_mix.T, d_mix_pre, preferred_element_type=jnp.float32)
    g_bmix = jnp.sum(d_mix_pre.astype(jnp.float32), axis=0)
    d_mix_in = jnp.dot(d_mix_pre, w_mix.T, preferred_element_type=jnp.float32)
    back_resid, back_mix = (
        lax.all_to_all(
            from_rows(d_resid.astype(jnp.bfloat16), nseq_count),
            "ch",
            split_axis=1,
            concat_axis=2,
            tiled=True,
        ),
        lax.all_to_all(
            from_rows(d_mix_in.astype(jnp.bfloat16), nseq_count),
            "ch",
            split_axis=1,
            concat_axis=2,
            tiled=True,
        ),
    )
    _, ema_pull = jax.vjp(
        ema_core, seq_f, ema_alpha, ema_delta, ema_beta, ema_eta, ema_omega, state_in
    )
    dx_ema, ga_first, gd_first, gb_first, g_eta, g_omega, state_grad = ema_pull(
        back_mix.astype(jnp.float32)
    )
    later_grad = prefix(
        (decay_all, state_grad), "tok", chain_combine, (jnp.ones_like(decay_all), zero_state), True
    )[1]
    _, state_pull = jax.vjp(state_advance, seq_f, ema_alpha, ema_delta, ema_beta, state_in)
    dx_state, ga_second, gd_second, gb_second, unused_grad = state_pull(later_grad)
    input_grad = back_resid.astype(jnp.float32) + dx_ema + dx_state
    g_mix_s, g_value_s, g_out_s, g_up_s, g_down_s = (
        lax.psum_scatter(g_mix, "ch", scatter_dimension=0, tiled=True),
        lax.psum_scatter(g_value, "ch", scatter_dimension=0, tiled=True),
        lax.psum_scatter(g_out, "ch", scatter_dimension=0, tiled=True),
        lax.psum_scatter(g_up, "ch", scatter_dimension=0, tiled=True),
        lax.psum_scatter(g_down, "ch", scatter_dimension=0, tiled=True),
    )
    summed = lax.psum(
        (
            g_mix_s,
            g_value_s,
            g_out_s,
            g_up_s,
            g_down_s,
            ga_first + ga_second,
            gd_first + gd_second,
            gb_first + gb_second,
            g_eta,
            g_omega,
        ),
        "tok",
    )
    smalls = lax.psum(
        (g_bmix, g_bvalue, g_bout, g_qscale, g_qshift, g_gain, g_lnbias, g_bup, g_bdown),
        ("ch", "tok"),
    )
    return (
        output,
        input_grad,
        summed[5],
        summed[6],
        summed[7],
        summed[8],
        summed[9],
        summed[0],
        smalls[0],
        summed[1],
        smalls[1],
        summed[2],
        smalls[2],
        smalls[3],
        smalls[4],
        smalls[5],
        smalls[6],
        summed[3],
        smalls[7],
        summed[4],
        smalls[8],
    )


def solution(mesh):
    placed = (
        P(None, "ch", "tok"),
        P(None, "ch", "tok"),
        P(),
        P("ch", None),
        P("ch", None),
        P("ch", None),
        P("ch", None),
        P("ch"),
        P(),
        P(),
        P(),
        P(),
        P(),
        P(),
        P(),
        P(),
        P(),
        P(),
        P(),
        P(),
        P(),
        P(),
    )
    return jax.shard_map(
        local,
        mesh=mesh,
        in_specs=placed,
        out_specs=(
            P(None, "ch", "tok"),
            P(None, "ch", "tok"),
            P("ch", None),
            P("ch", None),
            P("ch", None),
            P("ch", None),
            P("ch"),
            P("ch", None),
            P(),
            P("ch", None),
            P(),
            P("ch", None),
            P(),
            P(),
            P(),
            P(),
            P(),
            P("ch", None),
            P(),
            P("ch", None),
            P(),
        ),
        check_vma=False,
    )
```

profile of v0, /device:TPU:0, one launch (start us, length us, event | category | flops | bytes accessed | tf_op | source)
XLA Modules:
  0.0 922.2 jit_solution(10097495097072046068)
XLA Ops:
  9.8 7.3 all-to-all-start.1
  21.9 5.6 all-gather.3
  30.5 5.1 fusion.73
  35.7 5.6 all-gather.1
  41.3 7.6 while.30
  59.2 5.2 fusion.28
  68.1 3.5 fusion.77
  71.6 10.1 %bitcast_add_fusion.3 = f32[4,96,8,128]{3,2,0,1:T(8,128)} fusion(f32[96,4,8,128]{3,2,1,0:T(8,128)S(1)} %fusion.77, f32[96,128,128,1]{2,0,1,3:T(8,128)} %fusion.28, bf16[4,96,8,128]{3,2,1,0:T(8,128)(2,1)S(1)} %bitcast.299), kind=kOutput, calls=%fused_computation.96 | convolution fusion | flops 604372992 | bytes 10223616 | tf_op jit(solution)/shard_map/dts,ndbs->ndbt/dot_general | solution.py:51
  84.5 3.5 multiply_convert_fusion.4
  88.0 3.5 copy.343
  91.5 6.3 all-to-all-start
  103.0 21.0 %all-to-all-done = bf16[4,96,1024]{1,0,2:T(4,128)(2,1)} async-done(((bf16[4,96,1024]{1,0,2:T(4,128)(2,1)}), bf16[4,96,1024]{1,0,2:T(4,128)(2,1)}, u32[]{:S(2)}, u32[]{:S(2)}) %all-to-all-start) | async-done | bytes 786464 | tf_op jit(solution)/shard_map/all_to_all | solution.py:133
  128.7 5.6 convolution_add_fusion
  135.3 3.3 multiply_convert_fusion.2
  152.4 4.2 all-to-all-start.2
  158.4 18.2 %all-to-all-done.2 = bf16[4,768,128]{2,0,1:T(4,128)(2,1)} async-done(((bf16[4,768,128]{2,0,1:T(4,128)(2,1)}), bf16[4,768,128]{2,0,1:T(4,128)(2,1)}, u32[]{:S(2)}, u32[]{:S(2)}) %all-to-all-start.2) | async-done | bytes 786464 | tf_op jit(solution)/shard_map/all_to_all | solution.py:184
  181.6 29.6 %all_to_all.90 = bf16[4,96,1024]{1,0,2:T(4,128)(2,1)} all-to-all(bf16[4,96,1024]{1,0,2:T(4,128)(2,1)} %copy.355), channel_id=1, replica_groups=mesh['ch'=8,'tok'=4] {'ch'}, dimensions={2} | all-to-all | bytes 1572864 | tf_op jit(solution)/shard_map/all_to_all | solution.py:195
  215.8 5.6 convert_reduce_fusion.1
  223.8 4.8 convert_reduce_fusion.4
  228.7 5.6 fusion.19
  238.5 3.6 convolution_bitcast_fusion
  242.1 6.0 copy.413
  249.3 5.6 fusion.145
  255.7 5.6 fusion.142
  262.4 4.9 fusion.159
  273.7 6.5 fusion.146
  280.2 6.9 convolution_convert_fusion
  289.4 4.2 all-to-all-start.5
  293.6 5.8 add_convert_fusion
  301.6 11.5 %all-to-all-done.5 = bf16[4,768,128]{2,0,1:T(4,128)(2,1)} async-done(((bf16[4,768,128]{2,0,1:T(4,128)(2,1)}), bf16[4,768,128]{2,0,1:T(4,128)(2,1)}, u32[]{:S(2)}, u32[]{:S(2)}) %all-to-all-start.5) | async-done | bytes 786464 | tf_op jit(solution)/shard_map/all_to_all | solution.py:264
  313.1 4.4 all-to-all-start.4
  323.6 46.6 %all-reduce.8 = (f32[3200]{0:T(1024)}, f32[1536]{0:T(1024)}, f32[768]{0:T(1024)}, f32[2,128]{1,0:T(2,128)}, f32[2,128]{1,0:T(2,128)}, /*index=5*/f32[768]{0:T(10...) all-reduce(f32[3200]{0:T(1024)S(1)} %convert_reduce_fusion, ...), channel_id=1, replica_groups=mesh['ch'=8,'tok'=4] {'ch','tok'}, use_global_device_ids=true, to_apply=%region_33.34 | all-reduce | flops 9856 | bytes 78848 | tf_op jit(solution)/shard_map/psum | solution.py:306
  382.8 5.1 fusion.30
  395.1 3.7 multiply_reduce_fusion.6
  398.8 6.2 all-gather.2
  412.9 11.1 %add_bitcast_fusion = f32[4,96,8,128]{3,2,0,1:T(8,128)} fusion(f32[96,4,8,128]{3,2,1,0:T(8,128)S(1)} %fusion.80, f32[96,128,128,1]{2,0,1,3:T(8,128)} %fusion.28, f32[4,96,8,128]{3,2,0,1:T(8,128)S(1)} %copy-done.11), kind=kOutput, calls=%fused_computation.105 | convolution fusion | flops 604372992 | bytes 11010048 | tf_op jit(solution)/shard_map/transpose(jvp(dts,ndbs->ndbt))/dot_general | solution.py:51
  427.0 4.8 multiply_reduce_fusion.14
  431.9 5.1 bitcast_add_fusion.2
  436.9 6.2 multiply_reduce_fusion
  445.4 10.8 %reduce-scatter.14.cloned.1.call-done = f32[192,768]{1,0:T(8,128)} async-done(((f32[1536,768]{1,0:T(8,128)}), f32[192,768]{1,0:T(8,128)}) %reduce-scatter.14.cloned.1.call-update) | async-done | bytes 589840 | tf_op jit(solution)/shard_map/reduce_scatter | solution.py:289
  456.2 98.7 %reduce-scatter.12.cloned.1.call-done = f32[96,1536]{1,0:T(8,128)} async-done(((f32[768,1536]{1,0:T(8,128)}), f32[96,1536]{1,0:T(8,128)}) %reduce-scatter.12.cloned.1.call-update) | async-done | bytes 589840 | tf_op jit(solution)/shard_map/reduce_scatter | solution.py:288
  554.8 98.5 %reduce-scatter.10.cloned.1.call-done = f32[192,768]{1,0:T(8,128)} async-done(((f32[1536,768]{1,0:T(8,128)}), f32[192,768]{1,0:T(8,128)}) %reduce-scatter.10.cloned.1.call-update) | async-done | bytes 589840 | tf_op jit(solution)/shard_map/reduce_scatter | solution.py:287
  653.4 172.2 %reduce-scatter.8.cloned.1.call-done = f32[96,3200]{1,0:T(8,128)} async-done(((f32[768,3200]{1,0:T(8,128)}), f32[96,3200]{1,0:T(8,128)}) %reduce-scatter.8.cloned.1.call-update) | async-done | bytes 1228816 | tf_op jit(solution)/shard_map/reduce_scatter | solution.py:285
  834.7 5.1 convolution_bitcast_fusion.1
  839.9 8.0 fusion.2
  849.5 5.5 multiply_reduce_fusion.11
  856.2 13.2 %all-reduce.9 = (f32[96,16]{0,1:T(8,128)}, f32[96,16]{0,1:T(8,128)}, f32[96,16]{0,1:T(8,128)}, f32[96,16]{0,1:T(8,128)}, f32[96]{0:T(128)}) all-reduce(f32[96,16]{0,1:T(8,128)S(1)} %get-tuple-element.526, f32[96,16]{0,1:T(8,128)S(1)} %get-tuple-element.525, ...), channel_id=1, replica_groups=mesh['ch'=8,'tok'=4] {'tok'}, use_global_device_ids=true, to_apply=%region_23.24 | all-reduce | flops 6240 | bytes 49920 | tf_op jit(solution)/shard_map/psum | solution.py:291
  869.4 38.3 %all-reduce.13.cloned.1.call-done = (f32[96,3200]{1,0:T(8,128)}, f32[96,1536]{0,1:T(8,128)}, f32[192,768]{1,0:T(8,128)}, f32[96,1536]{1,0:T(8,128)}, f32[192,768]{1,0:T(8,128)}) async-done(((f32[96,3200]{1,0:T(8,128)}, f32[96,1536]{0,1:T(8,128)}, f32[192,768]{1,0:T(8,128)}, f32[96,1536]{1,0:T(8,128)}, f32[192,768]{1,0:T(8,128)}), (f32[96,3200]{1,0:T(8,128)}, f32[96,1536]{0,1:T(8,128)}, ...) | async-done | bytes 3588112 | tf_op jit(solution)/shard_map/psum | solution.py:291
  (429 shorter events, 151.3 us)
Async XLA Ops:
  7.2 134.8 %copy-start = (bf16[1536,768]{1,0:T(8,128)(2,1)S(1)}, bf16[1536,768]{1,0:T(8,128)(2,1)}, u32[]{:S(2)}) copy-start(bf16[1536,768]{1,0:T(8,128)(2,1)} %param.38) | copy-start | bytes 7077892
  7.2 10.4 %copy-start.84 = (f32[96,16]{0,1:T(8,128)S(1)}, f32[96,16]{0,1:T(8,128)}, u32[]{:S(2)}) copy-start(f32[96,16]{0,1:T(8,128)} %param.32) | copy-start | bytes 18436
  7.2 10.4 %copy-start.99 = (f32[96,16]{0,1:T(8,128)S(1)}, f32[96,16]{0,1:T(8,128)}, u32[]{:S(2)}) copy-start(f32[96,16]{0,1:T(8,128)} %param.31) | copy-start | bytes 18436
  7.2 10.4 %copy-start.103 = (f32[96,16]{0,1:T(8,128)S(1)}, f32[96,16]{0,1:T(8,128)}, u32[]{:S(2)}) copy-start(f32[96,16]{0,1:T(8,128)} %param.30) | copy-start | bytes 18436
  7.2 10.4 %copy-start.101 = (f32[96,16]{0,1:T(8,128)S(1)}, f32[96,16]{0,1:T(8,128)}, u32[]{:S(2)}) copy-start(f32[96,16]{0,1:T(8,128)} %param.29) | copy-start | bytes 18436
  9.8 81.7 %all-to-all-start.1 = ((bf16[4,96,1024]{1,0,2:T(4,128)(2,1)}), bf16[4,96,1024]{1,0,2:T(4,128)(2,1)}, u32[]{:S(2)}, u32[]{:S(2)}) async-start(bf16[4,96,1024]{1,0,2:T(4,128)(2,1)} %copy.347), calls=%async_computation.1 | async-start | bytes 2097152 | tf_op jit(solution)/shard_map/all_to_all | solution.py:132
  17.0 13.5 %copy-start.15 = (bf16[4,96,1024]{2,1,0:T(8,128)(2,1)S(1)}, bf16[4,96,1024]{2,1,0:T(8,128)(2,1)}, u32[]{:S(2)}) copy-start(bf16[4,96,1024]{2,1,0:T(8,128)(2,1)} %param.26) | copy-start | bytes 2359300
  18.3 12.1 %copy-start.86 = (f32[96,16]{0,1:T(8,128)}, f32[96,16]{0,1:T(8,128)S(1)}, u32[]{:S(2)}) copy-start(f32[96,16]{0,1:T(8,128)S(1)} %get-tuple-element.512) | copy-start | bytes 18436
  18.4 17.2 %copy-start.54 = (f32[96,16]{1,0:T(8,128)}, f32[96,16]{1,0:T(8,128)S(1)}, u32[]{:S(2)}) copy-start(f32[96,16]{1,0:T(8,128)S(1)} %copy.325) | copy-start | bytes 18436
  19.2 16.4 %copy-start.51 = (f32[96,16]{1,0:T(8,128)}, f32[96,16]{1,0:T(8,128)S(1)}, u32[]{:S(2)}) copy-start(f32[96,16]{1,0:T(8,128)S(1)} %copy.328) | copy-start | bytes 18436
  49.7 18.4 %copy-start.31 = (f32[96,8,16]{2,1,0:T(8,128)}, f32[96,8,16]{2,1,0:T(8,128)S(1)}, u32[]{:S(2)}) copy-start(f32[96,8,16]{2,1,0:T(8,128)S(1)} %multiply_exponential_fusion.4) | copy-start | bytes 147460
  88.0 10.4 %copy-start.120 = (f32[2,128]{1,0:T(2,128)S(1)}, f32[2,128]{1,0:T(2,128)}, u32[]{:S(2)}) copy-start(f32[2,128]{1,0:T(2,128)} %param.40) | copy-start | bytes 3076
  88.0 10.4 %copy-start.126 = (f32[2,128]{1,0:T(2,128)S(1)}, f32[2,128]{1,0:T(2,128)}, u32[]{:S(2)}) copy-start(f32[2,128]{1,0:T(2,128)} %param.41) | copy-start | bytes 3076
  91.5 32.6 %all-to-all-start = ((bf16[4,96,1024]{1,0,2:T(4,128)(2,1)}), bf16[4,96,1024]{1,0,2:T(4,128)(2,1)}, u32[]{:S(2)}, u32[]{:S(2)}) async-start(bf16[4,96,1024]{1,0,2:T(4,128)(2,1)} %copy.343), calls=%async_computation | async-start | bytes 2097152 | tf_op jit(solution)/shard_map/all_to_all | solution.py:133
  128.7 6.6 copy-start.23
  128.7 6.6 copy-start.130
  134.3 6.9 copy-start.30
  152.4 24.2 %all-to-all-start.2 = ((bf16[4,768,128]{2,0,1:T(4,128)(2,1)}), bf16[4,768,128]{2,0,1:T(4,128)(2,1)}, u32[]{:S(2)}, u32[]{:S(2)}) async-start(bf16[4,768,128]{2,0,1:T(4,128)(2,1)} %bitcast.313), calls=%async_computation.2 | async-start | bytes 1572864 | tf_op jit(solution)/shard_map/all_to_all | solution.py:184
  156.6 286.5 %reduce-scatter.16.cloned.1.call-start = ((), (), s32[]{:S(2)}) async-start(), calls=%async_computation.15 | async-start | bytes 5308416
  248.2 208.0 %reduce-scatter.14.cloned.1.call-start = ((), (), s32[]{:S(2)}) async-start(), calls=%async_computation.14 | async-start | bytes 5308416 | tf_op jit(solution)/shard_map/reduce_scatter | solution.py:289
  255.0 299.9 %reduce-scatter.12.cloned.1.call-start = ((), (), s32[]{:S(2)}) async-start(), calls=%async_computation.13 | async-start | bytes 5308416 | tf_op jit(solution)/shard_map/reduce_scatter | solution.py:288
  261.3 392.1 %reduce-scatter.10.cloned.1.call-start = ((), (), s32[]{:S(2)}) async-start(), calls=%async_computation.12 | async-start | bytes 5308416 | tf_op jit(solution)/shard_map/reduce_scatter | solution.py:287
  267.3 558.2 %reduce-scatter.8.cloned.1.call-start = ((), (), s32[]{:S(2)}) async-start(), calls=%async_computation.11 | async-start | bytes 11059200 | tf_op jit(solution)/shard_map/reduce_scatter | solution.py:285
  289.4 23.7 %all-to-all-start.5 = ((bf16[4,768,128]{2,0,1:T(4,128)(2,1)}), bf16[4,768,128]{2,0,1:T(4,128)(2,1)}, u32[]{:S(2)}, u32[]{:S(2)}) async-start(bf16[4,768,128]{2,0,1:T(4,128)(2,1)} %bitcast.312), calls=%async_computation.5 | async-start | bytes 1572864 | tf_op jit(solution)/shard_map/all_to_all | solution.py:264
  313.0 8.5 copy-start.121
  313.1 8.5 copy-start.122
  313.1 8.5 copy-start.20
  313.1 63.4 %all-to-all-start.4 = ((bf16[4,768,128]{2,0,1:T(4,128)(2,1)}), bf16[4,768,128]{2,0,1:T(4,128)(2,1)}, u32[]{:S(2)}, u32[]{:S(2)}) async-start(bf16[4,768,128]{2,0,1:T(4,128)(2,1)} %bitcast.48), calls=%async_computation.4 | async-start | bytes 1572864 | tf_op jit(solution)/shard_map/all_to_all | solution.py:257
  317.4 590.3 %all-reduce.13.cloned.1.call-start = ((), (), s32[]{:S(2)}) async-start(), calls=%async_computation.16 | async-start | bytes 7569408 | tf_op jit(solution)/shard_map/psum | solution.py:291
  395.1 9.9 %copy-start.40 = (f32[4,96,16]{1,2,0:T(8,128)S(1)}, f32[4,96,16]{1,2,0:T(8,128)}, u32[]{:S(2)}) copy-start(f32[4,96,16]{1,2,0:T(8,128)} %custom-call.1) | copy-start | bytes 73732
  839.8 8.0 copy-start.57
  839.8 9.5 %copy-start.39 = (f32[4,96,16]{2,0,1:T(4,128)S(1)}, f32[4,96,16]{2,0,1:T(4,128)}, u32[]{:S(2)}) copy-start(f32[4,96,16]{2,0,1:T(4,128)} %copy.339) | copy-start | bytes 73732
  839.8 9.5 %copy-start.61 = (f32[96,16,128]{2,1,0:T(8,128)S(1)}, f32[96,16,128]{2,1,0:T(8,128)}, u32[]{:S(2)}) copy-start(f32[96,16,128]{2,1,0:T(8,128)} %rev.11) | copy-start | bytes 2359300
  839.8 9.5 %copy-start.69 = (f32[96,16]{1,0:T(8,128)S(1)}, f32[96,16]{1,0:T(8,128)}, u32[]{:S(2)}) copy-start(f32[96,16]{1,0:T(8,128)} %copy.340) | copy-start | bytes 18436
  839.8 9.5 %copy-start.71 = (f32[96,16]{1,0:T(8,128)S(1)}, f32[96,16]{1,0:T(8,128)}, u32[]{:S(2)}) copy-start(f32[96,16]{1,0:T(8,128)} %copy.341) | copy-start | bytes 18436
  839.9 9.5 %copy-start.90 = (f32[96,16]{1,0:T(8,128)S(1)}, f32[96,16]{1,0:T(8,128)}, u32[]{:S(2)}) copy-start(f32[96,16]{1,0:T(8,128)} %copy.378) | copy-start | bytes 18436
  849.4 6.6 copy-start.83
  849.4 6.6 copy-start.85
  849.4 6.6 copy-start.87
  849.4 6.6 copy-start.94
  849.4 6.6 copy-start.95
  849.5 6.6 copy-start.96
  849.5 6.6 copy-start.97
  849.5 6.6 copy-start.98
  849.5 6.6 copy-start.100
  849.5 6.6 copy-start.102
  849.5 6.6 copy-start.104
  849.5 6.7 copy-start.123
  (103 other events, 277.9 us)
Sparse Core Ops, SparseCore 0:
  248.3 109.6 reduce-scatter.15
  361.7 94.4 reduce-scatter.13
  459.8 94.9 reduce-scatter.11
  558.3 94.9 reduce-scatter.9
  656.8 168.7 reduce-scatter.7
  828.2 79.4 all-reduce.12
where the time goes:
time: 930 us; the launch traced here: 922 us
  waiting for transfers between devices  469 us (50%)
  matrix products  152 us (16%)
  local copies, waits for them, and re-layouts  108 us (12%)
  blocking collectives  107 us (12%)
  other arithmetic  43.4 us (5%)
  starting transfers between devices  27.3 us (3%)
  between operations  16 us (2%)
    reduce_scatter x1, waiting for transfers between devices, local(): lax.psum_scatter(g_mix, 'ch', scatter_dimension=0, tiled=True)  172 us
    reduce_scatter x1, waiting for transfers between devices, local(): lax.psum_scatter(g_up, 'ch', scatter_dimension=0, tiled=True)  98.7 us
    reduce_scatter x1, waiting for transfers between devices, local(): lax.psum_scatter(g_out, 'ch', scatter_dimension=0, tiled=True)  98.5 us
    psum x1, blocking collectives, local(): lax.psum((g_bmix, g_bvalue, g_bout, g_qscale, g_qshift, g_gain, g_lnbias,...  46.6 us
    psum x1, waiting for transfers between devices, local(): lax.psum((g_mix_s, g_value_s, g_out_s, g_up_s, g_down_s, ga_first + ga_se...  38.3 us
    unnamed x291, local copies, waits for them, and re-layouts  36.7 us
    all_to_all x1, blocking collectives, local(): lax.all_to_all(grad_masked, 'ch', split_axis=2, concat_axis=1, tiled=True)  29.6 us
    dot_general x3, matrix products, ema_core(): inner = jnp.einsum('dts,ndbs->ndbt', toeplitz, blocks, precision=highest)  26.3 us
  transfers between devices with their start and end apart: 11, of which 8 were waited for; matrix products, arithmetic and copies ran while one was open for 23% of the time, Pallas kernels for 0%

commit v1 on v0

--- a/solution.py
+++ b/solution.py
@@ -87,6 +87,55 @@
 
 def from_rows(table, nseq_count):
     return jnp.swapaxes(table.reshape(nseq_count, -1, table.shape[1]), 1, 2)
+
+
+ORDER_A = (("tok", 1), ("ch", 0))
+ORDER_B = (("ch", 0), ("tok", 1))
+
+
+def bits_of(axis):
+    return lax.axis_size(axis).bit_length() - 1
+
+
+def exchange(part, axis, bit):
+    size = lax.axis_size(axis)
+    return lax.ppermute(part, axis, [(i, i ^ (1 << bit)) for i in range(size)])
+
+
+def reduce_rows(grad, order):
+    parts, rows, columns = grad.shape
+    ch_bits, tok_bits = bits_of("ch"), bits_of("tok")
+    own = rows >> (ch_bits + tok_bits)
+    names = [("ch", k) for k in reversed(range(ch_bits))] + [("tok", k) for k in reversed(range(tok_bits))]
+    stages = [("tok", 0)] + list(order)
+    stages += [name for name in reversed(names) if name not in stages]
+    kept = grad.reshape((parts,) + (2,) * len(names) + (own, columns))
+    arrived = None
+    for axis, bit in stages:
+        at = 1 + names.index((axis, bit))
+        mine = (lax.axis_index(axis) >> bit) & 1
+
+        def pick(which):
+            half = lax.dynamic_index_in_dim(kept, which, at, keepdims=False)
+            if arrived is None:
+                return half
+            other = lax.dynamic_index_in_dim(arrived, which, at, keepdims=False)
+            return (half.astype(jnp.float32) + other.astype(jnp.float32)).astype(jnp.bfloat16)
+
+        sent, kept = pick(1 - mine), pick(mine)
+        names.remove((axis, bit))
+        arrived = exchange(sent, axis, bit)
+    total = (kept.astype(jnp.float32) + arrived.astype(jnp.float32)).astype(jnp.bfloat16)
+    whole = lax.all_gather(total, "tok", axis=1)
+    return whole.reshape(parts, -1, columns).astype(jnp.float32)
+
+
+def reduce_pair(wide, tall, order):
+    rows, columns = tall.shape
+    low = jnp.bfloat16
+    merged = jnp.stack([wide.astype(low).reshape(rows, columns), tall.astype(low)])
+    merged = reduce_rows(merged, order)
+    return merged[0].reshape(-1, wide.shape[1]), merged[1]
 
 
 def local(
@@ -281,28 +330,13 @@
     _, state_pull = jax.vjp(state_advance, seq_f, ema_alpha, ema_delta, ema_beta, state_in)
     dx_state, ga_second, gd_second, gb_second, unused_grad = state_pull(later_grad)
     input_grad = back_resid.astype(jnp.float32) + dx_ema + dx_state
-    g_mix_s, g_value_s, g_out_s, g_up_s, g_down_s = (
-        lax.psum_scatter(g_mix, "ch", scatter_dimension=0, tiled=True),
-        lax.psum_scatter(g_value, "ch", scatter_dimension=0, tiled=True),
-        lax.psum_scatter(g_out, "ch", scatter_dimension=0, tiled=True),
-        lax.psum_scatter(g_up, "ch", scatter_dimension=0, tiled=True),
-        lax.psum_scatter(g_down, "ch", scatter_dimension=0, tiled=True),
-    )
-    summed = lax.psum(
-        (
-            g_mix_s,
-            g_value_s,
-            g_out_s,
-            g_up_s,
-            g_down_s,
-            ga_first + ga_second,
-            gd_first + gd_second,
-            gb_first + gb_second,
-            g_eta,
-            g_omega,
-        ),
-        "tok",
-    )
+    g_up_s, g_down_s = reduce_pair(g_up, g_down, ORDER_A)
+    g_value_s, g_out_s = reduce_pair(g_value, g_out, ORDER_B)
+    g_mix_s = reduce_rows(g_mix.astype(jnp.bfloat16)[None], ORDER_A)[0]
+    ema_grads = lax.psum(
+        (ga_first + ga_second, gd_first + gd_second, gb_first + gb_second, g_eta, g_omega), "tok"
+    )
+    summed = (g_mix_s, g_value_s, g_out_s, g_up_s, g_down_s) + ema_grads
     smalls = lax.psum(
         (g_bmix, g_bvalue, g_bout, g_qscale, g_qshift, g_gain, g_lnbias, g_bup, g_bdown),
         ("ch", "tok"),

time: 930 us -> 594 us (0.64)
  waiting for transfers between devices: 469 us -> 105 us
  other arithmetic: 43.4 us -> 73.6 us
  starting transfers between devices: 27.3 us -> 50.1 us
  between operations: 16 us -> 2.65 us
  matrix products: 152 us -> 140 us
  blocking collectives: 107 us -> 95.1 us
  local copies, waits for them, and re-layouts: 108 us -> 119 us
    reduce_scatter x4 -> x0, waiting for transfers between devices: 380 us -> none  [the longest x1 172 us: local(): lax.psum_scatter(g_mix, 'ch', scatter_dimension=0, tiled=True)]
    ppermute x0 -> x15, waiting for transfers between devices: none -> 38.4 us  [exchange(): return lax.ppermute(part, axis, [(i, i ^ 1 << bit) for i in range(size)])]
    psum x1 -> x0, waiting for transfers between devices: 38.3 us -> none  [local(): lax.psum((g_mix_s, g_value_s, g_out_s, g_up_s, g_down_s, ga_first + ga_se...]
    all_to_all x1 -> x0, blocking collectives: 29.6 us -> none  [local(): lax.all_to_all(grad_masked, 'ch', split_axis=2, concat_axis=1, tiled=True)]
    convert_element_type x0 -> x21, other arithmetic: none -> 28.2 us  [the longest x15 25.8 us: pick(): (half.astype(jnp.float32) + other.astype(jnp.float32)).astype(jnp.bfloat16)]
    all_to_all x0 -> x1, waiting for transfers between devices: none -> 24.8 us  [local(): lax.all_to_all(grad_masked, 'ch', split_axis=2, concat_axis=1, tiled=True)]
    all_gather x0 -> x3, blocking collectives: none -> 23.1 us  [reduce_rows(): whole = lax.all_gather(total, 'tok', axis=1)]
    ppermute x0 -> x15, starting transfers between devices: none -> 17.9 us  [exchange(): return lax.ppermute(part, axis, [(i, i ^ 1 << bit) for i in range(size)])]
  transfers between devices with their start and end apart: 11 -> 21, of which waited for: 8 -> 8; matrix products, arithmetic and copies ran while one was open for 23% -> 39% of each run, Pallas kernels for 0% -> 0%
where the time goes in v1:
time: 594 us; the launch traced here: 585 us
  matrix products  140 us (24%)
  local copies, waits for them, and re-layouts  119 us (20%)
  waiting for transfers between devices  105 us (18%)
  blocking collectives  95.1 us (16%)
  other arithmetic  73.6 us (12%)
  starting transfers between devices  50.1 us (8%)
    psum x1, blocking collectives, local(): lax.psum((g_bmix, g_bvalue, g_bout, g_qscale, g_qshift, g_gain, g_lnbias,...  42.2 us
    ppermute x15, waiting for transfers between devices, exchange(): return lax.ppermute(part, axis, [(i, i ^ 1 << bit) for i in range(size)])  38.4 us
    dot_general x3, matrix products, ema_core(): inner = jnp.einsum('dts,ndbs->ndbt', toeplitz, blocks, precision=highest)  28.2 us
    convert_element_type x15, other arithmetic, pick(): (half.astype(jnp.float32) + other.astype(jnp.float32)).astype(jnp.bfloat16)  25.8 us
    all_to_all x1, waiting for transfers between devices, local(): lax.all_to_all(grad_masked, 'ch', split_axis=2, concat_axis=1, tiled=True)  24.8 us
    all_gather x3, blocking collectives, reduce_rows(): whole = lax.all_gather(total, 'tok', axis=1)  23.1 us
    all_to_all x1, waiting for transfers between devices, local(): lax.all_to_all(activ.astype(jnp.bfloat16), 'ch', split_axis=2, concat_axi...  21.6 us
    all_to_all x1, waiting for transfers between devices, local(): lax.all_to_all(from_rows(result.astype(jnp.bfloat16), nseq_count), 'ch',...  19.8 us
  transfers between devices with their start and end apart: 21, of which 8 were waited for; matrix products, arithmetic and copies ran while one was open for 39% of the time, Pallas kernels for 0%

profile of v1, /device:TPU:0, one launch (start us, length us, event | category | flops | bytes accessed | tf_op | source)
XLA Modules:
  0.0 585.4 jit_solution(6185668429854411058)
XLA Ops:
  3.2 7.3 %all-to-all-start.1 = ((bf16[4,96,1024]{1,0,2:T(4,128)(2,1)}), bf16[4,96,1024]{1,0,2:T(4,128)(2,1)}, u32[]{:S(2)}, u32[]{:S(2)}) async-start(bf16[4,96,1024]{1,0,2:T(4,128)(2,1)} %copy.451), calls=%async_computation.1 | async-start | bytes 2097152 | tf_op jit(solution)/shard_map/all_to_all | solution.py:181
  15.4 5.6 all-gather.6
  23.9 5.1 fusion.88
  29.1 5.6 all-gather.1
  34.7 7.5 %while.30 = (s32[]{:T(128)}, f32[4,96,16]{1,2,0:T(8,128)}, s32[]{:T(128)}, f32[4,96,16]{1,2,0:T(8,128)}, f32[4,4,96,16]{2,3,1,0:T(8,128)S(1)}, /*index=5*/s32[]{:T(128)}, s32[]{:T(128)}) while((s32[]{:T(128)}, f32[4,96,16]{1,2,0:T(8,128)}, s32[]{:T(128)}, f32[4,96,16]{1,2,0:T(8,128)}, f32[4,4,96,16]{2,3,1,0:T(8,128)S(1)}, ...), condition=%wide.region_1.2_spmd.clone, body=%wide.region_0.1_spmd.clone.sunk | while | flops 24580 | bytes 92273 | solution.py:27
  52.7 5.2 fusion.29
  61.5 3.5 fusion.92
  65.0 10.1 %bitcast_add_fusion.3 = f32[4,96,8,128]{3,2,0,1:T(8,128)} fusion(f32[96,4,8,128]{3,2,1,0:T(8,128)S(1)} %fusion.92, f32[96,128,128,1]{2,0,1,3:T(8,128)} %fusion.29, bf16[4,96,8,128]{3,2,1,0:T(8,128)(2,1)S(1)} %bitcast.447), kind=kOutput, calls=%fused_computation.130 | convolution fusion | flops 604372992 | bytes 10223616 | tf_op jit(solution)/shard_map/dts,ndbs->ndbt/dot_general | solution.py:51
  77.9 3.5 multiply_convert_fusion.4
  81.5 3.5 copy.447
  84.9 6.3 %all-to-all-start = ((bf16[4,96,1024]{1,0,2:T(4,128)(2,1)}), bf16[4,96,1024]{1,0,2:T(4,128)(2,1)}, u32[]{:S(2)}, u32[]{:S(2)}) async-start(bf16[4,96,1024]{1,0,2:T(4,128)(2,1)} %copy.447), calls=%async_computation | async-start | bytes 2097152 | tf_op jit(solution)/shard_map/all_to_all | solution.py:182
  95.9 21.6 %all-to-all-done = bf16[4,96,1024]{1,0,2:T(4,128)(2,1)} async-done(((bf16[4,96,1024]{1,0,2:T(4,128)(2,1)}), bf16[4,96,1024]{1,0,2:T(4,128)(2,1)}, u32[]{:S(2)}, u32[]{:S(2)}) %all-to-all-start) | async-done | bytes 786464 | tf_op jit(solution)/shard_map/all_to_all | solution.py:182
  122.2 5.6 convolution_add_fusion
  146.1 4.6 all-to-all-start.2
  150.9 19.8 %all-to-all-done.2 = bf16[4,768,128]{2,0,1:T(4,128)(2,1)} async-done(((bf16[4,768,128]{2,0,1:T(4,128)(2,1)}), bf16[4,768,128]{2,0,1:T(4,128)(2,1)}, u32[]{:S(2)}, u32[]{:S(2)}) %all-to-all-start.2) | async-done | bytes 786464 | tf_op jit(solution)/shard_map/all_to_all | solution.py:233
  175.7 4.2 all-to-all-start.3
  180.7 24.8 %all-to-all-done.3 = bf16[4,96,1024]{1,0,2:T(4,128)(2,1)} async-done(((bf16[4,96,1024]{1,0,2:T(4,128)(2,1)}), bf16[4,96,1024]{1,0,2:T(4,128)(2,1)}, u32[]{:S(2)}, u32[]{:S(2)}) %all-to-all-start.3) | async-done | bytes 786464 | tf_op jit(solution)/shard_map/all_to_all | solution.py:244
  210.1 5.0 convert_reduce_fusion.1
  222.9 3.6 fusion.19
  238.0 6.7 %convolution_convert_fusion.5 = bf16[512,768]{1,0:T(8,128)(2,1)} fusion(bf16[768,3200]{1,0:T(8,128)(2,1)} %param.34, bf16[512,768]{1,0:T(8,128)(2,1)S(1)} %copy-done.43, bf16[512,1536]{1,0:T(8,128)(2,1)} %get-tuple-element.511, bf16[512,128]{1,0:T(8,128)(2,1)S(1)} %get-tuple-element.513, bf16[512,768]{1,0:T(8,128)(2,1)S(1)} %copy-done.45), kind=kOutput, calls=%fused_computation.158 | convolution fusion | flops 2530082816 | bytes 8978432 | tf_op jit(solution)/shard_map/dot_general | solution.py:304
  244.8 5.3 convolution_convert_fusion
  254.6 4.0 add_convert_fusion
  264.1 4.2 all-to-all-start.5
  272.8 4.3 copy.495
  277.1 3.5 stack.34
  280.6 3.4 copy_bitcast_fusion.1
  286.2 3.5 copy_bitcast_fusion
  290.6 42.2 %all-reduce.8 = (f32[3200]{0:T(1024)}, f32[1536]{0:T(1024)}, f32[768]{0:T(1024)}, f32[2,128]{1,0:T(2,128)}, f32[2,128]{1,0:T(2,128)}, /*index=5*/f32[768]{0:T(10...) all-reduce(f32[3200]{0:T(1024)S(1)} %convert_reduce_fusion, ...), channel_id=1, replica_groups=mesh['ch'=8,'tok'=4] {'ch','tok'}, use_global_device_ids=true, to_apply=%region_31.32 | all-reduce | flops 9856 | bytes 78848 | tf_op jit(solution)/shard_map/psum | solution.py:340
  339.3 5.6 all-to-all-start.4
  351.1 5.3 fusion.39
  365.8 4.5 multiply_reduce_fusion.6
  371.3 5.4 all-gather.2
  382.5 5.6 multiply_reduce_fusion
  400.3 11.5 %add_bitcast_fusion = f32[4,96,8,128]{3,2,0,1:T(8,128)} fusion(f32[96,4,8,128]{3,2,1,0:T(8,128)} %fusion.95, f32[96,128,128,1]{2,0,1,3:T(8,128)} %fusion.29, f32[4,96,8,128]{3,2,0,1:T(8,128)} %reshape.712), kind=kOutput, calls=%fused_computation.139 | convolution fusion | flops 604372992 | bytes 11010048 | tf_op jit(solution)/shard_map/transpose(jvp(dts,ndbs->ndbt))/dot_general | solution.py:51
  414.7 4.5 multiply_reduce_fusion.14
  422.4 6.5 %convolution_bitcast_fusion = f32[96,128,128]{2,1,0:T(8,128)S(1)} fusion(f32[4,96,8,128]{3,2,0,1:T(8,128)} %reshape.712, bf16[4,96,8,128]{3,2,1,0:T(8,128)(2,1)S(1)} %bitcast.449), kind=kOutput, calls=%fused_computation.78 | convolution fusion | flops 603979776 | bytes 8650752 | tf_op jit(solution)/shard_map/transpose(jvp(dts,ndbs->ndbt))/dot_general | solution.py:51
  429.0 7.9 %fusion.2 = f32[96,128,1]{1,0,2:T(8,128)S(1)} fusion(f32[96,128,128]{2,1,0:T(8,128)S(1)} %convolution_bitcast_fusion, f32[128,128]{1,0:T(8,128)S(1)} %copy-done.84), kind=kOutput, calls=%fused_computation.7 | convolution fusion | flops 2418016256 | bytes 6406144 | tf_op jit(solution)/shard_map/transpose(jvp(dm,mts->dts))/dot_general | solution.py:49
  441.0 4.2 fusion.35
  451.0 3.8 fusion.31
  455.9 4.0 multiply_reduce_fusion.11
  462.8 6.8 %bitcast_add_fusion.2 = f32[4,96,1024]{2,0,1:T(4,128)S(1)} fusion(f32[4,96,1024]{2,0,1:T(4,128)} %reshape.714, f32[4,96,1024]{2,0,1:T(4,128)} %reshape.713, f32[4,96,1024]{2,0,1:T(4,128)} %get-tuple-element.501, f32[96,4,16]{2,1,0:T(4,128)S(1)} %copy-done.101, f32[96,16]{1,0:T(8,128)S(1)} %copy-done.78, f32[1024]{0:T(1024)S(1)} %copy-done.129, ...), kind=kOutput, calls=%fused_computation.123 | convolution fusion | flops 80216064 | bytes 6332800 | tf_op jit(solution)/shard_map/transpose(jvp(djs,nds->ndj))/dot_general | solution.py:76
  482.7 17.9 %collective-permute-done.1 = bf16[1,2,2,2,24,3200]{5,4,1,3,2,0:T(8,128)(2,1)} collective-permute-done((bf16[1,2,2,2,24,3200]{5,4,1,3,2,0:T(8,128)(2,1)}, bf16[1,2,2,2,24,3200]{5,4,1,3,2,0:T(8,128)(2,1)}, u32[]{:S(2)}, u32[]{:S(2)}) %collective-permute-start.1) | collective-permute-done | bytes 1228832 | tf_op jit(solution)/shard_map/ppermute | solution.py:102
  507.6 13.2 %all-reduce.9 = (f32[96,16]{0,1:T(8,128)}, f32[96,16]{0,1:T(8,128)}, f32[96,16]{0,1:T(8,128)}, f32[96,16]{0,1:T(8,128)}, f32[96]{0:T(128)}) all-reduce(f32[96,16]{0,1:T(8,128)S(1)} %get-tuple-element.537, f32[96,16]{0,1:T(8,128)S(1)} %get-tuple-element.536, ...), channel_id=1, replica_groups=mesh['ch'=8,'tok'=4] {'tok'}, use_global_device_ids=true, to_apply=%region_23.24 | all-reduce | flops 6240 | bytes 49920 | tf_op jit(solution)/shard_map/psum | solution.py:336
  527.4 6.1 %collective-permute-done.13 = bf16[2,2,48,768]{3,2,0,1:T(8,128)(2,1)S(1)} collective-permute-done((bf16[2,2,48,768]{3,2,0,1:T(8,128)(2,1)S(1)}, bf16[2,2,48,768]{3,2,0,1:T(8,128)(2,1)S(1)}, u32[]{:S(2)}, u32[]{:S(2)}) %collective-permute-start.13) | collective-permute-done | bytes 294944 | tf_op jit(solution)/shard_map/ppermute | solution.py:102
  543.3 8.5 %all-gather.5 = bf16[2,192,768]{2,1,0:T(8,128)(2,1)S(1)} all-gather(bf16[2,48,768]{2,1,0:T(8,128)(2,1)S(1)} %fusion.144), channel_id=7, replica_groups=mesh['ch'=8,'tok'=4] {'tok'}, dimensions={1}, use_global_device_ids=true | all-gather | bytes 737280 | tf_op jit(solution)/shard_map/all_gather | solution.py:129
  551.9 7.7 %all-gather.4 = bf16[2,192,768]{2,1,0:T(8,128)(2,1)S(1)} all-gather(bf16[2,48,768]{2,1,0:T(8,128)(2,1)S(1)} %fusion.147), channel_id=6, replica_groups=mesh['ch'=8,'tok'=4] {'tok'}, dimensions={1}, use_global_device_ids=true | all-gather | bytes 737280 | tf_op jit(solution)/shard_map/all_gather | solution.py:129
  567.6 8.5 %collective-permute-done.4 = bf16[1,24,3200]{2,1,0:T(8,128)(2,1)S(1)} collective-permute-done((bf16[1,24,3200]{2,1,0:T(8,128)(2,1)S(1)}, bf16[1,24,3200]{2,1,0:T(8,128)(2,1)S(1)}, u32[]{:S(2)}, u32[]{:S(2)}) %collective-permute-start.4) | collective-permute-done | bytes 153632 | tf_op jit(solution)/shard_map/ppermute | solution.py:102
  577.1 7.0 %all-gather.3 = bf16[4,24,3200]{2,1,0:T(8,128)(2,1)S(1)} all-gather(bf16[1,24,3200]{2,1,0:T(8,128)(2,1)S(1)} %fusion.139), channel_id=5, replica_groups=mesh['ch'=8,'tok'=4] {'tok'}, dimensions={0}, use_global_device_ids=true | all-gather | bytes 768000 | tf_op jit(solution)/shard_map/all_gather | solution.py:129
  (498 shorter events, 218.9 us)
Async XLA Ops:
  0.7 134.9 %copy-start = (bf16[1536,768]{1,0:T(8,128)(2,1)S(1)}, bf16[1536,768]{1,0:T(8,128)(2,1)}, u32[]{:S(2)}) copy-start(bf16[1536,768]{1,0:T(8,128)(2,1)} %param.38) | copy-start | bytes 7077892
  0.7 10.4 %copy-start.104 = (f32[96,16]{0,1:T(8,128)S(1)}, f32[96,16]{0,1:T(8,128)}, u32[]{:S(2)}) copy-start(f32[96,16]{0,1:T(8,128)} %param.32) | copy-start | bytes 18436
  0.7 10.4 %copy-start.121 = (f32[96,16]{0,1:T(8,128)S(1)}, f32[96,16]{0,1:T(8,128)}, u32[]{:S(2)}) copy-start(f32[96,16]{0,1:T(8,128)} %param.31) | copy-start | bytes 18436
  0.7 10.4 %copy-start.125 = (f32[96,16]{0,1:T(8,128)S(1)}, f32[96,16]{0,1:T(8,128)}, u32[]{:S(2)}) copy-start(f32[96,16]{0,1:T(8,128)} %param.30) | copy-start | bytes 18436
  0.7 10.4 %copy-start.123 = (f32[96,16]{0,1:T(8,128)S(1)}, f32[96,16]{0,1:T(8,128)}, u32[]{:S(2)}) copy-start(f32[96,16]{0,1:T(8,128)} %param.29) | copy-start | bytes 18436
  3.2 81.7 %all-to-all-start.1 = ((bf16[4,96,1024]{1,0,2:T(4,128)(2,1)}), bf16[4,96,1024]{1,0,2:T(4,128)(2,1)}, u32[]{:S(2)}, u32[]{:S(2)}) async-start(bf16[4,96,1024]{1,0,2:T(4,128)(2,1)} %copy.451), calls=%async_computation.1 | async-start | bytes 2097152 | tf_op jit(solution)/shard_map/all_to_all | solution.py:181
  10.5 13.5 %copy-start.16 = (bf16[4,96,1024]{2,1,0:T(8,128)(2,1)S(1)}, bf16[4,96,1024]{2,1,0:T(8,128)(2,1)}, u32[]{:S(2)}) copy-start(bf16[4,96,1024]{2,1,0:T(8,128)(2,1)} %param.26) | copy-start | bytes 2359300
  11.7 12.1 %copy-start.106 = (f32[96,16]{0,1:T(8,128)}, f32[96,16]{0,1:T(8,128)S(1)}, u32[]{:S(2)}) copy-start(f32[96,16]{0,1:T(8,128)S(1)} %get-tuple-element.507) | copy-start | bytes 18436
  11.8 17.2 %copy-start.75 = (f32[96,16]{1,0:T(8,128)}, f32[96,16]{1,0:T(8,128)S(1)}, u32[]{:S(2)}) copy-start(f32[96,16]{1,0:T(8,128)S(1)} %copy.429) | copy-start | bytes 18436
  12.6 16.4 %copy-start.72 = (f32[96,16]{1,0:T(8,128)}, f32[96,16]{1,0:T(8,128)S(1)}, u32[]{:S(2)}) copy-start(f32[96,16]{1,0:T(8,128)S(1)} %copy.432) | copy-start | bytes 18436
  43.1 18.4 %copy-start.35 = (f32[96,8,16]{2,1,0:T(8,128)}, f32[96,8,16]{2,1,0:T(8,128)S(1)}, u32[]{:S(2)}) copy-start(f32[96,8,16]{2,1,0:T(8,128)S(1)} %multiply_exponential_fusion.4) | copy-start | bytes 147460
  81.5 9.8 %copy-start.130 = (f32[2,128]{1,0:T(2,128)S(1)}, f32[2,128]{1,0:T(2,128)}, u32[]{:S(2)}) copy-start(f32[2,128]{1,0:T(2,128)} %param.40) | copy-start | bytes 3076
  81.5 9.8 %copy-start.134 = (f32[2,128]{1,0:T(2,128)S(1)}, f32[2,128]{1,0:T(2,128)}, u32[]{:S(2)}) copy-start(f32[2,128]{1,0:T(2,128)} %param.41) | copy-start | bytes 3076
  84.9 32.6 %all-to-all-start = ((bf16[4,96,1024]{1,0,2:T(4,128)(2,1)}), bf16[4,96,1024]{1,0,2:T(4,128)(2,1)}, u32[]{:S(2)}, u32[]{:S(2)}) async-start(bf16[4,96,1024]{1,0,2:T(4,128)(2,1)} %copy.447), calls=%async_computation | async-start | bytes 2097152 | tf_op jit(solution)/shard_map/all_to_all | solution.py:182
  127.8 7.1 %copy-start.34 = (f32[512,3200]{1,0:T(8,128)}, f32[512,3200]{1,0:T(8,128)S(1)}, u32[]{:S(2)}) copy-start(f32[512,3200]{1,0:T(8,128)S(1)} %convolution_add_fusion) | copy-start | bytes 19660804
  143.9 6.8 %copy-start.135 = (s32[4]{0:T(128)S(1)}, s32[4]{0:T(128)}, u32[]{:S(2)}) copy-start(s32[4]{0:T(128)} %param.28) | copy-start | bytes 52
  146.1 24.6 %all-to-all-start.2 = ((bf16[4,768,128]{2,0,1:T(4,128)(2,1)}), bf16[4,768,128]{2,0,1:T(4,128)(2,1)}, u32[]{:S(2)}, u32[]{:S(2)}) async-start(bf16[4,768,128]{2,0,1:T(4,128)(2,1)} %bitcast.466), calls=%async_computation.2 | async-start | bytes 1572864 | tf_op jit(solution)/shard_map/all_to_all | solution.py:233
  175.7 29.8 %all-to-all-start.3 = ((bf16[4,96,1024]{1,0,2:T(4,128)(2,1)}), bf16[4,96,1024]{1,0,2:T(4,128)(2,1)}, u32[]{:S(2)}, u32[]{:S(2)}) async-start(bf16[4,96,1024]{1,0,2:T(4,128)(2,1)} %copy.459), calls=%async_computation.3 | async-start | bytes 2097152 | tf_op jit(solution)/shard_map/all_to_all | solution.py:244
  210.1 9.9 %slice-start = ((s8[6553600]{0:T(1024)(128)(4,1)}), s8[4194304]{0:T(1024)(128)(4,1)S(1)}, s32[]{:S(2)}) async-start(s8[6553600]{0:T(1024)(128)(4,1)} %bitcast.459), calls=%async_computation.6 | async-start | bytes 8388608
  264.1 75.2 %all-to-all-start.5 = ((bf16[4,768,128]{2,0,1:T(4,128)(2,1)}), bf16[4,768,128]{2,0,1:T(4,128)(2,1)}, u32[]{:S(2)}, u32[]{:S(2)}) async-start(bf16[4,768,128]{2,0,1:T(4,128)(2,1)} %bitcast.54), calls=%async_computation.5 | async-start | bytes 1572864 | tf_op jit(solution)/shard_map/all_to_all | solution.py:313
  284.0 157.0 %collective-permute-start.10 = (bf16[2,2,2,2,2,48,768]{6,5,0,1,3,2,4:T(8,128)(2,1)}, bf16[2,2,2,2,2,48,768]{6,5,0,1,3,2,4:T(8,128)(2,1)}, u32[]{:S(2)}, u32[]{:S(2)}) collective-permute-start(bf16[2,2,2,2,2,48,768]{6,5,0,1,3,2,4:T(8,128)(2,1)} %copy_bitcast_fusion.1), channel_id=1, source_target_pairs={{0,1},{1,0},{2,3},{3,2},{4,5},{5,4},{6,7},{7,6},{8,9},{9,8},{10,11... | collective-permute-start | bytes 7077896 | tf_op jit(solution)/shard_map/ppermute | solution.py:102
  285.7 160.7 %collective-permute-start.5 = (bf16[2,2,2,2,2,48,768]{6,5,0,1,4,2,3:T(8,128)(2,1)}, bf16[2,2,2,2,2,48,768]{6,5,0,1,4,2,3:T(8,128)(2,1)}, u32[]{:S(2)}, u32[]{:S(2)}) collective-permute-start(bf16[2,2,2,2,2,48,768]{6,5,0,1,4,2,3:T(8,128)(2,1)} %copy_bitcast_fusion.2), channel_id=1, source_target_pairs={{0,1},{1,0},{2,3},{3,2},{4,5},{5,4},{6,7},{7,6},{8,9},{9,8},{10,11... | collective-permute-start | bytes 7077896 | tf_op jit(solution)/shard_map/ppermute | solution.py:102
  289.7 161.2 %collective-permute-start = (bf16[1,2,2,2,2,24,3200]{6,5,1,3,2,4,0:T(8,128)(2,1)}, bf16[1,2,2,2,2,24,3200]{6,5,1,3,2,4,0:T(8,128)(2,1)}, u32[]{:S(2)}, u32[]{:S(2)}) collective-permute-start(bf16[1,2,2,2,2,24,3200]{6,5,1,3,2,4,0:T(8,128)(2,1)} %copy_bitcast_fusion), channel_id=1, source_target_pairs={{0,1},{1,0},{2,3},{3,2},{4,5},{5,4},{6,7},{7,6},{8,9},{9,8},{10,11... | collective-permute-start | bytes 7372808 | tf_op jit(solution)/shard_map/ppermute | solution.py:102
  339.3 51.7 %all-to-all-start.4 = ((bf16[4,768,128]{2,0,1:T(4,128)(2,1)}), bf16[4,768,128]{2,0,1:T(4,128)(2,1)}, u32[]{:S(2)}, u32[]{:S(2)}) async-start(bf16[4,768,128]{2,0,1:T(4,128)(2,1)} %bitcast.465), calls=%async_computation.4 | async-start | bytes 1572864 | tf_op jit(solution)/shard_map/all_to_all | solution.py:306
  365.8 14.9 %copy-start.95 = (f32[96,16]{1,0:T(8,128)S(1)}, f32[96,16]{1,0:T(8,128)}, u32[]{:S(2)}) copy-start(f32[96,16]{1,0:T(8,128)} %copy.434) | copy-start | bytes 18436
  429.0 8.6 %copy-start.77 = (f32[96,16]{1,0:T(8,128)S(1)}, f32[96,16]{1,0:T(8,128)}, u32[]{:S(2)}) copy-start(f32[96,16]{1,0:T(8,128)} %copy-done.75) | copy-start | bytes 18436
  429.0 12.0 %copy-start.33 = (bf16[2,2,2,2,1,1,48,768]{7,6,5,4,3,2,1,0:T(8,128)(2,1)S(1)}, bf16[2,2,2,2,1,1,48,768]{7,6,5,4,3,2,1,0:T(8,128)(2,1)}, u32[]{:S(2)}) copy-start(bf16[2,2,2,2,1,1,48,768]{7,6,5,4,3,2,1,0:T(8,128)(2,1)} %get-tuple-element.518) | copy-start | bytes 3538948
  445.2 29.1 %collective-permute-start.11 = (bf16[2,2,2,2,48,768]{5,4,0,1,3,2:T(8,128)(2,1)}, bf16[2,2,2,2,48,768]{5,4,0,1,3,2:T(8,128)(2,1)}, u32[]{:S(2)}, u32[]{:S(2)}) collective-permute-start(bf16[2,2,2,2,48,768]{5,4,0,1,3,2:T(8,128)(2,1)} %get-tuple-element.529), channel_id=1, source_target_pairs={{0,2},{1,3},{2,0},{3,1},{4,6},{5,7},{6,4},{7,5},{8,10},{9,11},{10,... | collective-permute-start | bytes 3538952 | tf_op jit(solution)/shard_map/ppermute | solution.py:102
  449.0 30.6 %collective-permute-start.6 = (bf16[2,2,2,2,48,768]{5,4,3,2,1,0:T(8,128)(2,1)}, bf16[2,2,2,2,48,768]{5,4,3,2,1,0:T(8,128)(2,1)}, u32[]{:S(2)}, u32[]{:S(2)}) collective-permute-start(bf16[2,2,2,2,48,768]{5,4,3,2,1,0:T(8,128)(2,1)} %fusion.36), channel_id=1, source_target_pairs={{0,4},{4,0},{8,12},{12,8},{16,20},{20,16},{24,28},{28,24},{1,5},{5... | collective-permute-start | bytes 3538952 | tf_op jit(solution)/shard_map/ppermute | solution.py:102
  454.9 45.7 %collective-permute-start.1 = (bf16[1,2,2,2,24,3200]{5,4,1,3,2,0:T(8,128)(2,1)}, bf16[1,2,2,2,24,3200]{5,4,1,3,2,0:T(8,128)(2,1)}, u32[]{:S(2)}, u32[]{:S(2)}) collective-permute-start(bf16[1,2,2,2,24,3200]{5,4,1,3,2,0:T(8,128)(2,1)} %get-tuple-element.525), channel_id=1, source_target_pairs={{0,2},{1,3},{2,0},{3,1},{4,6},{5,7},{6,4},{7,5},{8,10},{9,11},{10,... | collective-permute-start | bytes 3686408 | tf_op jit(solution)/shard_map/ppermute | solution.py:102
  455.9 6.9 %copy-start.74 = (f32[96,16]{1,0:T(8,128)S(1)}, f32[96,16]{1,0:T(8,128)}, u32[]{:S(2)}) copy-start(f32[96,16]{1,0:T(8,128)} %copy-done.72) | copy-start | bytes 18436
  455.9 6.9 %copy-start.101 = (f32[96,4,16]{2,1,0:T(4,128)S(1)}, f32[96,4,16]{2,1,0:T(4,128)}, u32[]{:S(2)}) copy-start(f32[96,4,16]{2,1,0:T(4,128)} %copy.472) | copy-start | bytes 73732
  455.9 6.9 %copy-start.129 = (f32[1024]{0:T(1024)S(1)}, f32[1024]{0:T(1024)}, u32[]{:S(2)}) copy-start(f32[1024]{0:T(1024)} %multiply_add_fusion.4) | copy-start | bytes 12292
  455.9 6.9 %copy-start.133 = (f32[96]{0:T(128)S(1)}, f32[96]{0:T(128)}, u32[]{:S(2)}) copy-start(f32[96]{0:T(128)} %param.33) | copy-start | bytes 1156
  462.8 6.8 %copy-start.5 = (bf16[1536,768]{1,0:T(8,128)(2,1)S(1)}, bf16[1536,768]{1,0:T(8,128)(2,1)}, u32[]{:S(2)}) copy-start(bf16[1536,768]{1,0:T(8,128)(2,1)} %convolution_convert_fusion.3) | copy-start | bytes 7077892
  476.7 24.0 %copy-start.31 = (bf16[1,2,2,2,24,3200]{5,4,1,3,2,0:T(8,128)(2,1)S(1)}, bf16[1,2,2,2,24,3200]{5,4,1,3,2,0:T(8,128)(2,1)}, u32[]{:S(2)}) copy-start(bf16[1,2,2,2,24,3200]{5,4,1,3,2,0:T(8,128)(2,1)} %get-tuple-element.524) | copy-start | bytes 3686404
  477.5 43.2 %collective-permute-start.12 = (bf16[2,2,2,48,768]{4,3,0,2,1:T(8,128)(2,1)}, bf16[2,2,2,48,768]{4,3,0,2,1:T(8,128)(2,1)}, u32[]{:S(2)}, u32[]{:S(2)}) collective-permute-start(bf16[2,2,2,48,768]{4,3,0,2,1:T(8,128)(2,1)} %copy.509), channel_id=1, source_target_pairs={{0,4},{4,0},{8,12},{12,8},{16,20},{20,16},{24,28},{28,24},{1,5},{5... | collective-permute-start | bytes 1769480 | tf_op jit(solution)/shard_map/ppermute | solution.py:102
  481.6 43.6 %collective-permute-start.7 = (bf16[2,2,2,48,768]{4,3,2,1,0:T(8,128)(2,1)}, bf16[2,2,2,48,768]{4,3,2,1,0:T(8,128)(2,1)}, u32[]{:S(2)}, u32[]{:S(2)}) collective-permute-start(bf16[2,2,2,48,768]{4,3,2,1,0:T(8,128)(2,1)} %fusion.116), channel_id=1, source_target_pairs={{0,2},{1,3},{2,0},{3,1},{4,6},{5,7},{6,4},{7,5},{8,10},{9,11},{10,... | collective-permute-start | bytes 1769480 | tf_op jit(solution)/shard_map/ppermute | solution.py:102
  503.3 32.1 %collective-permute-start.2 = (bf16[1,2,2,24,3200]{4,3,2,1,0:T(8,128)(2,1)}, bf16[1,2,2,24,3200]{4,3,2,1,0:T(8,128)(2,1)}, u32[]{:S(2)}, u32[]{:S(2)}) collective-permute-start(bf16[1,2,2,24,3200]{4,3,2,1,0:T(8,128)(2,1)} %copy.493), channel_id=1, source_target_pairs={{0,4},{4,0},{8,12},{12,8},{16,20},{20,16},{24,28},{28,24},{1,5},{5... | collective-permute-start | bytes 1843208 | tf_op jit(solution)/shard_map/ppermute | solution.py:102
  505.5 15.2 %copy-start.49 = (bf16[2,2,2,1,48,768]{5,4,0,1,3,2:T(8,128)(2,1)S(1)}, bf16[2,2,2,1,48,768]{5,4,0,1,3,2:T(8,128)(2,1)}, u32[]{:S(2)}) copy-start(bf16[2,2,2,1,48,768]{5,4,0,1,3,2:T(8,128)(2,1)} %get-tuple-element.526) | copy-start | bytes 1769476
  521.9 11.6 %collective-permute-start.13 = (bf16[2,2,48,768]{3,2,0,1:T(8,128)(2,1)S(1)}, bf16[2,2,48,768]{3,2,0,1:T(8,128)(2,1)S(1)}, u32[]{:S(2)}, u32[]{:S(2)}) collective-permute-start(bf16[2,2,48,768]{3,2,0,1:T(8,128)(2,1)S(1)} %get-tuple-element.533), channel_id=1, source_target_pairs={{0,8},{4,12},{8,0},{12,4},{16,24},{20,28},{24,16},{28,20},{1,9},{5... | collective-permute-start | bytes 884744 | tf_op jit(solution)/shard_map/ppermute | solution.py:102
  526.2 16.5 %collective-permute-start.8 = (bf16[2,2,48,768]{3,2,1,0:T(8,128)(2,1)S(1)}, bf16[2,2,48,768]{3,2,1,0:T(8,128)(2,1)S(1)}, u32[]{:S(2)}, u32[]{:S(2)}) collective-permute-start(bf16[2,2,48,768]{3,2,1,0:T(8,128)(2,1)S(1)} %fusion.141), channel_id=1, source_target_pairs={{0,8},{4,12},{8,0},{12,4},{16,24},{20,28},{24,16},{28,20},{1,9},{5... | collective-permute-start | bytes 884744 | tf_op jit(solution)/shard_map/ppermute | solution.py:102
  533.6 9.7 %collective-permute-start.14 = (bf16[2,48,768]{2,1,0:T(8,128)(2,1)S(1)}, bf16[2,48,768]{2,1,0:T(8,128)(2,1)S(1)}, u32[]{:S(2)}, u32[]{:S(2)}) collective-permute-start(bf16[2,48,768]{2,1,0:T(8,128)(2,1)S(1)} %fusion.166), channel_id=1, source_target_pairs={{0,16},{4,20},{8,24},{12,28},{16,0},{20,4},{24,8},{28,12},{1,17},{... | collective-permute-start | bytes 442376 | tf_op jit(solution)/shard_map/ppermute | solution.py:102
  537.4 27.2 %collective-permute-start.3 = (bf16[1,2,24,3200]{3,2,1,0:T(8,128)(2,1)}, bf16[1,2,24,3200]{3,2,1,0:T(8,128)(2,1)}, u32[]{:S(2)}, u32[]{:S(2)}) collective-permute-start(bf16[1,2,24,3200]{3,2,1,0:T(8,128)(2,1)} %get-tuple-element.531), channel_id=1, source_target_pairs={{0,8},{4,12},{8,0},{12,4},{16,24},{20,28},{24,16},{28,20},{1,9},{5... | collective-permute-start | bytes 921608 | tf_op jit(solution)/shard_map/ppermute | solution.py:102
  542.8 9.0 %collective-permute-start.9 = (bf16[2,48,768]{2,1,0:T(8,128)(2,1)S(1)}, bf16[2,48,768]{2,1,0:T(8,128)(2,1)S(1)}, u32[]{:S(2)}, u32[]{:S(2)}) collective-permute-start(bf16[2,48,768]{2,1,0:T(8,128)(2,1)S(1)} %fusion.164), channel_id=1, source_target_pairs={{0,16},{4,20},{8,24},{12,28},{16,0},{20,4},{24,8},{28,12},{1,17},{... | collective-permute-start | bytes 442376 | tf_op jit(solution)/shard_map/ppermute | solution.py:102
  563.8 12.3 %copy-start.65 = (bf16[1,2,1,24,3200]{4,3,2,1,0:T(8,128)(2,1)S(1)}, bf16[1,2,1,24,3200]{4,3,2,1,0:T(8,128)(2,1)}, u32[]{:S(2)}) copy-start(bf16[1,2,1,24,3200]{4,3,2,1,0:T(8,128)(2,1)} %get-tuple-element.530) | copy-start | bytes 921604
  565.6 10.5 %collective-permute-start.4 = (bf16[1,24,3200]{2,1,0:T(8,128)(2,1)S(1)}, bf16[1,24,3200]{2,1,0:T(8,128)(2,1)S(1)}, u32[]{:S(2)}, u32[]{:S(2)}) collective-permute-start(bf16[1,24,3200]{2,1,0:T(8,128)(2,1)S(1)} %fusion.162), channel_id=1, source_target_pairs={{0,16},{4,20},{8,24},{12,28},{16,0},{20,4},{24,8},{28,12},{1,17},{... | collective-permute-start | bytes 460808 | tf_op jit(solution)/shard_map/ppermute | solution.py:102
  566.7 18.4 %copy-start.1 = (bf16[1536,768]{1,0:T(8,128)(2,1)S(1)}, bf16[1536,768]{1,0:T(8,128)(2,1)}, u32[]{:S(2)}) copy-start(bf16[1536,768]{1,0:T(8,128)(2,1)} %param.38) | copy-start | bytes 7077892
  (124 other events, 417.0 us)

commit v2 on v1

--- a/solution.py
+++ b/solution.py
@@ -1,30 +1,349 @@
 import jax
 import jax.numpy as jnp
 from jax import lax
+from jax.experimental import pallas as pl
+from jax.experimental.pallas import tpu as pltpu
 from jax.sharding import PartitionSpec as P
 
 GROUP = 128
-
-
-highest = lax.Precision.HIGHEST
-
-
-def prefix(shard, axis, combine, identity, reverse):
-    size, position = (lax.axis_size(axis), lax.axis_index(axis))
-    everything = jax.tree.map(lambda part: lax.all_gather(part, axis), shard)
-    start = jax.tree.map(
-        lambda part, zero: jnp.broadcast_to(jnp.asarray(zero, part.dtype), part.shape),
-        shard,
-        identity,
-    )
-
-    def lap(k, before):
-        at = size - 1 - k if reverse else k
-        reached = at > position if reverse else at < position
-        new = combine(before, jax.tree.map(lambda part: part[at], everything))
-        return jax.tree.map(lambda a, b: jnp.where(reached, a, b), new, before)
-
-    return lax.fori_loop(0, size, lap, start)
+SUB = 8
+LANES = 128
+f32 = jnp.float32
+
+
+def by_tile(shape, dim):
+    block = tuple(LANES if k == dim else size for k, size in enumerate(shape))
+    return pl.BlockSpec(block, lambda i: tuple(i if k == dim else 0 for k in range(len(shape))))
+
+
+def in_smem():
+    return pl.BlockSpec(memory_space=pltpu.SMEM)
+
+
+def roomy(mib=56):
+    return pltpu.CompilerParams(vmem_limit_bytes=mib * 1024 * 1024)
+
+
+def work(flops, moved, exps=0):
+    return pl.CostEstimate(flops=flops, bytes_accessed=moved, transcendentals=exps)
+
+
+def rates(params_ref):
+    rate = jax.nn.sigmoid(params_ref[0])
+    drop = rate * jax.nn.sigmoid(params_ref[1])
+    weight = params_ref[3] * rate * params_ref[2]
+    return 1.0 - drop, jnp.log1p(-drop), weight
+
+
+def spread(ref, j):
+    return jnp.broadcast_to(ref[pl.ds(j, 1), :], (SUB, LANES))
+
+
+def tree_sum(parts):
+    while len(parts) > 1:
+        parts = [a + b for a, b in zip(parts[::2], parts[1::2])] + parts[len(parts) & ~1 :]
+    return parts[0]
+
+
+def block_rows(g, t):
+    return pl.ds(g * GROUP + t, SUB, stride=GROUP)
+
+
+def state_rows(g, j, expand):
+    return pl.ds(g * expand + j, SUB, stride=expand)
+
+
+def ema_ends_kernel(x_ref, params_ref, xs_ref, ends_ref, total_ref, decay_ref):
+    length = x_ref.shape[1]
+    expand = params_ref.shape[1]
+    blocks = length // GROUP
+    decay, log_decay, _ = rates(params_ref)
+    decay_ref[...] = decay
+    for b in range(blocks):
+        rows = pl.ds(b * GROUP, GROUP)
+        xs_ref[rows, :] = x_ref[:, rows].astype(f32).T
+    factors = [spread(decay_ref, j) for j in range(expand)]
+    for g in range(0, blocks, SUB):
+
+        def step(t, states):
+            now = xs_ref[block_rows(g, t), :]
+            return tuple(f * s + now for f, s in zip(factors, states))
+
+        states = (jnp.zeros((SUB, LANES), f32),) * expand
+        states = lax.fori_loop(0, GROUP, step, states, unroll=8)
+        for j in range(expand):
+            ends_ref[state_rows(g, j, expand), :] = states[j]
+    jump = jnp.exp(GROUP * log_decay)
+    carry = jnp.zeros_like(jump)
+    for b in range(blocks):
+        carry = jump * carry + ends_ref[pl.ds(b * expand, expand), :]
+    total_ref[...] = carry
+
+
+def ema_ends(x, params):
+    columns, length = x.shape
+    expand = params.shape[1]
+    shapes = ((length, columns), (length // GROUP * expand, columns), (expand, columns))
+    return pl.pallas_call(
+        ema_ends_kernel,
+        grid=(columns // LANES,),
+        out_shape=tuple(jax.ShapeDtypeStruct(shape, f32) for shape in shapes),
+        in_specs=[by_tile(x.shape, 0), by_tile(params.shape, 2)],
+        out_specs=tuple(by_tile(shape, 1) for shape in shapes),
+        scratch_shapes=[pltpu.VMEM((expand, LANES), f32)],
+        compiler_params=roomy(),
+        cost_estimate=work(2 * expand * length * columns, 6 * length * columns),
+    )(x, params)
+
+
+def ema_mix_kernel(
+    place_ref, xs_ref, ends_ref, params_ref, omega_ref, totals_ref,
+    mixed_ref, slope_ref, entry_ref, decay_ref, weight_ref, smooth_ref,
+):
+    length = xs_ref.shape[0]
+    expand = params_ref.shape[1]
+    blocks = length // GROUP
+    decay, log_decay, weight = rates(params_ref)
+    decay_ref[...] = decay
+    weight_ref[...] = weight
+    whole = jnp.exp(length * log_decay)
+    jump = jnp.exp(GROUP * log_decay)
+    carry = jnp.zeros_like(jump)
+    for k in range(totals_ref.shape[0]):
+        carry = jnp.where(k < place_ref[0], whole * carry + totals_ref[k], carry)
+    for b in range(blocks):
+        rows = pl.ds(b * expand, expand)
+        entry_ref[rows, :] = carry
+        carry = jump * carry + ends_ref[rows, :]
+    factors = [spread(decay_ref, j) for j in range(expand)]
+    weights = [spread(weight_ref, j) for j in range(expand)]
+    for g in range(0, blocks, SUB):
+
+        def step(t, states):
+            now = xs_ref[block_rows(g, t), :]
+            states = tuple(f * s + now for f, s in zip(factors, states))
+            smooth_ref[block_rows(g, t), :] = tree_sum([w * s for w, s in zip(weights, states)])
+            return states
+
+        start = tuple(entry_ref[state_rows(g, j, expand), :] for j in range(expand))
+        lax.fori_loop(0, GROUP, step, start, unroll=8)
+    for b in range(blocks):
+        rows = pl.ds(b * GROUP, GROUP)
+        pre = smooth_ref[rows, :] + omega_ref[...] * xs_ref[rows, :]
+        sigma = jax.nn.sigmoid(pre)
+        mixed_ref[b] = (pre * sigma).T.astype(mixed_ref.dtype)
+        slope_ref[rows, :] = (sigma * (1.0 + pre * (1.0 - sigma))).astype(slope_ref.dtype)
+
+
+def ema_mix(place, xs, ends, params, omega, totals):
+    length, columns = xs.shape
+    expand = params.shape[1]
+    mixed = (length // GROUP, columns, GROUP)
+    return pl.pallas_call(
+        ema_mix_kernel,
+        grid=(columns // LANES,),
+        out_shape=(
+            jax.ShapeDtypeStruct(mixed, jnp.bfloat16),
+            jax.ShapeDtypeStruct(xs.shape, jnp.bfloat16),
+            jax.ShapeDtypeStruct(ends.shape, f32),
+        ),
+        in_specs=[
+            in_smem(), by_tile(xs.shape, 1), by_tile(ends.shape, 1), by_tile(params.shape, 2),
+            by_tile(omega.shape, 1), by_tile(totals.shape, 2),
+        ],
+        out_specs=(by_tile(mixed, 1), by_tile(xs.shape, 1), by_tile(ends.shape, 1)),
+        scratch_shapes=[
+            pltpu.VMEM((expand, LANES), f32),
+            pltpu.VMEM((expand, LANES), f32),
+            pltpu.VMEM((length, LANES), f32),
+        ],
+        compiler_params=roomy(),
+        cost_estimate=work(4 * expand * length * columns, 10 * length * columns, length * columns),
+    )(place, xs, ends, params, omega, totals)
+
+
+def ema_back_kernel(dmix_ref, slope_ref, params_ref, pull_ref, heads_ref, total_ref, decay_ref):
+    length = slope_ref.shape[0]
+    expand = params_ref.shape[1]
+    blocks = length // GROUP
+    decay, log_decay, _ = rates(params_ref)
+    decay_ref[...] = decay
+    for b in range(blocks):
+        rows = pl.ds(b * GROUP, GROUP)
+        pull_ref[rows, :] = dmix_ref[b].astype(f32).T * slope_ref[rows, :].astype(f32)
+    factors = [spread(decay_ref, j) for j in range(expand)]
+    for g in range(0, blocks, SUB):
+
+        def step(t, states):
+            now = pull_ref[block_rows(g, GROUP - 1 - t), :]
+            return tuple(f * s + now for f, s in zip(factors, states))
+
+        states = (jnp.zeros((SUB, LANES), f32),) * expand
+        states = lax.fori_loop(0, GROUP, step, states, unroll=8)
+        for j in range(expand):
+            heads_ref[state_rows(g, j, expand), :] = states[j]
+    jump = jnp.exp(GROUP * log_decay)
+    carry = jnp.zeros_like(jump)
+    for b in reversed(range(blocks)):
+        carry = jump * carry + heads_ref[pl.ds(b * expand, expand), :]
+    total_ref[...] = carry
+
+
+def ema_back(dmix, slope, params):
+    length, columns = slope.shape
+    expand = params.shape[1]
+    shapes = ((length, columns), (length // GROUP * expand, columns), (expand, columns))
+    return pl.pallas_call(
+        ema_back_kernel,
+        grid=(columns // LANES,),
+        out_shape=tuple(jax.ShapeDtypeStruct(shape, f32) for shape in shapes),
+        in_specs=[by_tile(dmix.shape, 1), by_tile(slope.shape, 1), by_tile(params.shape, 2)],
+        out_specs=tuple(by_tile(shape, 1) for shape in shapes),
+        scratch_shapes=[pltpu.VMEM((expand, LANES), f32)],
+        compiler_params=roomy(),
+        cost_estimate=work(2 * expand * length * columns, 8 * length * columns),
+    )(dmix, slope, params)
+
+
+def ema_sums_kernel(xs_ref, pull_ref, entry_ref, params_ref, sums_ref, tails_ref, decay_ref):
+    length = xs_ref.shape[0]
+    expand = params_ref.shape[1]
+    blocks = length // GROUP
+    half = expand // 2
+    decay, _, _ = rates(params_ref)
+    decay_ref[...] = decay
+    for low in range(0, expand, half):
+        factors = [spread(decay_ref, low + j) for j in range(half)]
+        zero = (jnp.zeros((SUB, LANES), f32),) * half
+        plain, turned = zero, zero
+        for g in range(0, blocks, SUB):
+
+            def step(t, held):
+                states, slants, plain, turned = held
+                now, pull = xs_ref[block_rows(g, t), :], pull_ref[block_rows(g, t), :]
+                slants = tuple(f * p + s for f, p, s in zip(factors, slants, states))
+                states = tuple(f * s + now for f, s in zip(factors, states))
+                plain = tuple(a + pull * s for a, s in zip(plain, states))
+                turned = tuple(a + pull * p for a, p in zip(turned, slants))
+                return states, slants, plain, turned
+
+            start = tuple(entry_ref[state_rows(g, low + j, expand), :] for j in range(half))
+            held = (start, zero, plain, turned)
+            _, slants, plain, turned = lax.fori_loop(0, GROUP, step, held, unroll=4)
+            for j in range(half):
+                tails_ref[state_rows(g, low + j, expand), :] = slants[j]
+        for j in range(half):
+            sums_ref[pl.ds(low + j, 1), :] = jnp.sum(plain[j], axis=0, keepdims=True)
+            sums_ref[pl.ds(expand + low + j, 1), :] = jnp.sum(turned[j], axis=0, keepdims=True)
+    straight = jnp.zeros((SUB, LANES), f32)
+    for b in range(0, length, SUB):
+        straight = straight + xs_ref[pl.ds(b, SUB), :] * pull_ref[pl.ds(b, SUB), :]
+    sums_ref[pl.ds(2 * expand, SUB), :] = straight
+
+
+def ema_sums(xs, pull, entry, params):
+    length, columns = xs.shape
+    expand = params.shape[1]
+    shapes = ((2 * expand + SUB, columns), entry.shape)
+    return pl.pallas_call(
+        ema_sums_kernel,
+        grid=(columns // LANES,),
+        out_shape=tuple(jax.ShapeDtypeStruct(shape, f32) for shape in shapes),
+        in_specs=[by_tile(xs.shape, 1), by_tile(xs.shape, 1), by_tile(entry.shape, 1), by_tile(params.shape, 2)],
+        out_specs=tuple(by_tile(shape, 1) for shape in shapes),
+        scratch_shapes=[pltpu.VMEM((expand, LANES), f32)],
+        compiler_params=roomy(),
+        cost_estimate=work(8 * expand * length * columns, 8 * length * columns),
+    )(xs, pull, entry, params)
+
+
+def ema_finish_kernel(
+    place_ref, pull_ref, heads_ref, params_ref, omega_ref, totals_ref, sums_ref, tails_ref, direct_ref,
+    grad_ref, total_ref, decay_ref, weight_ref, enter_ref, smooth_ref,
+):
+    length = pull_ref.shape[0]
+    expand = params_ref.shape[1]
+    blocks = length // GROUP
+    decay, log_decay, weight = rates(params_ref)
+    decay_ref[...] = decay
+    weight_ref[...] = weight
+    whole = jnp.exp(length * log_decay)
+    jump = jnp.exp(GROUP * log_decay)
+    carry = jnp.zeros_like(jump)
+    for k in reversed(range(totals_ref.shape[0])):
+        carry = jnp.where(k > place_ref[0], whole * carry + totals_ref[k], carry)
+    turned = sums_ref[pl.ds(expand, expand), :]
+    for b in reversed(range(blocks)):
+        rows = pl.ds(b * expand, expand)
+        enter_ref[rows, :] = carry
+        turned = turned + carry * decay * tails_ref[rows, :]
+        carry = jump * carry + heads_ref[rows, :]
+    total_ref[...] = sums_ref[...]
+    total_ref[pl.ds(expand, expand), :] = turned
+    factors = [spread(decay_ref, j) for j in range(expand)]
+    weights = [spread(weight_ref, j) for j in range(expand)]
+    for g in range(0, blocks, SUB):
+
+        def step(t, states):
+            now = pull_ref[block_rows(g, GROUP - 1 - t), :]
+            states = tuple(f * s + now for f, s in zip(factors, states))
+            back = tree_sum([w * s for w, s in zip(weights, states)])
+            smooth_ref[block_rows(g, GROUP - 1 - t), :] = back
+            return states
+
+        start = tuple(enter_ref[state_rows(g, j, expand), :] for j in range(expand))
+        lax.fori_loop(0, GROUP, step, start, unroll=8)
+    for b in range(blocks):
+        rows = pl.ds(b * GROUP, GROUP)
+        back = smooth_ref[rows, :] + omega_ref[...] * pull_ref[rows, :]
+        grad_ref[:, rows] = back.T + direct_ref[b].astype(f32)
+
+
+def ema_finish(place, pull, heads, params, omega, totals, sums, tails, direct):
+    length, columns = pull.shape
+    expand = params.shape[1]
+    return pl.pallas_call(
+        ema_finish_kernel,
+        grid=(columns // LANES,),
+        out_shape=(jax.ShapeDtypeStruct((columns, length), f32), jax.ShapeDtypeStruct(sums.shape, f32)),
+        in_specs=[
+            in_smem(), by_tile(pull.shape, 1), by_tile(heads.shape, 1), by_tile(params.shape, 2),
+            by_tile(omega.shape, 1), by_tile(totals.shape, 2), by_tile(sums.shape, 1),
+            by_tile(tails.shape, 1), by_tile(direct.shape, 1),
+        ],
+        out_specs=(by_tile((columns, length), 0), by_tile(sums.shape, 1)),
+        scratch_shapes=[
+            pltpu.VMEM((expand, LANES), f32),
+            pltpu.VMEM((expand, LANES), f32),
+            pltpu.VMEM((heads.shape[0], LANES), f32),
+            pltpu.VMEM((length, LANES), f32),
+        ],
+        compiler_params=roomy(),
+        cost_estimate=work(4 * expand * length * columns, 14 * length * columns),
+    )(place, pull, heads, params, omega, totals, sums, tails, direct)
+
+
+def pad_to_lanes(part, dim):
+    extra = -part.shape[dim] % LANES
+    if extra == 0:
+        return part
+    return jnp.pad(part, [(0, extra if k == dim else 0) for k in range(part.ndim)])
+
+
+def ema_params(alpha, delta, beta, eta, count):
+    packed = jnp.swapaxes(jnp.stack([alpha, delta, beta, eta]), 1, 2)
+    return pad_to_lanes(jnp.tile(packed, (1, 1, count)), 2)
+
+
+def ema_param_grads(total, alpha, delta, beta, eta, count):
+    channels, expand = alpha.shape
+    summed = jnp.sum(total[:, : count * channels].reshape(-1, count, channels), axis=1)
+    plain, turned = summed[:expand].T, summed[expand : 2 * expand].T
+    omega = jnp.sum(summed[2 * expand :], axis=0)
+    rate, damp = jax.nn.sigmoid(alpha), jax.nn.sigmoid(delta)
+    g_alpha = eta * beta * rate * (1.0 - rate) * (plain - damp * rate * turned)
+    g_delta = -(eta * beta * rate * rate * damp * (1.0 - damp)) * turned
+    return g_alpha, g_delta, rate * eta * plain, rate * beta * plain, omega
 
 
 def silu_slope(preact):
@@ -32,61 +351,18 @@
     return sigma * (1.0 + preact * (1.0 - sigma))
 
 
-def decay_logs(alpha_logit, delta_logit):
-    return jnp.log1p(-jax.nn.sigmoid(alpha_logit) * jax.nn.sigmoid(delta_logit))
-
-
-def ema_core(seq_f, alpha_logit, delta_logit, beta, eta, omega, state_in):
-    nseq_count, channels, local_len = seq_f.shape
-    blocks_n = local_len // GROUP
-    log_decay = decay_logs(alpha_logit, delta_logit)
-    scaled = jax.nn.sigmoid(alpha_logit) * beta
-    offsets = jnp.arange(GROUP, dtype=jnp.float32)
-    powers = jnp.exp(offsets[None, None, :] * log_decay[:, :, None])
-    kernel = jnp.einsum("dj,djt->dt", eta * scaled, powers, precision=highest)
-    lag = offsets[:, None] - offsets[None, :]
-    onehot = (lag[None] == offsets[:, None, None]).astype(jnp.float32)
-    toeplitz = jnp.einsum("dm,mts->dts", kernel, onehot, precision=highest)
-    blocks = seq_f.reshape(nseq_count, channels, blocks_n, GROUP)
-    inner = jnp.einsum("dts,ndbs->ndbt", toeplitz, blocks, precision=highest)
-    state_pow = scaled[:, :, None] * jnp.flip(powers, axis=2)
-    running = jnp.einsum("djs,ndbs->ndbj", state_pow, blocks, precision=highest)
-    span = 1
-    while span < blocks_n:
-        factor = jnp.exp(span * GROUP * log_decay)
-        moved = jnp.pad(running, ((0, 0), (0, 0), (span, 0), (0, 0)))[:, :, :blocks_n]
-        running = running + factor[None, :, None, :] * moved
-        span = span * 2
-    starts = jnp.pad(running, ((0, 0), (0, 0), (1, 0), (0, 0)))[:, :, :blocks_n]
-    group_ids = jnp.arange(blocks_n, dtype=jnp.float32)
-    entry = jnp.exp(group_ids[None, :, None] * (GROUP * log_decay)[:, None, :])
-    starts = starts + entry[None] * state_in[:, :, None, :]
-    carry_pow = eta[:, :, None] * powers * jnp.exp(log_decay)[:, :, None]
-    smooth = inner + jnp.einsum("djt,ndbj->ndbt", carry_pow, starts, precision=highest)
-    smooth = smooth.reshape(nseq_count, channels, local_len)
-    return jax.nn.silu(smooth + omega[None, :, None] * seq_f)
-
-
-def state_advance(seq_f, alpha_logit, delta_logit, beta, state_in):
-    local_len = seq_f.shape[2]
-    log_decay = decay_logs(alpha_logit, delta_logit)
-    scaled = jax.nn.sigmoid(alpha_logit) * beta
-    reverse_pos = jnp.arange(local_len - 1, -1, -1, dtype=jnp.float32)
-    weights = scaled[:, :, None] * jnp.exp(reverse_pos[None, None, :] * log_decay[:, :, None])
-    fresh = jnp.einsum("djs,nds->ndj", weights, seq_f, precision=highest)
-    return jnp.exp(local_len * log_decay)[None] * state_in + fresh
-
-
-def chain_combine(earlier, later):
-    return (earlier[0] * later[0], later[0][None] * earlier[1] + later[1])
-
-
-def to_rows(columns):
-    return jnp.swapaxes(columns, 1, 2).reshape(-1, columns.shape[1])
-
-
-def from_rows(table, nseq_count):
-    return jnp.swapaxes(table.reshape(nseq_count, -1, table.shape[1]), 1, 2)
+def to_rows(parts):
+    devices, count, channels, length = parts.shape
+    return parts.transpose(1, 3, 0, 2).reshape(count * length, devices * channels)
+
+
+def from_rows(table, count, devices):
+    length, channels = table.shape[0] // count, table.shape[1] // devices
+    return table.reshape(count, length, devices, channels).transpose(2, 0, 3, 1)
+
+
+def swap(parts):
+    return lax.all_to_all(parts, "ch", split_axis=0, concat_axis=0, tiled=True)
 
 
 ORDER_A = (("tok", 1), ("ch", 0))
@@ -168,19 +444,21 @@
     vwidth = w_value.shape[1]
     scale = zwidth ** (-0.5)
     tok_index = lax.axis_index("tok")
-    seq_f = inputs.astype(jnp.float32)
-    log_total = local_len * decay_logs(ema_alpha, ema_delta)
-    decay_all = jnp.exp(log_total)
-    zero_state = jnp.zeros((nseq_count, channels, ema_alpha.shape[1]), jnp.float32)
-    state_dev = state_advance(seq_f, ema_alpha, ema_delta, ema_beta, zero_state)
-    state_in = prefix(
-        (decay_all, state_dev), "tok", chain_combine, (jnp.ones_like(decay_all), zero_state), False
-    )[1]
-    activ = ema_core(seq_f, ema_alpha, ema_delta, ema_beta, ema_eta, ema_omega, state_in)
-    recv_in, recv_mix = (
-        lax.all_to_all(inputs, "ch", split_axis=2, concat_axis=1, tiled=True),
-        lax.all_to_all(activ.astype(jnp.bfloat16), "ch", split_axis=2, concat_axis=1, tiled=True),
-    )
+    devices = lax.axis_size("ch")
+    columns = nseq_count * channels
+    span = local_len // devices
+    place = tok_index.astype(jnp.int32)[None]
+
+    def by_block(part):
+        return part.reshape(nseq_count, channels, devices, span).transpose(2, 0, 1, 3)
+
+    recv_in = swap(by_block(inputs))
+    params = ema_params(ema_alpha, ema_delta, ema_beta, ema_eta, nseq_count)
+    omega = pad_to_lanes(jnp.tile(ema_omega, nseq_count)[None], 1)
+    xs, ends, total = ema_ends(pad_to_lanes(inputs.reshape(columns, local_len), 0), params)
+    totals = lax.all_gather(total, "tok")
+    mixed, slope, entry = ema_mix(place, xs, ends, params, omega, totals)
+    recv_mix = swap(mixed[:, :columns].reshape(devices, nseq_count, channels, span))
     tok_in = to_rows(recv_in)
     tok_mix = to_rows(recv_mix)
     row_count = tok_in.shape[0]
@@ -230,18 +508,12 @@
     ffn_pre = jnp.dot(normed_bf, w_up, preferred_element_type=jnp.float32) + b_up
     ffn_hidden = jax.nn.silu(ffn_pre).astype(jnp.bfloat16)
     result = normed + jnp.dot(ffn_hidden, w_down, preferred_element_type=jnp.float32) + b_down
-    out_local = lax.all_to_all(
-        from_rows(result.astype(jnp.bfloat16), nseq_count),
-        "ch",
-        split_axis=1,
-        concat_axis=2,
-        tiled=True,
-    )
+    out_local = swap(from_rows(result.astype(jnp.bfloat16), nseq_count, devices))
     seq_pos = tok_index * local_len + jnp.arange(local_len, dtype=jnp.int32)
     live = (seq_pos[None, :] < seq_lengths[:, None])[:, None, :]
+    out_local = out_local.transpose(1, 2, 0, 3).reshape(inputs.shape)
     output = jnp.where(live, out_local, jnp.zeros_like(out_local))
-    grad_masked = jnp.where(live, out_grad, jnp.zeros_like(out_grad))
-    grad_rows = to_rows(lax.all_to_all(grad_masked, "ch", split_axis=2, concat_axis=1, tiled=True))
+    grad_rows = to_rows(swap(by_block(jnp.where(live, out_grad, jnp.zeros_like(out_grad)))))
     grad_f = grad_rows.astype(jnp.float32)
     g_down = jnp.dot(ffn_hidden.T, grad_rows, preferred_element_type=jnp.float32)
     g_bdown = jnp.sum(grad_f, axis=0)
@@ -302,39 +574,20 @@
     g_mix = jnp.dot(tok_mix.T, d_mix_pre, preferred_element_type=jnp.float32)
     g_bmix = jnp.sum(d_mix_pre.astype(jnp.float32), axis=0)
     d_mix_in = jnp.dot(d_mix_pre, w_mix.T, preferred_element_type=jnp.float32)
-    back_resid, back_mix = (
-        lax.all_to_all(
-            from_rows(d_resid.astype(jnp.bfloat16), nseq_count),
-            "ch",
-            split_axis=1,
-            concat_axis=2,
-            tiled=True,
-        ),
-        lax.all_to_all(
-            from_rows(d_mix_in.astype(jnp.bfloat16), nseq_count),
-            "ch",
-            split_axis=1,
-            concat_axis=2,
-            tiled=True,
-        ),
-    )
-    _, ema_pull = jax.vjp(
-        ema_core, seq_f, ema_alpha, ema_delta, ema_beta, ema_eta, ema_omega, state_in
-    )
-    dx_ema, ga_first, gd_first, gb_first, g_eta, g_omega, state_grad = ema_pull(
-        back_mix.astype(jnp.float32)
-    )
-    later_grad = prefix(
-        (decay_all, state_grad), "tok", chain_combine, (jnp.ones_like(decay_all), zero_state), True
-    )[1]
-    _, state_pull = jax.vjp(state_advance, seq_f, ema_alpha, ema_delta, ema_beta, state_in)
-    dx_state, ga_second, gd_second, gb_second, unused_grad = state_pull(later_grad)
-    input_grad = back_resid.astype(jnp.float32) + dx_ema + dx_state
+    back_mix = swap(from_rows(d_mix_in.astype(jnp.bfloat16), nseq_count, devices))
+    back_resid = swap(from_rows(d_resid.astype(jnp.bfloat16), nseq_count, devices))
+    back_mix = pad_to_lanes(back_mix.reshape(devices, columns, span), 1)
+    back_resid = pad_to_lanes(back_resid.reshape(devices, columns, span), 1)
+    pull, heads, total = ema_back(back_mix, slope, params)
+    totals = lax.all_gather(total, "tok")
+    sums, tails = ema_sums(xs, pull, entry, params)
+    input_grad, sums = ema_finish(place, pull, heads, params, omega, totals, sums, tails, back_resid)
+    input_grad = input_grad[:columns].reshape(inputs.shape)
     g_up_s, g_down_s = reduce_pair(g_up, g_down, ORDER_A)
     g_value_s, g_out_s = reduce_pair(g_value, g_out, ORDER_B)
     g_mix_s = reduce_rows(g_mix.astype(jnp.bfloat16)[None], ORDER_A)[0]
-    ema_grads = lax.psum(
-        (ga_first + ga_second, gd_first + gd_second, gb_first + gb_second, g_eta, g_omega), "tok"
+    ema_grads = ema_param_grads(
+        lax.psum(sums, "tok"), ema_alpha, ema_delta, ema_beta, ema_eta, nseq_count
     )
     summed = (g_mix_s, g_value_s, g_out_s, g_up_s, g_down_s) + ema_grads
     smalls = lax.psum(

time: 594 us -> 477 us (0.80)
  matrix products: 140 us -> 64.4 us
  local copies, waits for them, and re-layouts: 119 us -> 63.6 us
  Pallas kernels: 0 us -> 37.9 us
  blocking collectives: 95.1 us -> 122 us
  waiting for transfers between devices: 105 us -> 85.6 us
  other arithmetic: 73.6 us -> 54.7 us
  starting transfers between devices: 50.1 us -> 42 us
    dot_general x16 -> x0, matrix products: 82.8 us -> none  [the longest x3 28.2 us: ema_core(): inner = jnp.einsum('dts,ndbs->ndbt', toeplitz, blocks, precision=highest)]
    pallas_call x0 -> x5, Pallas kernels: none -> 37.9 us  [the longest x1 12.6 us: ema_sums(): pl.pallas_call(ema_sums_kernel, grid=(columns // LANES,), out_shape=tuple...]
    psum x1, blocking collectives: 42.2 us -> 72.8 us  [local(): lax.psum((g_bmix, g_bvalue, g_bout, g_qscale, g_qshift, g_gain, g_lnbias,...]
    all_to_all x6, waiting for transfers between devices: 66.3 us -> 55.1 us  [swap(): return lax.all_to_all(parts, 'ch', split_axis=0, concat_axis=0, tiled=True)]
    convert_element_type x5 -> x3, local copies, waits for them, and re-layouts: 13.1 us -> 4.28 us  [the longest x1 1.45 us: local(): d_resid.astype(jnp.bfloat16)]
    reduce_sum x4 -> x2, other arithmetic: 10.8 us -> 2.76 us  [the longest x1 1.54 us: ema_param_grads(): jnp.sum(total[:, :count * channels].reshape(-1, count, channels), axis=1)]
    ppermute x15, waiting for transfers between devices: 38.4 us -> 30.5 us  [exchange(): return lax.ppermute(part, axis, [(i, i ^ 1 << bit) for i in range(size)])]
    unnamed x306 -> x160, local copies, waits for them, and re-layouts: 19.4 us -> 11.9 us
  transfers between devices with their start and end apart: 21 -> 21, of which waited for: 8 -> 9; matrix products, arithmetic and copies ran while one was open for 39% -> 17% of each run, Pallas kernels for 0% -> 8%
where the time goes in v2:
time: 477 us; the launch traced here: 472 us
  blocking collectives  122 us (26%)
  waiting for transfers between devices  85.6 us (18%)
  matrix products  64.4 us (14%)
  local copies, waits for them, and re-layouts  63.6 us (13%)
  other arithmetic  54.7 us (11%)
  starting transfers between devices  42 us (9%)
  Pallas kernels  37.9 us (8%)
    psum x1, blocking collectives, local(): lax.psum((g_bmix, g_bvalue, g_bout, g_qscale, g_qshift, g_gain, g_lnbias,...  72.8 us
    all_to_all x6, waiting for transfers between devices, swap(): return lax.all_to_all(parts, 'ch', split_axis=0, concat_axis=0, tiled=True)  55.1 us
    ppermute x15, waiting for transfers between devices, exchange(): return lax.ppermute(part, axis, [(i, i ^ 1 << bit) for i in range(size)])  30.5 us
    all_to_all x6, starting transfers between devices, swap(): return lax.all_to_all(parts, 'ch', split_axis=0, concat_axis=0, tiled=True)  30 us
    all_gather x3, blocking collectives, reduce_rows(): whole = lax.all_gather(total, 'tok', axis=1)  22.6 us
    convert_element_type x15, other arithmetic, pick(): (half.astype(jnp.float32) + other.astype(jnp.float32)).astype(jnp.bfloat16)  20.1 us
    psum x1, blocking collectives, local(): lax.psum(sums, 'tok')  13.8 us
    all_gather x2, blocking collectives, local(): totals = lax.all_gather(total, 'tok')  12.8 us
  transfers between devices with their start and end apart: 21, of which 9 were waited for; matrix products, arithmetic and copies ran while one was open for 17% of the time, Pallas kernels for 8%

profile of v2, /device:TPU:0, one launch (start us, length us, event | category | flops | bytes accessed | tf_op | source)
XLA Modules:
  0.0 472.2 jit_solution(13710706563900446081)
XLA Ops:
  3.7 7.3 %all-to-all-start.1 = ((bf16[8,4,96,128]{3,1,2,0:T(4,128)(2,1)}), bf16[8,4,96,128]{3,1,2,0:T(4,128)(2,1)S(1)}, u32[]{:S(2)}, u32[]{:S(2)}) async-start(bf16[8,4,96,128]{3,1,2,0:T(4,128)(2,1)} %bitcast.346), calls=%async_computation.1 | async-start | bytes 1572864 | tf_op jit(solution)/shard_map/all_to_all | solution.py:365
  12.4 4.9 %shard_map.373 = (f32[1024,384]{1,0:T(8,128)}, f32[128,384]{1,0:T(8,128)}, f32[16,384]{1,0:T(8,128)}) custom-call(bf16[384,1024]{1,0:T(8,128)(2,1)} %bitcast.340, f32[4,16,384]{2,1,0:T(8,128)} %tile.7.params_ref), custom_call_target="tpu_custom_call" | custom-call | flops 12582912 | bytes 2359296 | tf_op jit(solution)/shard_map/pallas_call | solution.py:87
  17.3 6.8 %all-gather = f32[64,384]{1,0:T(8,128)} all-gather(f32[16,384]{1,0:T(8,128)} %get-tuple-element.36), channel_id=2, replica_groups=mesh['ch'=8,'tok'=4] {'tok'}, dimensions={0}, use_global_device_ids=true | all-gather | bytes 122880 | tf_op jit(solution)/shard_map/all_gather | solution.py:459
  24.1 7.2 %shard_map.374 = (bf16[8,384,128]{2,1,0:T(8,128)(2,1)}, bf16[1024,384]{1,0:T(8,128)(2,1)}, f32[128,384]{1,0:T(8,128)}) custom-call(s32[1]{0:T(128)} %bitcast.place_ref, f32[1024,384]{1,0:T(8,128)} %get-tuple-element.34.xs_ref, f32[128,384]{1,0:T(8,128)} %get-tuple-element.35.ends_ref, f32[4,16,384]{2,1,0:T(8,128)} %tile.7.params_ref, ...), custom_call_target="tpu_custom_call" | custom-call | flops 25165824 | bytes 3932160 | tf_op jit(solution)/shard_map/pallas_call | solution.py:142
  31.3 2.5 copy.134
  34.6 6.3 %all-to-all-start = ((bf16[8,4,96,128]{3,1,2,0:T(4,128)(2,1)}), bf16[8,4,96,128]{3,1,2,0:T(4,128)(2,1)S(1)}, u32[]{:S(2)}, u32[]{:S(2)}) async-start(bf16[8,4,96,128]{3,1,2,0:T(4,128)(2,1)} %copy.134), calls=%async_computation | async-start | bytes 1572864 | tf_op jit(solution)/shard_map/all_to_all | solution.py:365
  45.5 16.1 %all-to-all-done = bf16[8,4,96,128]{3,1,2,0:T(4,128)(2,1)S(1)} async-done(((bf16[8,4,96,128]{3,1,2,0:T(4,128)(2,1)}), bf16[8,4,96,128]{3,1,2,0:T(4,128)(2,1)S(1)}, u32[]{:S(2)}, u32[]{:S(2)}) %all-to-all-start) | async-done | bytes 786464 | tf_op jit(solution)/shard_map/all_to_all | solution.py:365
  61.6 5.6 %convolution_add_fusion = f32[512,3200]{1,0:T(8,128)S(1)} fusion(bf16[768,3200]{1,0:T(8,128)(2,1)} %param.30, f32[3200]{0:T(1024)S(1)} %copy-done.50, bf16[96,8,4,128]{3,2,1,0:T(4,128)(2,1)S(1)} %bitcast.337), kind=kOutput, calls=%fused_computation.2 | convolution fusion | flops 2518220800 | bytes 12268032 | tf_op jit(solution)/shard_map/dot_general | solution.py:468
  67.7 3.6 multiply_convert_fusion.2
  74.8 3.1 fusion.80
  81.9 2.8 add_convert_fusion.1
  87.1 4.1 all-to-all-start.2
  91.9 19.3 %all-to-all-done.2 = bf16[8,4,96,128]{3,1,2,0:T(4,128)(2,1)S(1)} async-done(((bf16[8,4,96,128]{3,1,2,0:T(4,128)(2,1)}), bf16[8,4,96,128]{3,1,2,0:T(4,128)(2,1)S(1)}, u32[]{:S(2)}, u32[]{:S(2)}) %all-to-all-start.2) | async-done | bytes 786464 | tf_op jit(solution)/shard_map/all_to_all | solution.py:365
  117.9 3.5 all-to-all-start.3
  122.0 19.8 %all-to-all-done.3 = bf16[8,4,96,128]{3,1,2,0:T(4,128)(2,1)S(1)} async-done(((bf16[8,4,96,128]{3,1,2,0:T(4,128)(2,1)}), bf16[8,4,96,128]{3,1,2,0:T(4,128)(2,1)S(1)}, u32[]{:S(2)}, u32[]{:S(2)}) %all-to-all-start.3) | async-done | bytes 786464 | tf_op jit(solution)/shard_map/all_to_all | solution.py:365
  142.8 6.6 %convert_reduce_fusion.1 = (f32[1536]{0:T(1024)}, bf16[512,1536]{1,0:T(8,128)(2,1)}) fusion(f32[512,1536]{1,0:T(8,128)} %copy-done.73, bf16[1536,768]{1,0:T(8,128)(2,1)} %param.42, bf16[96,8,4,128]{3,2,1,0:T(4,128)(2,1)S(1)} %bitcast.327), kind=kOutput, calls=%fused_computation.30 | convolution fusion | flops 1216608768 | bytes 7870464 | tf_op jit(solution)/shard_map/dot_general | solution.py:521
  149.4 3.5 convolution_convert_fusion.1
  155.2 5.4 %multiply_reduce_fusion = (f32[768]{0:T(1024)}, f32[512]{0:T(512)S(1)}, f32[512]{0:T(512)S(1)}, f32[768]{0:T(1024)}, f32[512,768]{1,0:T(8,128)S(1)}) fusion(f32[512,768]{1,0:T(8,128)} %copy-done.9, f32[512]{0:T(512)S(1)} %add_rsqrt_fusion, f32[512]{0:T(512)S(1)} %broadcast_multiply_fusion.2, f32[768]{0:T(1024)S(1)} %copy-done.54, ...), kind=kOutput, calls=%fused_computation.72 | convolution fusion | flops 1212282368 | bytes 7881728 | tf_op jit(solution)/shard_map/dot_general | solution.py:525
  160.6 5.0 %convert_reduce_fusion.4 = (f32[768]{0:T(1024)}, bf16[512,768]{1,0:T(8,128)(2,1)S(1)}, bf16[512,768]{1,0:T(8,128)(2,1)}) fusion(f32[512,768]{1,0:T(8,128)S(1)} %copy-done.34, f32[512,3200]{1,0:T(8,128)} %copy-done.2, f32[512]{0:T(512)S(1)} %broadcast_multiply_fusion, f32[512,768]{1,0:T(8,128)S(1)} %copy-done.10, f32[512]{0:T(512)S(1)} %broadcast_multiply_fusion.2, ...), kind=kLoop, calls=%fused_computation.73 | loop fusion | flops 11795712 | bytes 8665088 | tf_op jit(solution)/shard_map/reduce_sum | solution.py:538
  165.7 5.7 %multiply_convert_fusion = (bf16[512,1536]{1,0:T(8,128)(2,1)S(1)}, bf16[512,1536]{1,0:T(8,128)(2,1)}) fusion(f32[512,3200]{1,0:T(8,128)} %copy-done.2, f32[4,128,1536]{2,1,0:T(8,128)S(1)} %copy-done.6, bf16[512,768]{1,0:T(8,128)(2,1)S(1)} %get-tuple-element.63, bf16[1536,768]{1,0:T(8,128)(2,1)S(1)} %copy-done), kind=kOutput, calls=%fused_computation.32 | convolution fusion | flops 1218183168 | bytes 12582912 | tf_op jit(solution)/shard_map/dot_general | solution.py:539
  174.1 2.9 convolution_convert_fusion.3
  183.3 4.7 convert_reduce_fusion.2
  188.0 2.9 fusion.5
  190.9 4.3 copy.152
  195.1 3.5 stack.54
  198.6 3.4 copy_bitcast_fusion.1
  206.7 4.0 convolution_convert_fusion
  213.7 3.7 convolution_convert_fusion.5
  224.7 4.2 all-to-all-start.4
  229.0 6.0 %add_convert_fusion = bf16[512,768]{1,0:T(8,128)(2,1)} fusion(bf16[512,1536]{1,0:T(8,128)(2,1)} %copy-done.31, bf16[768,1536]{1,0:T(8,128)(2,1)} %param.32, f32[512,768]{1,0:T(8,128)} %copy-done.9, f32[512,768]{1,0:T(8,128)} %copy-done.35, f32[512]{0:T(512)S(1)} %broadcast_multiply_fusion, f32[512]{0:T(512)S(1)} %copy-done.52, f32[768]{0:T(1024)S(1)} %copy-done.56, ...), kind=kOutput, calls=%fused_computation.74 | convolution fusion | flops 1213464576 | bytes 9448448 | tf_op jit(solution)/shard_map/dot_general | solution.py:567
  240.5 3.3 constant_dynamic-slice_fusion.4
  243.9 3.5 fusion.12
  248.1 2.6 fusion.13
  252.5 4.6 all-to-all-start.5
  257.1 4.5 fusion.8
  264.7 72.8 %all-reduce = (f32[3200]{0:T(1024)}, f32[1536]{0:T(1024)}, f32[768]{0:T(1024)}, f32[2,128]{1,0:T(2,128)}, f32[2,128]{1,0:T(2,128)}, /*index=5*/f32[768]{0:T(1024)}, f32[768]{0:T(1024)}, f32[1536]{0:T(1024)}, f32[768]{0:T(1024)}) all-reduce(f32[3200]{0:T(1024)S(1)} %convert_reduce_fusion, ...), channel_id=1, replica_groups=mesh['ch'=8,'tok'=4] {'ch','tok'}, use_global_device_ids=true, to_apply=%region_11.12 | all-reduce | flops 9856 | bytes 78848 | tf_op jit(solution)/shard_map/psum | solution.py:593
  341.9 5.2 %shard_map.375 = (f32[1024,384]{1,0:T(8,128)}, f32[128,384]{1,0:T(8,128)}, f32[16,384]{1,0:T(8,128)}) custom-call(bf16[8,384,128]{2,1,0:T(8,128)(2,1)} %bitcast.348, bf16[1024,384]{1,0:T(8,128)(2,1)} %get-tuple-element.38.slope_ref, f32[4,16,384]{2,1,0:T(8,128)} %tile.7.params_ref), custom_call_target="tpu_custom_call" | custom-call | flops 12582912 | bytes 3145728 | tf_op jit(solution)/shard_map/pallas_call | solution.py:196
  347.1 12.6 %shard_map.376 = (f32[40,384]{1,0:T(8,128)}, f32[128,384]{1,0:T(8,128)}) custom-call(f32[1024,384]{1,0:T(8,128)} %get-tuple-element.34.xs_ref, f32[1024,384]{1,0:T(8,128)} %get-tuple-element.39.pull_ref, f32[128,384]{1,0:T(8,128)} %get-tuple-element.42.entry_ref, f32[4,16,384]{2,1,0:T(8,128)} %tile.7.params_ref), custom_call_target="tpu_custom_call" | custom-call | flops 50331648 | bytes 3145728 | tf_op jit(solution)/shard_map/pallas_call | solution.py:248
  359.7 6.0 %all-gather.1 = f32[64,384]{1,0:T(8,128)} all-gather(f32[16,384]{1,0:T(8,128)S(1)} %copy-done.49), channel_id=3, replica_groups=mesh['ch'=8,'tok'=4] {'tok'}, dimensions={0}, use_global_device_ids=true | all-gather | bytes 122880 | tf_op jit(solution)/shard_map/all_gather | solution.py:582
  365.7 8.1 %shard_map.377 = (f32[384,1024]{1,0:T(8,128)}, f32[40,384]{1,0:T(8,128)}) custom-call(s32[1]{0:T(128)} %bitcast.place_ref, f32[1024,384]{1,0:T(8,128)} %get-tuple-element.39.pull_ref, f32[128,384]{1,0:T(8,128)} %get-tuple-element.40.heads_ref, f32[4,16,384]{2,1,0:T(8,128)} %tile.7.params_ref, f32[1,384]{1,0:T(1,128)} %broadcast_in_dim_tile.3.omega_ref, ...), custom_call_target="tpu_custom_call" | custom-call | flops 25165824 | bytes 5505024 | tf_op jit(solution)/shard_map/pallas_call | solution.py:305
  375.4 13.8 %psum.70 = f32[40,4,96]{2,1,0:T(4,128)} all-reduce(f32[40,4,96]{2,1,0:T(4,128)} %reshape.654), channel_id=1, replica_groups=mesh['ch'=8,'tok'=4] {'tok'}, use_global_device_ids=true, to_apply=%region_7.8 | all-reduce | flops 15360 | bytes 122880 | tf_op jit(solution)/shard_map/psum | solution.py:590
  402.1 9.7 %collective-permute-done.12 = bf16[2,2,2,48,768]{4,3,0,2,1:T(8,128)(2,1)S(1)} collective-permute-done((bf16[2,2,2,48,768]{4,3,0,2,1:T(8,128)(2,1)S(1)}, bf16[2,2,2,48,768]{4,3,0,2,1:T(8,128)(2,1)S(1)}, u32[]{:S(2)}, u32[]{:S(2)}) %collective-permute-start.12) | collective-permute-done | bytes 589856 | tf_op jit(solution)/shard_map/ppermute | solution.py:378
  415.5 6.4 %collective-permute-done.13 = bf16[2,2,48,768]{3,2,0,1:T(8,128)(2,1)S(1)} collective-permute-done((bf16[2,2,48,768]{3,2,0,1:T(8,128)(2,1)S(1)}, bf16[2,2,48,768]{3,2,0,1:T(8,128)(2,1)S(1)}, u32[]{:S(2)}, u32[]{:S(2)}) %collective-permute-start.13) | collective-permute-done | bytes 294944 | tf_op jit(solution)/shard_map/ppermute | solution.py:378
  426.5 4.7 collective-permute-done.14
  431.2 7.5 %all-gather.4 = bf16[2,192,768]{2,1,0:T(8,128)(2,1)S(1)} all-gather(bf16[2,48,768]{2,1,0:T(8,128)(2,1)S(1)} %fusion.53), channel_id=6, replica_groups=mesh['ch'=8,'tok'=4] {'tok'}, dimensions={1}, use_global_device_ids=true | all-gather | bytes 737280 | tf_op jit(solution)/shard_map/all_gather | solution.py:405
  438.8 7.7 %all-gather.3 = bf16[2,192,768]{2,1,0:T(8,128)(2,1)S(1)} all-gather(bf16[2,48,768]{2,1,0:T(8,128)(2,1)S(1)} %fusion.56), channel_id=5, replica_groups=mesh['ch'=8,'tok'=4] {'tok'}, dimensions={1}, use_global_device_ids=true | all-gather | bytes 737280 | tf_op jit(solution)/shard_map/all_gather | solution.py:405
  453.5 8.8 %collective-permute-done.4 = bf16[1,24,3200]{2,1,0:T(8,128)(2,1)S(1)} collective-permute-done((bf16[1,24,3200]{2,1,0:T(8,128)(2,1)S(1)}, bf16[1,24,3200]{2,1,0:T(8,128)(2,1)S(1)}, u32[]{:S(2)}, u32[]{:S(2)}) %collective-permute-start.4) | collective-permute-done | bytes 153632 | tf_op jit(solution)/shard_map/ppermute | solution.py:378
  463.3 7.5 %all-gather.2 = bf16[4,24,3200]{2,1,0:T(8,128)(2,1)S(1)} all-gather(bf16[1,24,3200]{2,1,0:T(8,128)(2,1)S(1)} %fusion.48), channel_id=4, replica_groups=mesh['ch'=8,'tok'=4] {'tok'}, dimensions={0}, use_global_device_ids=true | all-gather | bytes 768000 | tf_op jit(solution)/shard_map/all_gather | solution.py:405
  (277 shorter events, 102.7 us)
Async XLA Ops:
  0.7 74.2 %copy-start = (bf16[1536,768]{1,0:T(8,128)(2,1)S(1)}, bf16[1536,768]{1,0:T(8,128)(2,1)}, u32[]{:S(2)}) copy-start(bf16[1536,768]{1,0:T(8,128)(2,1)} %param.34) | copy-start | bytes 7077892
  2.1 8.8 %copy-start.63 = (f32[96]{0:T(128)S(1)}, f32[96]{0:T(128)}, u32[]{:S(2)}) copy-start(f32[96]{0:T(128)} %param.29) | copy-start | bytes 1156
  2.1 9.5 %copy-start.43 = (f32[96,16]{0,1:T(8,128)S(1)}, f32[96,16]{0,1:T(8,128)}, u32[]{:S(2)}) copy-start(f32[96,16]{0,1:T(8,128)} %param.28) | copy-start | bytes 18436
  2.2 9.4 %copy-start.45 = (f32[96,16]{0,1:T(8,128)S(1)}, f32[96,16]{0,1:T(8,128)}, u32[]{:S(2)}) copy-start(f32[96,16]{0,1:T(8,128)} %param.27) | copy-start | bytes 18436
  2.2 9.4 %copy-start.47 = (f32[96,16]{0,1:T(8,128)S(1)}, f32[96,16]{0,1:T(8,128)}, u32[]{:S(2)}) copy-start(f32[96,16]{0,1:T(8,128)} %param.26) | copy-start | bytes 18436
  2.2 9.4 %copy-start.48 = (f32[96,16]{0,1:T(8,128)S(1)}, f32[96,16]{0,1:T(8,128)}, u32[]{:S(2)}) copy-start(f32[96,16]{0,1:T(8,128)} %param.25) | copy-start | bytes 18436
  3.7 30.1 %all-to-all-start.1 = ((bf16[8,4,96,128]{3,1,2,0:T(4,128)(2,1)}), bf16[8,4,96,128]{3,1,2,0:T(4,128)(2,1)S(1)}, u32[]{:S(2)}, u32[]{:S(2)}) async-start(bf16[8,4,96,128]{3,1,2,0:T(4,128)(2,1)} %bitcast.346), calls=%async_computation.1 | async-start | bytes 1572864 | tf_op jit(solution)/shard_map/all_to_all | solution.py:365
  31.3 9.7 %copy-start.57 = (f32[2,128]{1,0:T(2,128)S(1)}, f32[2,128]{1,0:T(2,128)}, u32[]{:S(2)}) copy-start(f32[2,128]{1,0:T(2,128)} %param.36) | copy-start | bytes 3076
  31.3 9.7 %copy-start.62 = (f32[2,128]{1,0:T(2,128)S(1)}, f32[2,128]{1,0:T(2,128)}, u32[]{:S(2)}) copy-start(f32[2,128]{1,0:T(2,128)} %param.37) | copy-start | bytes 3076
  34.6 26.9 %all-to-all-start = ((bf16[8,4,96,128]{3,1,2,0:T(4,128)(2,1)}), bf16[8,4,96,128]{3,1,2,0:T(4,128)(2,1)S(1)}, u32[]{:S(2)}, u32[]{:S(2)}) async-start(bf16[8,4,96,128]{3,1,2,0:T(4,128)(2,1)} %copy.134), calls=%async_computation | async-start | bytes 1572864 | tf_op jit(solution)/shard_map/all_to_all | solution.py:365
  41.0 20.6 %copy-start.50 = (f32[3200]{0:T(1024)S(1)}, f32[3200]{0:T(1024)}, u32[]{:S(2)}) copy-start(f32[3200]{0:T(1024)} %param.31) | copy-start | bytes 38404
  61.6 6.1 %copy-start.67 = (f32[1536]{0:T(1024)S(1)}, f32[1536]{0:T(1024)}, u32[]{:S(2)}) copy-start(f32[1536]{0:T(1024)} %param.33) | copy-start | bytes 18436
  67.2 6.8 %copy-start.2 = (f32[512,3200]{1,0:T(8,128)}, f32[512,3200]{1,0:T(8,128)S(1)}, u32[]{:S(2)}) copy-start(f32[512,3200]{1,0:T(8,128)S(1)} %convolution_add_fusion) | copy-start | bytes 19660804
  87.1 24.1 %all-to-all-start.2 = ((bf16[8,4,96,128]{3,1,2,0:T(4,128)(2,1)}), bf16[8,4,96,128]{3,1,2,0:T(4,128)(2,1)S(1)}, u32[]{:S(2)}, u32[]{:S(2)}) async-start(bf16[8,4,96,128]{3,1,2,0:T(4,128)(2,1)} %bitcast.349), calls=%async_computation.2 | async-start | bytes 1572864 | tf_op jit(solution)/shard_map/all_to_all | solution.py:365
  117.9 23.9 %all-to-all-start.3 = ((bf16[8,4,96,128]{3,1,2,0:T(4,128)(2,1)}), bf16[8,4,96,128]{3,1,2,0:T(4,128)(2,1)S(1)}, u32[]{:S(2)}, u32[]{:S(2)}) async-start(bf16[8,4,96,128]{3,1,2,0:T(4,128)(2,1)} %bitcast.344), calls=%async_computation.3 | async-start | bytes 1572864 | tf_op jit(solution)/shard_map/all_to_all | solution.py:365
  142.8 6.6 %copy-start.74 = (f32[512,1536]{1,0:T(8,128)S(1)}, f32[512,1536]{1,0:T(8,128)}, u32[]{:S(2)}) copy-start(f32[512,1536]{1,0:T(8,128)} %copy-done.73) | copy-start | bytes 9437188
  165.6 8.4 %copy-start.20 = (bf16[512,768]{1,0:T(8,128)(2,1)}, bf16[512,768]{1,0:T(8,128)(2,1)S(1)}, u32[]{:S(2)}) copy-start(bf16[512,768]{1,0:T(8,128)(2,1)S(1)} %get-tuple-element.63) | copy-start | bytes 2359300
  198.6 8.0 %copy-start.29 = (bf16[512,1536]{1,0:T(8,128)(2,1)S(1)}, bf16[512,1536]{1,0:T(8,128)(2,1)}, u32[]{:S(2)}) copy-start(bf16[512,1536]{1,0:T(8,128)(2,1)} %get-tuple-element.70) | copy-start | bytes 4718596
  202.1 41.8 %collective-permute-start.10 = (bf16[2,2,2,2,2,48,768]{6,5,0,1,3,2,4:T(8,128)(2,1)}, bf16[2,2,2,2,2,48,768]{6,5,0,1,3,2,4:T(8,128)(2,1)}, u32[]{:S(2)}, u32[]{:S(2)}) collective-permute-start(bf16[2,2,2,2,2,48,768]{6,5,0,1,3,2,4:T(8,128)(2,1)} %copy_bitcast_fusion.1), channel_id=1, source_target_pairs={{0,1},{1,0},{2,3},{3,2},{4,5},{5,4},{6,7},{7,6},{8,9},{9,8},{10,11... | collective-permute-start | bytes 7077896 | tf_op jit(solution)/shard_map/ppermute | solution.py:378
  202.2 11.5 %slice-start = ((s8[4915200]{0:T(1024)(128)(4,1)}), s8[4194304]{0:T(1024)(128)(4,1)S(1)}, s32[]{:S(2)}) async-start(s8[4915200]{0:T(1024)(128)(4,1)} %bitcast.335), calls=%async_computation.6 | async-start | bytes 8388608
  203.7 44.3 %collective-permute-start.5 = (bf16[2,2,2,2,2,48,768]{6,5,0,1,4,2,3:T(8,128)(2,1)}, bf16[2,2,2,2,2,48,768]{6,5,0,1,4,2,3:T(8,128)(2,1)}, u32[]{:S(2)}, u32[]{:S(2)}) collective-permute-start(bf16[2,2,2,2,2,48,768]{6,5,0,1,4,2,3:T(8,128)(2,1)} %copy_bitcast_fusion.2), channel_id=1, source_target_pairs={{0,1},{1,0},{2,3},{3,2},{4,5},{5,4},{6,7},{7,6},{8,9},{9,8},{10,11... | collective-permute-start | bytes 7077896 | tf_op jit(solution)/shard_map/ppermute | solution.py:378
  206.7 7.0 %copy-start.41 = (bf16[512,128]{1,0:T(8,128)(2,1)}, bf16[512,128]{1,0:T(8,128)(2,1)S(1)}, u32[]{:S(2)}) copy-start(bf16[512,128]{1,0:T(8,128)(2,1)S(1)} %get-tuple-element.71) | copy-start | bytes 393220
  206.7 7.0 %slice-start.1 = ((s8[4915200]{0:T(1024)(128)(4,1)}), s8[720896]{0:T(1024)(128)(4,1)S(1)}, s32[]{:S(2)}) async-start(s8[4915200]{0:T(1024)(128)(4,1)} %bitcast.335), calls=%async_computation.7 | async-start | bytes 1441792
  213.6 43.5 %collective-permute-start = (bf16[1,2,2,2,2,24,3200]{6,5,1,3,2,4,0:T(8,128)(2,1)}, bf16[1,2,2,2,2,24,3200]{6,5,1,3,2,4,0:T(8,128)(2,1)}, u32[]{:S(2)}, u32[]{:S(2)}) collective-permute-start(bf16[1,2,2,2,2,24,3200]{6,5,1,3,2,4,0:T(8,128)(2,1)} %copy_bitcast_fusion), channel_id=1, source_target_pairs={{0,1},{1,0},{2,3},{3,2},{4,5},{5,4},{6,7},{7,6},{8,9},{9,8},{10,11... | collective-permute-start | bytes 7372808 | tf_op jit(solution)/shard_map/ppermute | solution.py:378
  224.7 27.8 %all-to-all-start.4 = ((bf16[8,4,96,128]{3,1,2,0:T(4,128)(2,1)}), bf16[8,4,96,128]{3,1,2,0:T(4,128)(2,1)}, u32[]{:S(2)}, u32[]{:S(2)}) async-start(bf16[8,4,96,128]{3,1,2,0:T(4,128)(2,1)} %bitcast.27), calls=%async_computation.4 | async-start | bytes 1572864 | tf_op jit(solution)/shard_map/all_to_all | solution.py:365
  247.3 146.5 %collective-permute-start.11 = (bf16[2,2,2,2,48,768]{5,4,0,1,3,2:T(8,128)(2,1)}, bf16[2,2,2,2,48,768]{5,4,0,1,3,2:T(8,128)(2,1)}, u32[]{:S(2)}, u32[]{:S(2)}) collective-permute-start(bf16[2,2,2,2,48,768]{5,4,0,1,3,2:T(8,128)(2,1)} %get-tuple-element.85), channel_id=1, source_target_pairs={{0,2},{1,3},{2,0},{3,1},{4,6},{5,7},{6,4},{7,5},{8,10},{9,11},{10,... | collective-permute-start | bytes 3538952 | tf_op jit(solution)/shard_map/ppermute | solution.py:378
  250.6 145.5 %collective-permute-start.6 = (bf16[2,2,2,2,48,768]{5,4,3,2,1,0:T(8,128)(2,1)}, bf16[2,2,2,2,48,768]{5,4,3,2,1,0:T(8,128)(2,1)}, u32[]{:S(2)}, u32[]{:S(2)}) collective-permute-start(bf16[2,2,2,2,48,768]{5,4,3,2,1,0:T(8,128)(2,1)} %fusion.13), channel_id=1, source_target_pairs={{0,4},{4,0},{8,12},{12,8},{16,20},{20,16},{24,28},{28,24},{1,5},{5... | collective-permute-start | bytes 3538952 | tf_op jit(solution)/shard_map/ppermute | solution.py:378
  252.5 87.2 %all-to-all-start.5 = ((bf16[8,4,96,128]{3,1,2,0:T(4,128)(2,1)}), bf16[8,4,96,128]{3,1,2,0:T(4,128)(2,1)}, u32[]{:S(2)}, u32[]{:S(2)}) async-start(bf16[8,4,96,128]{3,1,2,0:T(4,128)(2,1)} %bitcast.345), calls=%async_computation.5 | async-start | bytes 1572864 | tf_op jit(solution)/shard_map/all_to_all | solution.py:365
  257.1 6.5 %copy-start.59 = (f32[128]{0:T(128)S(1)}, f32[128]{0:T(128)}, u32[]{:S(2)}) copy-start(f32[128]{0:T(128)} %get-tuple-element.48) | copy-start | bytes 1540
  257.1 7.0 %copy-start.22 = (bf16[512,768]{1,0:T(8,128)(2,1)S(1)}, bf16[512,768]{1,0:T(8,128)(2,1)}, u32[]{:S(2)}) copy-start(bf16[512,768]{1,0:T(8,128)(2,1)} %copy-done.20) | copy-start | bytes 2359300
  257.1 7.0 %copy-start.24 = (bf16[512,768]{1,0:T(8,128)(2,1)S(1)}, bf16[512,768]{1,0:T(8,128)(2,1)}, u32[]{:S(2)}) copy-start(bf16[512,768]{1,0:T(8,128)(2,1)} %get-tuple-element.68) | copy-start | bytes 2359300
  257.1 7.0 %copy-start.30 = (bf16[512,1536]{1,0:T(8,128)(2,1)S(1)}, bf16[512,1536]{1,0:T(8,128)(2,1)}, u32[]{:S(2)}) copy-start(bf16[512,1536]{1,0:T(8,128)(2,1)} %get-tuple-element.70) | copy-start | bytes 4718596
  257.1 7.0 %copy-start.42 = (bf16[512,128]{1,0:T(8,128)(2,1)S(1)}, bf16[512,128]{1,0:T(8,128)(2,1)}, u32[]{:S(2)}) copy-start(bf16[512,128]{1,0:T(8,128)(2,1)} %copy-done.41) | copy-start | bytes 393220
  261.7 137.1 %collective-permute-start.1 = (bf16[1,2,2,2,24,3200]{5,4,1,3,2,0:T(8,128)(2,1)}, bf16[1,2,2,2,24,3200]{5,4,1,3,2,0:T(8,128)(2,1)}, u32[]{:S(2)}, u32[]{:S(2)}) collective-permute-start(bf16[1,2,2,2,24,3200]{5,4,1,3,2,0:T(8,128)(2,1)} %get-tuple-element.81), channel_id=1, source_target_pairs={{0,2},{1,3},{2,0},{3,1},{4,6},{5,7},{6,4},{7,5},{8,10},{9,11},{10,... | collective-permute-start | bytes 3686408 | tf_op jit(solution)/shard_map/ppermute | solution.py:378
  347.1 12.6 %copy-start.49 = (f32[16,384]{1,0:T(8,128)S(1)}, f32[16,384]{1,0:T(8,128)}, u32[]{:S(2)}) copy-start(f32[16,384]{1,0:T(8,128)} %get-tuple-element.41) | copy-start | bytes 73732
  365.7 25.1 %copy-start.44 = (f32[96,16]{0,1:T(8,128)S(1)}, f32[96,16]{0,1:T(8,128)}, u32[]{:S(2)}) copy-start(f32[96,16]{0,1:T(8,128)} %param.28) | copy-start | bytes 18436
  365.7 25.1 %copy-start.46 = (f32[96,16]{0,1:T(8,128)S(1)}, f32[96,16]{0,1:T(8,128)}, u32[]{:S(2)}) copy-start(f32[96,16]{0,1:T(8,128)} %param.27) | copy-start | bytes 18436
  395.4 16.3 %collective-permute-start.12 = (bf16[2,2,2,48,768]{4,3,0,2,1:T(8,128)(2,1)S(1)}, bf16[2,2,2,48,768]{4,3,0,2,1:T(8,128)(2,1)S(1)}, u32[]{:S(2)}, u32[]{:S(2)}) collective-permute-start(bf16[2,2,2,48,768]{4,3,0,2,1:T(8,128)(2,1)S(1)} %copy.166), channel_id=1, source_target_pairs={{0,4},{4,0},{8,12},{12,8},{16,20},{20,16},{24,28},{28,24},{1,5},{5... | collective-permute-start | bytes 1769480 | tf_op jit(solution)/shard_map/ppermute | solution.py:378
  397.3 16.4 %collective-permute-start.7 = (bf16[2,2,2,48,768]{4,3,2,1,0:T(8,128)(2,1)S(1)}, bf16[2,2,2,48,768]{4,3,2,1,0:T(8,128)(2,1)S(1)}, u32[]{:S(2)}, u32[]{:S(2)}) collective-permute-start(bf16[2,2,2,48,768]{4,3,2,1,0:T(8,128)(2,1)S(1)} %fusion.41), channel_id=1, source_target_pairs={{0,2},{1,3},{2,0},{3,1},{4,6},{5,7},{6,4},{7,5},{8,10},{9,11},{10,... | collective-permute-start | bytes 1769480 | tf_op jit(solution)/shard_map/ppermute | solution.py:378
  400.3 22.4 %collective-permute-start.2 = (bf16[1,2,2,24,3200]{4,3,2,1,0:T(8,128)(2,1)S(1)}, bf16[1,2,2,24,3200]{4,3,2,1,0:T(8,128)(2,1)S(1)}, u32[]{:S(2)}, u32[]{:S(2)}) collective-permute-start(bf16[1,2,2,24,3200]{4,3,2,1,0:T(8,128)(2,1)S(1)} %copy.150), channel_id=1, source_target_pairs={{0,4},{4,0},{8,12},{12,8},{16,20},{20,16},{24,28},{28,24},{1,5},{5... | collective-permute-start | bytes 1843208 | tf_op jit(solution)/shard_map/ppermute | solution.py:378
  411.9 10.0 %collective-permute-start.13 = (bf16[2,2,48,768]{3,2,0,1:T(8,128)(2,1)S(1)}, bf16[2,2,48,768]{3,2,0,1:T(8,128)(2,1)S(1)}, u32[]{:S(2)}, u32[]{:S(2)}) collective-permute-start(bf16[2,2,48,768]{3,2,0,1:T(8,128)(2,1)S(1)} %get-tuple-element.89), channel_id=1, source_target_pairs={{0,8},{4,12},{8,0},{12,4},{16,24},{20,28},{24,16},{28,20},{1,9},{5... | collective-permute-start | bytes 884744 | tf_op jit(solution)/shard_map/ppermute | solution.py:378
  413.8 11.3 %collective-permute-start.8 = (bf16[2,2,48,768]{3,2,1,0:T(8,128)(2,1)S(1)}, bf16[2,2,48,768]{3,2,1,0:T(8,128)(2,1)S(1)}, u32[]{:S(2)}, u32[]{:S(2)}) collective-permute-start(bf16[2,2,48,768]{3,2,1,0:T(8,128)(2,1)S(1)} %fusion.50), channel_id=1, source_target_pairs={{0,8},{4,12},{8,0},{12,4},{16,24},{20,28},{24,16},{28,20},{1,9},{5... | collective-permute-start | bytes 884744 | tf_op jit(solution)/shard_map/ppermute | solution.py:378
  421.9 9.2 %collective-permute-start.14 = (bf16[2,48,768]{2,1,0:T(8,128)(2,1)S(1)}, bf16[2,48,768]{2,1,0:T(8,128)(2,1)S(1)}, u32[]{:S(2)}, u32[]{:S(2)}) collective-permute-start(bf16[2,48,768]{2,1,0:T(8,128)(2,1)S(1)} %fusion.72), channel_id=1, source_target_pairs={{0,16},{4,20},{8,24},{12,28},{16,0},{20,4},{24,8},{28,12},{1,17},{... | collective-permute-start | bytes 442376 | tf_op jit(solution)/shard_map/ppermute | solution.py:378
  423.8 27.8 %collective-permute-start.3 = (bf16[1,2,24,3200]{3,2,1,0:T(8,128)(2,1)}, bf16[1,2,24,3200]{3,2,1,0:T(8,128)(2,1)}, u32[]{:S(2)}, u32[]{:S(2)}) collective-permute-start(bf16[1,2,24,3200]{3,2,1,0:T(8,128)(2,1)} %get-tuple-element.87), channel_id=1, source_target_pairs={{0,8},{4,12},{8,0},{12,4},{16,24},{20,28},{24,16},{28,20},{1,9},{5... | collective-permute-start | bytes 921608 | tf_op jit(solution)/shard_map/ppermute | solution.py:378
  425.1 13.7 %collective-permute-start.9 = (bf16[2,48,768]{2,1,0:T(8,128)(2,1)S(1)}, bf16[2,48,768]{2,1,0:T(8,128)(2,1)S(1)}, u32[]{:S(2)}, u32[]{:S(2)}) collective-permute-start(bf16[2,48,768]{2,1,0:T(8,128)(2,1)S(1)} %fusion.70), channel_id=1, source_target_pairs={{0,16},{4,20},{8,24},{12,28},{16,0},{20,4},{24,8},{28,12},{1,17},{... | collective-permute-start | bytes 442376 | tf_op jit(solution)/shard_map/ppermute | solution.py:378
  450.7 11.6 %copy-start.37 = (bf16[1,2,1,24,3200]{4,3,2,1,0:T(8,128)(2,1)S(1)}, bf16[1,2,1,24,3200]{4,3,2,1,0:T(8,128)(2,1)}, u32[]{:S(2)}) copy-start(bf16[1,2,1,24,3200]{4,3,2,1,0:T(8,128)(2,1)} %get-tuple-element.86) | copy-start | bytes 921604
  452.5 9.7 %collective-permute-start.4 = (bf16[1,24,3200]{2,1,0:T(8,128)(2,1)S(1)}, bf16[1,24,3200]{2,1,0:T(8,128)(2,1)S(1)}, u32[]{:S(2)}, u32[]{:S(2)}) collective-permute-start(bf16[1,24,3200]{2,1,0:T(8,128)(2,1)S(1)} %fusion.68), channel_id=1, source_target_pairs={{0,16},{4,20},{8,24},{12,28},{16,0},{20,4},{24,8},{28,12},{1,17},{... | collective-permute-start | bytes 460808 | tf_op jit(solution)/shard_map/ppermute | solution.py:378
  452.6 19.3 %copy-start.1 = (bf16[1536,768]{1,0:T(8,128)(2,1)S(1)}, bf16[1536,768]{1,0:T(8,128)(2,1)}, u32[]{:S(2)}) copy-start(bf16[1536,768]{1,0:T(8,128)(2,1)} %param.34) | copy-start | bytes 7077892
  (51 other events, 167.9 us)

commit v3 on v2

--- a/solution.py
+++ b/solution.py
@@ -1,3 +1,4 @@
+import functools
 import jax
 import jax.numpy as jnp
 from jax import lax
@@ -346,27 +347,465 @@
     return g_alpha, g_delta, rate * eta * plain, rate * beta * plain, omega
 
 
-def silu_slope(preact):
-    sigma = jax.nn.sigmoid(preact)
-    return sigma * (1.0 + preact * (1.0 - sigma))
-
-
-def to_rows(parts):
-    devices, count, channels, length = parts.shape
-    return parts.transpose(1, 3, 0, 2).reshape(count * length, devices * channels)
-
-
-def from_rows(table, count, devices):
-    length, channels = table.shape[0] // count, table.shape[1] // devices
-    return table.reshape(count, length, devices, channels).transpose(2, 0, 3, 1)
-
-
-def swap(parts):
-    return lax.all_to_all(parts, "ch", split_axis=0, concat_axis=0, tiled=True)
-
-
-ORDER_A = (("tok", 1), ("ch", 0))
-ORDER_B = (("ch", 0), ("tok", 1))
+low = jnp.bfloat16
+CHUNK = 256
+
+
+def nn(left, right):
+    return jnp.dot(left, right, preferred_element_type=f32)
+
+
+def nt(left, right):
+    return lax.dot_general(left, right, (((1,), (1,)), ((), ())), preferred_element_type=f32)
+
+
+def silu_pair(pre):
+    sigma = jax.nn.sigmoid(pre)
+    return pre * sigma, sigma * (1.0 + pre * (1.0 - sigma))
+
+
+def each(width, body, size=CHUNK, unroll=1):
+    def lap(i, none):
+        body(pl.multiple_of(i * size, size))
+        return none
+
+    lax.fori_loop(0, width // size, lap, 0, unroll=unroll)
+
+
+def fetch(pairs, sems):
+    copies = [pltpu.make_async_copy(src, dst, sems.at[i]) for i, (src, dst) in enumerate(pairs)]
+    for copy in copies:
+        copy.start()
+    return copies
+
+
+def wide_block(ref, n):
+    part = ref[:, n]
+    return part.reshape(part.shape[0] * part.shape[1], part.shape[2])
+
+
+def live_lanes(place_ref, lengths_ref, n, shape):
+    return place_ref[0] + lax.broadcasted_iota(jnp.int32, shape, 1) < lengths_ref[n]
+
+
+def span_of(ref, n):
+    return pl.ds(n * GROUP, GROUP)
+
+
+def call(kernel, outs, ins, smem=0, hbm=0, scratch=(), flops=0, moved=0):
+    spaces = [pltpu.SMEM] * smem + [pl.ANY] * hbm + [pltpu.VMEM] * (len(ins) - smem - hbm)
+    return pl.pallas_call(
+        kernel,
+        out_shape=tuple(jax.ShapeDtypeStruct(shape, kind) for shape, kind in outs),
+        in_specs=[pl.BlockSpec(memory_space=space) for space in spaces],
+        out_specs=tuple(pl.BlockSpec(memory_space=pltpu.VMEM) for _ in outs),
+        scratch_shapes=list(scratch),
+        compiler_params=roomy(58),
+        cost_estimate=work(flops, moved),
+    )(*ins)
+
+
+def vectors(width, mwidth, vwidth, ff):
+    sizes = (
+        ("mix", mwidth), ("value", vwidth), ("out", width), ("gain", width),
+        ("shift", width), ("up", ff), ("down", width),
+    )
+    place, at = {}, 0
+    for name, size in sizes:
+        place[name] = at
+        at += size
+    return place
+
+
+def piece(ref, base, at, size):
+    return ref[:, pl.ds(pl.multiple_of(base + at, 128), size)]
+
+
+def value_kernel(base, w_hbm, x_ref, vec_ref, rows_ref, values_ref, slope_ref, w_ref, sems):
+    copies = fetch([(w_hbm, w_ref)], sems)
+    for n in range(x_ref.shape[1]):
+        rows_ref[pl.ds(n * GROUP, GROUP), :] = wide_block(x_ref, n).T
+    copies[0].wait()
+
+    def chunk(at):
+        cols = pl.ds(at, CHUNK)
+        act, slope = silu_pair(nn(rows_ref[...], w_ref[:, cols]) + piece(vec_ref, base, at, CHUNK))
+        values_ref[:, cols] = act.astype(low)
+        slope_ref[:, cols] = slope.astype(low)
+
+    each(w_ref.shape[1], chunk)
+
+
+def value_part(x, w_value, vec, where):
+    width, vwidth = w_value.shape
+    count = x.shape[1] * GROUP
+    return call(
+        functools.partial(value_kernel, where["value"]),
+        [((count, width), low), ((count, vwidth), low), ((count, vwidth), low)],
+        (w_value, x, vec),
+        hbm=1,
+        scratch=[pltpu.VMEM(w_value.shape, low), pltpu.SemaphoreType.DMA((1,))],
+        flops=2 * count * width * vwidth,
+        moved=8 * count * vwidth,
+    )
+
+
+def forward_kernel(
+    where, place_ref, lengths_ref, wmix_hbm, wout_hbm, wup_hbm, wdown_hbm,
+    mixed_ref, x_ref, values_ref, vec_ref, qscale_ref, qshift_ref,
+    out_ref, query_ref, key_ref, shared_ref, qslope_ref, probs_ref, reset_ref, turned_ref, gated_t_ref,
+    hslope_ref, uslope_ref, keep_ref, unit_ref, rstd_ref, normed_t_ref, hidden_t_ref, fslope_ref,
+    wmix_ref, wout_ref, wup_ref, wdown_ref, m_ref, update_ref, gated_ref, blend_ref, normed_ref, ffn_ref, sems,
+):
+    width, vwidth = wout_ref.shape[1], wout_ref.shape[0]
+    zwidth = qscale_ref.shape[1]
+    seqs = mixed_ref.shape[1]
+    copies = fetch(
+        [(wmix_hbm, wmix_ref), (wout_hbm, wout_ref), (wup_hbm, wup_ref), (wdown_hbm, wdown_ref)], sems
+    )
+    for n in range(seqs):
+        m_ref[pl.ds(n * GROUP, GROUP), :] = wide_block(mixed_ref, n).T
+    copies[0].wait()
+
+    def mix(at, size=CHUNK):
+        cols = pl.ds(at, size)
+        return nn(m_ref[...], wmix_ref[:, cols]) + piece(vec_ref, where["mix"], at, size)
+
+    shared, qslope = silu_pair(mix(width, zwidth))
+    shared_ref[...] = shared
+    qslope_ref[...] = qslope
+    query_ref[...] = (shared * qscale_ref[pl.ds(0, 1), :] + qshift_ref[pl.ds(0, 1), :]).astype(low)
+    key_ref[...] = (shared * qscale_ref[pl.ds(1, 1), :] + qshift_ref[pl.ds(1, 1), :]).astype(low)
+    causal = lax.broadcasted_iota(jnp.int32, (GROUP, GROUP), 0) >= lax.broadcasted_iota(
+        jnp.int32, (GROUP, GROUP), 1
+    )
+    for n in range(seqs):
+        rows = pl.ds(n * GROUP, GROUP)
+        scores = jnp.where(causal, nt(query_ref[rows, :], key_ref[rows, :]) * zwidth**-0.5, -1e30)
+        scores = jnp.exp(scores - jnp.max(scores, axis=-1, keepdims=True))
+        probs_ref[rows, :] = scores / jnp.sum(scores, axis=-1, keepdims=True)
+
+    def gate(at):
+        update_ref[:, pl.ds(at, CHUNK)] = jax.nn.sigmoid(mix(at))
+
+    each(width, gate)
+
+    def attend(at):
+        cols = pl.ds(at, CHUNK)
+        reset, slope = silu_pair(mix(pl.multiple_of(width + zwidth + at, 128)))
+        attended = jnp.concatenate(
+            [
+                nn(probs_ref[pl.ds(n * GROUP, GROUP), :].astype(low), values_ref[pl.ds(n * GROUP, GROUP), cols])
+                for n in range(seqs)
+            ],
+            axis=0,
+        )
+        reset_ref[:, cols] = reset.astype(low)
+        turned_ref[:, cols] = (attended * slope).astype(low)
+        gated = (reset * attended).astype(low)
+        gated_ref[:, cols] = gated
+        gated_t_ref[cols, :] = gated.T
+
+    each(vwidth, attend)
+    copies[1].wait()
+
+    def hide(at):
+        cols = pl.ds(at, CHUNK)
+        pre = mix(pl.multiple_of(width + zwidth + vwidth + at, 128))
+        pre = pre + nn(gated_ref[...], wout_ref[:, cols]) + piece(vec_ref, where["out"], at, CHUNK)
+        hidden, slope = silu_pair(pre)
+        update = update_ref[:, cols]
+        keep = 1.0 - update
+        resid = x_ref[:, cols].astype(f32)
+        hslope_ref[:, cols] = (update * slope).astype(low)
+        uslope_ref[:, cols] = ((hidden - resid) * update * keep).astype(low)
+        keep_ref[:, cols] = keep.astype(low)
+        blend_ref[:, cols] = update * hidden + keep * resid
+
+    each(width, hide)
+    for n in range(seqs):
+        rows = pl.ds(n * GROUP, GROUP)
+        blend = blend_ref[rows, :]
+        centered = blend - jnp.mean(blend, axis=-1, keepdims=True)
+        rstd = lax.rsqrt(jnp.mean(centered * centered, axis=-1, keepdims=True) + 1e-05)
+        unit = centered * rstd
+        unit_ref[rows, :] = unit.astype(low)
+        rstd_ref[rows, :] = jnp.broadcast_to(rstd, (GROUP, LANES))
+        normed = unit * piece(vec_ref, where["gain"], 0, width) + piece(vec_ref, where["shift"], 0, width)
+        blend_ref[rows, :] = normed
+        normed_ref[rows, :] = normed.astype(low)
+        normed_t_ref[:, rows] = normed.astype(low).T
+    copies[2].wait()
+
+    def lift(at):
+        cols = pl.ds(at, CHUNK)
+        act, slope = silu_pair(nn(normed_ref[...], wup_ref[:, cols]) + piece(vec_ref, where["up"], at, CHUNK))
+        fslope_ref[:, cols] = slope.astype(low)
+        act = act.astype(low)
+        ffn_ref[:, cols] = act
+        hidden_t_ref[cols, :] = act.T
+
+    each(wup_ref.shape[1], lift)
+    copies[3].wait()
+
+    def drop(at):
+        cols = pl.ds(at, CHUNK)
+        blend_ref[:, cols] = blend_ref[:, cols] + nn(ffn_ref[...], wdown_ref[:, cols]) + piece(vec_ref, where["down"], at, CHUNK)
+
+    each(width, drop)
+    for n in range(seqs):
+        result = blend_ref[pl.ds(n * GROUP, GROUP), :].astype(low).T
+        result = jnp.where(live_lanes(place_ref, lengths_ref, n, result.shape), result, jnp.zeros_like(result))
+        out_ref[:, n] = result.reshape(out_ref.shape[0], out_ref.shape[2], GROUP)
+
+
+def forward_part(place, lengths, mixed, x, values, w_mix, w_out, w_up, w_down, vec, where, qk_scale, qk_shift):
+    vwidth, width = w_out.shape
+    zwidth = qk_scale.shape[1]
+    ff = w_up.shape[1]
+    count = x.shape[0]
+    narrow, wide = (count, width), (count, vwidth)
+    outs = [
+        (mixed.shape, low), ((count, zwidth), low), ((count, zwidth), low), ((count, zwidth), f32),
+        ((count, zwidth), f32), ((count, GROUP), f32), (wide, low), (wide, low), ((vwidth, count), low),
+        (narrow, low), (narrow, low), (narrow, low), (narrow, low), ((count, LANES), f32),
+        ((width, count), low), ((ff, count), low), ((count, ff), low),
+    ]
+    scratch = [pltpu.VMEM(w.shape, low) for w in (w_mix, w_out, w_up, w_down)]
+    scratch += [pltpu.VMEM(narrow, low), pltpu.VMEM(narrow, f32), pltpu.VMEM(wide, low)]
+    scratch += [pltpu.VMEM(narrow, f32), pltpu.VMEM(narrow, low), pltpu.VMEM((count, ff), low)]
+    scratch += [pltpu.SemaphoreType.DMA((4,))]
+    macs = w_mix.size + w_out.size + w_up.size + w_down.size
+    return call(
+        functools.partial(forward_kernel, where),
+        outs,
+        (place, lengths, w_mix, w_out, w_up, w_down, mixed, x, values, vec, qk_scale, qk_shift),
+        smem=2,
+        hbm=4,
+        scratch=scratch,
+        flops=2 * count * macs,
+        moved=2 * macs + 30 * count * width,
+    )
+
+
+def column_sum(part):
+    return jnp.sum(part.astype(f32), axis=0, keepdims=True)
+
+
+def split_product(side, keep_ref, send_ref, left, right_ref):
+    half = keep_ref.shape[1]
+    total = right_ref.shape[1]
+    for ref, which in ((keep_ref, side), (send_ref, 1 - side)):
+        base = which * (total - half)
+        for at in range(0, half, CHUNK):
+            size = min(CHUNK, half - at)
+            cols = pl.ds(pl.multiple_of(base + at, 128), size)
+            ref[:, pl.ds(at, size)] = nn(left, right_ref[:, cols]).astype(low)
+
+
+def split_narrow(side, keep_ref, send_ref, left_ref, right_ref):
+    half = keep_ref.shape[1]
+
+    def chunk(at):
+        rows = pl.ds(at, CHUNK)
+        both = nn(left_ref[rows, :], right_ref[...]).astype(low)
+        near, far = both[:, :half], both[:, half:]
+        keep_ref[rows, :] = jnp.where(side == 0, near, far)
+        send_ref[rows, :] = jnp.where(side == 0, far, near)
+
+    each(left_ref.shape[0], chunk)
+
+
+def back_ffn_kernel(
+    base, place_ref, lengths_ref, side_ref, wdown_hbm, wup_hbm,
+    grad_ref, hidden_t_ref, fslope_ref, normed_t_ref, unit_ref, rstd_ref, vec_ref, hslope_ref, uslope_ref, kept_ref,
+    down_keep_ref, down_send_ref, up_keep_ref, up_send_ref, dh_ref, du_ref, direct_ref,
+    small_ref,
+    wdown_ref, wup_ref, g_ref, dffn_ref, dn_ref, sems,
+):
+    width, ff = wup_ref.shape
+    seqs = grad_ref.shape[1]
+    copies = fetch([(wdown_hbm, wdown_ref), (wup_hbm, wup_ref)], sems)
+    for n in range(seqs):
+        part = wide_block(grad_ref, n)
+        part = jnp.where(live_lanes(place_ref, lengths_ref, n, part.shape), part, jnp.zeros_like(part))
+        g_ref[pl.ds(n * GROUP, GROUP), :] = part.T
+    small_ref[:, pl.ds(0, width)] = column_sum(g_ref[...])
+    split_narrow(side_ref[0], down_keep_ref, down_send_ref, hidden_t_ref, g_ref)
+    copies[0].wait()
+
+    def lift(at):
+        part = pl.ds(at, CHUNK)
+        pulled = (nt(g_ref[...], wdown_ref[part, :]) * fslope_ref[:, part].astype(f32)).astype(low)
+        dffn_ref[:, part] = pulled
+        small_ref[:, pl.ds(pl.multiple_of(width + at, 128), CHUNK)] = column_sum(pulled)
+
+    each(ff, lift)
+    split_product(side_ref[0], up_keep_ref, up_send_ref, normed_t_ref[...], dffn_ref)
+    copies[1].wait()
+
+    def drop(at):
+        part = pl.ds(at, CHUNK)
+        pulled = g_ref[:, part].astype(f32) + nt(dffn_ref[...], wup_ref[part, :])
+        dn_ref[:, part] = pulled
+        turned = column_sum(pulled * unit_ref[:, part].astype(f32))
+        small_ref[:, pl.ds(pl.multiple_of(width + ff + at, 128), CHUNK)] = turned
+        small_ref[:, pl.ds(pl.multiple_of(2 * width + ff + at, 128), CHUNK)] = column_sum(pulled)
+
+    each(width, drop)
+    for n in range(seqs):
+        rows = pl.ds(n * GROUP, GROUP)
+        unit = unit_ref[rows, :].astype(f32)
+        pulled = dn_ref[rows, :] * piece(vec_ref, base, 0, width)
+        inner = jnp.mean(pulled * unit, axis=-1, keepdims=True)
+        blend = pulled - jnp.mean(pulled, axis=-1, keepdims=True) - unit * inner
+        blend = blend * rstd_ref[rows, :][:, :1]
+        dh_ref[rows, :] = (blend * hslope_ref[rows, :].astype(f32)).astype(low)
+        du_ref[rows, :] = (blend * uslope_ref[rows, :].astype(f32)).astype(low)
+        direct_ref[rows, :] = (blend * kept_ref[rows, :].astype(f32)).astype(low)
+
+
+def back_ffn(place, lengths, side, grad, hidden_t, fslope, normed_t, unit, rstd, vec, where, hslope, uslope, kept, w_down, w_up):
+    width, ff = w_up.shape
+    count = fslope.shape[0]
+    narrow = (count, width)
+    outs = [((ff, width // 2), low)] * 2 + [((width, ff // 2), low)] * 2 + [(narrow, low)] * 3
+    outs += [((1, 3 * width + ff), f32)]
+    scratch = [pltpu.VMEM(w_down.shape, low), pltpu.VMEM(w_up.shape, low), pltpu.VMEM(narrow, low)]
+    scratch += [pltpu.VMEM((count, ff), low), pltpu.VMEM(narrow, f32), pltpu.SemaphoreType.DMA((2,))]
+    return call(
+        functools.partial(back_ffn_kernel, where["gain"]),
+        outs,
+        (place, lengths, side, w_down, w_up, grad, hidden_t, fslope, normed_t, unit, rstd, vec, hslope, uslope, kept),
+        smem=3,
+        hbm=2,
+        scratch=scratch,
+        flops=8 * count * width * ff,
+        moved=8 * width * ff + 20 * count * width,
+    )
+
+
+def back_attend_kernel(
+    side_ref, wout_hbm, wmix_hbm, wvalue_hbm,
+    dh_ref, du_ref, direct_ref, gated_t_ref, reset_ref, turned_ref, values_ref, vslope_ref, probs_ref,
+    query_ref, key_ref, shared_ref, qslope_ref, qscale_ref,
+    out_keep_ref, out_send_ref, dmix_ref, dvalue_ref, mixed_ref, resid_ref,
+    small_ref,
+    wout_ref, wmix_ref, wvalue_ref, datt_ref, sems,
+):
+    vwidth, width = wout_ref.shape
+    zwidth = qscale_ref.shape[1]
+    count = dh_ref.shape[0]
+    seqs = count // GROUP
+    copies = fetch([(wout_hbm, wout_ref), (wmix_hbm, wmix_ref), (wvalue_hbm, wvalue_ref)], sems)
+    dmix_ref[:, pl.ds(0, width)] = du_ref[...]
+    dmix_ref[:, pl.ds(width + zwidth + vwidth, width)] = dh_ref[...]
+    small_ref[:, pl.ds(0, width)] = column_sum(dh_ref[...])
+    copies[0].wait()
+
+    def gate(at):
+        part = pl.ds(at, CHUNK)
+        pulled = nt(dh_ref[...], wout_ref[part, :])
+        dmix_ref[:, pl.ds(pl.multiple_of(width + zwidth + at, 128), CHUNK)] = (
+            pulled * turned_ref[:, part].astype(f32)
+        ).astype(low)
+        datt_ref[:, part] = (pulled * reset_ref[:, part].astype(f32)).astype(low)
+
+    each(vwidth, gate)
+    scale = zwidth**-0.5
+    q_scale, k_scale = qscale_ref[pl.ds(0, 1), :], qscale_ref[pl.ds(1, 1), :]
+    zero = jnp.zeros((1, zwidth), f32)
+    sums = [zero, zero, zero, zero]
+    for n in range(seqs):
+        rows = pl.ds(n * GROUP, GROUP)
+        probs = probs_ref[rows, :]
+        pulled = nt(datt_ref[rows, :], values_ref[rows, :])
+        pulled = probs * (pulled - jnp.sum(pulled * probs, axis=-1, keepdims=True))
+        pulled = pulled.astype(low)
+        d_query = nn(pulled, key_ref[rows, :]) * scale
+        d_key = nn(pulled.T, query_ref[rows, :]) * scale
+        probs_t = probs.astype(low).T
+        shared = shared_ref[rows, :]
+        found = (d_query * shared, d_key * shared, d_query, d_key)
+        sums = [a + jnp.sum(b, axis=0, keepdims=True) for a, b in zip(sums, found)]
+        dmix_ref[rows, pl.ds(width, zwidth)] = (
+            (d_query * q_scale + d_key * k_scale) * qslope_ref[rows, :]
+        ).astype(low)
+        dvalue_ref[rows, :] = (nn(probs_t, datt_ref[rows, :]) * vslope_ref[rows, :].astype(f32)).astype(low)
+    mwidth = dmix_ref.shape[1]
+    for k in range(4):
+        small_ref[:, pl.ds(width + mwidth + vwidth + k * zwidth, zwidth)] = sums[k]
+    copies[1].wait()
+
+    def turn(result, ref, n):
+        ref[:, n] = result.astype(low).T.reshape(ref.shape[0], ref.shape[2], GROUP)
+
+    for n in range(0, seqs, 2):
+        result = nt(dmix_ref[pl.ds(n * GROUP, 2 * GROUP), :], wmix_ref[...])
+        turn(result[:GROUP], mixed_ref, n)
+        turn(result[GROUP:], mixed_ref, n + 1)
+    copies[2].wait()
+    for n in range(0, seqs, 2):
+        rows = pl.ds(n * GROUP, 2 * GROUP)
+        result = direct_ref[rows, :].astype(f32) + nt(dvalue_ref[rows, :], wvalue_ref[...])
+        turn(result[:GROUP], resid_ref, n)
+        turn(result[GROUP:], resid_ref, n + 1)
+    split_narrow(side_ref[0], out_keep_ref, out_send_ref, gated_t_ref, dh_ref)
+    small_ref[:, pl.ds(width, mwidth)] = column_sum(dmix_ref[...])
+    small_ref[:, pl.ds(width + mwidth, vwidth)] = column_sum(dvalue_ref[...])
+
+
+def back_attend(side, folded, dh, du, direct, gated_t, reset, turned, values, vslope, probs, query, key, shared, qslope, qk_scale, w_out, w_mix, w_value):
+    vwidth, width = w_out.shape
+    mwidth = w_mix.shape[1]
+    count = dh.shape[0]
+    outs = [((vwidth, width // 2), low)] * 2 + [((count, mwidth), low), ((count, vwidth), low)]
+    outs += [(folded, low)] * 2 + [((1, width + mwidth + vwidth + 2 * qk_scale.size), f32)]
+    scratch = [pltpu.VMEM(w.shape, low) for w in (w_out, w_mix, w_value)]
+    scratch += [pltpu.VMEM((count, vwidth), low), pltpu.SemaphoreType.DMA((3,))]
+    macs = 2 * w_out.size + w_mix.size + w_value.size
+    return call(
+        back_attend_kernel,
+        outs,
+        (side, w_out, w_mix, w_value, dh, du, direct, gated_t, reset, turned, values, vslope, probs, query, key, shared, qslope, qk_scale),
+        smem=1,
+        hbm=3,
+        scratch=scratch,
+        flops=2 * count * macs,
+        moved=2 * macs + 20 * count * width,
+    )
+
+
+def back_weights_kernel(
+    side_ref, mixed_ref, x_ref, dmix_ref, dvalue_ref, mix_keep_ref, mix_send_ref, value_keep_ref, value_send_ref, side_t_ref
+):
+    seqs = mixed_ref.shape[1]
+    for n in range(seqs):
+        side_t_ref[:, pl.ds(n * GROUP, GROUP)] = wide_block(mixed_ref, n)
+    split_product(side_ref[0], mix_keep_ref, mix_send_ref, side_t_ref[...], dmix_ref)
+    for n in range(seqs):
+        side_t_ref[:, pl.ds(n * GROUP, GROUP)] = wide_block(x_ref, n)
+    split_product(side_ref[0], value_keep_ref, value_send_ref, side_t_ref[...], dvalue_ref)
+
+
+def back_weights(side, mixed, x, dmix, dvalue):
+    count, mwidth = dmix.shape
+    vwidth = dvalue.shape[1]
+    width = x.shape[0] * x.shape[2]
+    half = -(-mwidth // 256) * 128
+    return call(
+        back_weights_kernel,
+        [((width, half), low)] * 2 + [((width, vwidth // 2), low)] * 2,
+        (side, mixed, x, dmix, dvalue),
+        smem=1,
+        scratch=[pltpu.VMEM((width, count), low)],
+        flops=2 * count * width * (mwidth + vwidth),
+        moved=2 * width * (mwidth + vwidth),
+    )
+
+
+Y_FIRST = (("tok", 1), ("ch", 0))
+X_FIRST = (("ch", 0), ("tok", 1))
 
 
 def bits_of(axis):
@@ -378,40 +817,79 @@
     return lax.ppermute(part, axis, [(i, i ^ (1 << bit)) for i in range(size)])
 
 
-def reduce_rows(grad, order):
-    parts, rows, columns = grad.shape
-    ch_bits, tok_bits = bits_of("ch"), bits_of("tok")
-    own = rows >> (ch_bits + tok_bits)
-    names = [("ch", k) for k in reversed(range(ch_bits))] + [("tok", k) for k in reversed(range(tok_bits))]
-    stages = [("tok", 0)] + list(order)
-    stages += [name for name in reversed(names) if name not in stages]
-    kept = grad.reshape((parts,) + (2,) * len(names) + (own, columns))
-    arrived = None
+def side_of(axis, bit):
+    return (lax.axis_index(axis) >> bit) & 1
+
+
+def add(left, right):
+    return (left.astype(f32) + right.astype(f32)).astype(low)
+
+
+def by_owner(grad):
+    dims = (2,) * (bits_of("ch") + bits_of("tok") - 1)
+    return grad.reshape(dims + (-1, grad.shape[-1]))
+
+
+def fold(part, columns):
+    runs = [part[..., at : at + columns] for at in range(0, part.shape[-1], columns)]
+    return jnp.concatenate(runs, axis=-2)
+
+
+def reduce_rows(kept, sent, merge, order):
+    arrived = [exchange(part, "tok", 0) for part in sent]
+    names = [("ch", k) for k in reversed(range(bits_of("ch")))]
+    names += [("tok", k) for k in reversed(range(1, bits_of("tok")))]
+    stages = list(order) + [name for name in reversed(names) if name not in order]
+    kept, arrived = [by_owner(part) for part in kept], [by_owner(part) for part in arrived]
     for axis, bit in stages:
-        at = 1 + names.index((axis, bit))
-        mine = (lax.axis_index(axis) >> bit) & 1
+        at = names.index((axis, bit))
+        mine = side_of(axis, bit)
 
         def pick(which):
-            half = lax.dynamic_index_in_dim(kept, which, at, keepdims=False)
-            if arrived is None:
-                return half
-            other = lax.dynamic_index_in_dim(arrived, which, at, keepdims=False)
-            return (half.astype(jnp.float32) + other.astype(jnp.float32)).astype(jnp.bfloat16)
-
-        sent, kept = pick(1 - mine), pick(mine)
+            def one(part):
+                return lax.dynamic_index_in_dim(part, which, at, keepdims=False)
+
+            parts = [add(one(a), one(b)) for a, b in zip(kept, arrived)]
+            return merge(parts) if len(parts) > 1 else parts[0]
+
+        sent, kept = pick(1 - mine), [pick(mine)]
         names.remove((axis, bit))
-        arrived = exchange(sent, axis, bit)
-    total = (kept.astype(jnp.float32) + arrived.astype(jnp.float32)).astype(jnp.bfloat16)
-    whole = lax.all_gather(total, "tok", axis=1)
-    return whole.reshape(parts, -1, columns).astype(jnp.float32)
-
-
-def reduce_pair(wide, tall, order):
-    rows, columns = tall.shape
-    low = jnp.bfloat16
-    merged = jnp.stack([wide.astype(low).reshape(rows, columns), tall.astype(low)])
-    merged = reduce_rows(merged, order)
-    return merged[0].reshape(-1, wide.shape[1]), merged[1]
+        arrived = [exchange(sent, axis, bit)]
+    return add(kept[0], arrived[0])
+
+
+def gather_tok(part):
+    whole = part[None]
+    for bit in reversed(range(bits_of("tok"))):
+        other = exchange(whole, "tok", bit)
+        mine = side_of("tok", bit)
+        near, far = jnp.where(mine == 0, whole, other), jnp.where(mine == 0, other, whole)
+        whole = jnp.stack([near, far], axis=1).reshape((-1,) + part.shape)
+    return whole
+
+
+def sum_tok(part):
+    for bit in range(bits_of("tok")):
+        part = part + exchange(part, "tok", bit)
+    return part
+
+
+def swap(parts):
+    return lax.all_to_all(parts, "ch", split_axis=0, concat_axis=0, tiled=True)
+
+
+def folded(parts):
+    devices, count, channels, span = parts.shape
+    if channels % 16 == 0:
+        return parts
+    return parts.transpose(1, 0, 2, 3).reshape(1, count, devices * channels, span)
+
+
+def unfolded(parts, devices):
+    if parts.shape[0] == devices:
+        return parts
+    _, count, channels, span = parts.shape
+    return parts.reshape(count, devices, channels // devices, span).transpose(1, 0, 2, 3)
 
 
 def local(
@@ -438,238 +916,147 @@
     w_down,
     b_down,
 ):
-    nseq_count, channels, local_len = inputs.shape
-    width = w_mix.shape[0]
-    zwidth = qk_scale.shape[1]
-    vwidth = w_value.shape[1]
-    scale = zwidth ** (-0.5)
-    tok_index = lax.axis_index("tok")
+    count, channels, local_len = inputs.shape
+    width, mwidth = w_mix.shape
+    vwidth, ff = w_value.shape[1], w_up.shape[1]
     devices = lax.axis_size("ch")
-    columns = nseq_count * channels
+    columns = count * channels
     span = local_len // devices
-    place = tok_index.astype(jnp.int32)[None]
+    tok_index = lax.axis_index("tok").astype(jnp.int32)
+    first = (tok_index * local_len + lax.axis_index("ch").astype(jnp.int32) * span)[None]
+    side = (tok_index & 1)[None]
+    place = tok_index[None]
 
     def by_block(part):
-        return part.reshape(nseq_count, channels, devices, span).transpose(2, 0, 1, 3)
-
-    recv_in = swap(by_block(inputs))
-    params = ema_params(ema_alpha, ema_delta, ema_beta, ema_eta, nseq_count)
-    omega = pad_to_lanes(jnp.tile(ema_omega, nseq_count)[None], 1)
+        return part.reshape(count, channels, devices, span).transpose(2, 0, 1, 3)
+
+    def by_column(parts):
+        return pad_to_lanes(unfolded(parts, devices).reshape(devices, columns, span), 1)
+
+    recv_in = folded(swap(by_block(inputs)))
+    params = ema_params(ema_alpha, ema_delta, ema_beta, ema_eta, count)
+    omega = pad_to_lanes(jnp.tile(ema_omega, count)[None], 1)
     xs, ends, total = ema_ends(pad_to_lanes(inputs.reshape(columns, local_len), 0), params)
     totals = lax.all_gather(total, "tok")
     mixed, slope, entry = ema_mix(place, xs, ends, params, omega, totals)
-    recv_mix = swap(mixed[:, :columns].reshape(devices, nseq_count, channels, span))
-    tok_in = to_rows(recv_in)
-    tok_mix = to_rows(recv_mix)
-    row_count = tok_in.shape[0]
-    blocks_n = row_count // GROUP
-    value_pre = jnp.dot(tok_in, w_value, preferred_element_type=jnp.float32) + b_value
-    values = jax.nn.silu(value_pre).astype(jnp.bfloat16)
-    mix_pre = jnp.dot(tok_mix, w_mix, preferred_element_type=jnp.float32) + b_mix
-    gate_pre = mix_pre[:, :width]
-    query_pre = mix_pre[:, width : width + zwidth]
-    reset_pre = mix_pre[:, width + zwidth : width + zwidth + vwidth]
-    hidden_mix = mix_pre[:, width + zwidth + vwidth :]
-    update = jax.nn.sigmoid(gate_pre)
-    shared = jax.nn.silu(query_pre)
-    queries = (shared * qk_scale[0] + qk_shift[0]).astype(jnp.bfloat16)
-    keys_all = (shared * qk_scale[1] + qk_shift[1]).astype(jnp.bfloat16)
-    reset = jax.nn.silu(reset_pre)
-    query_blk = queries.reshape(blocks_n, GROUP, zwidth)
-    key_blk = keys_all.reshape(blocks_n, GROUP, zwidth)
-    value_blk = values.reshape(blocks_n, GROUP, vwidth)
-    position = jnp.arange(GROUP)
-    causal = position[:, None] >= position[None, :]
-
-    def block_scores():
-        raw = (
-            jnp.einsum("cqz,ckz->cqk", query_blk, key_blk, preferred_element_type=jnp.float32)
-            * scale
-        )
-        return jnp.where(causal[None], raw, -1e30)
-
-    scores = block_scores()
-    top_score = jnp.max(scores, axis=-1, keepdims=True)
-    log_norm = top_score + jnp.log(jnp.sum(jnp.exp(scores - top_score), axis=-1, keepdims=True))
-    probs_bf = jnp.exp(scores - log_norm).astype(jnp.bfloat16)
-    attended = jnp.einsum(
-        "cqk,ckv->cqv", probs_bf, value_blk, preferred_element_type=jnp.float32
-    ).reshape(row_count, vwidth)
-    gated = (reset * attended).astype(jnp.bfloat16)
-    hidden_pre = hidden_mix + jnp.dot(gated, w_out, preferred_element_type=jnp.float32) + b_out
-    hidden = jax.nn.silu(hidden_pre)
-    resid = tok_in.astype(jnp.float32)
-    blend = update * hidden + (1.0 - update) * resid
-    centered = blend - jnp.mean(blend, axis=-1, keepdims=True)
-    rstd = lax.rsqrt(jnp.mean(centered * centered, axis=-1, keepdims=True) + 1e-05)
-    unit = centered * rstd
-    normed = unit * ln_gain + ln_bias
-    normed_bf = normed.astype(jnp.bfloat16)
-    ffn_pre = jnp.dot(normed_bf, w_up, preferred_element_type=jnp.float32) + b_up
-    ffn_hidden = jax.nn.silu(ffn_pre).astype(jnp.bfloat16)
-    result = normed + jnp.dot(ffn_hidden, w_down, preferred_element_type=jnp.float32) + b_down
-    out_local = swap(from_rows(result.astype(jnp.bfloat16), nseq_count, devices))
-    seq_pos = tok_index * local_len + jnp.arange(local_len, dtype=jnp.int32)
-    live = (seq_pos[None, :] < seq_lengths[:, None])[:, None, :]
-    out_local = out_local.transpose(1, 2, 0, 3).reshape(inputs.shape)
-    output = jnp.where(live, out_local, jnp.zeros_like(out_local))
-    grad_rows = to_rows(swap(by_block(jnp.where(live, out_grad, jnp.zeros_like(out_grad)))))
-    grad_f = grad_rows.astype(jnp.float32)
-    g_down = jnp.dot(ffn_hidden.T, grad_rows, preferred_element_type=jnp.float32)
-    g_bdown = jnp.sum(grad_f, axis=0)
-    d_ffn = (
-        jnp.dot(grad_rows, w_down.T, preferred_element_type=jnp.float32) * silu_slope(ffn_pre)
-    ).astype(jnp.bfloat16)
-    g_up = jnp.dot(normed_bf.T, d_ffn, preferred_element_type=jnp.float32)
-    g_bup = jnp.sum(d_ffn.astype(jnp.float32), axis=0)
-    d_normed = grad_f + jnp.dot(d_ffn, w_up.T, preferred_element_type=jnp.float32)
-    g_gain = jnp.sum(d_normed * unit, axis=0)
-    g_lnbias = jnp.sum(d_normed, axis=0)
-    d_unit = d_normed * ln_gain
-    d_blend = rstd * (
-        d_unit
-        - jnp.mean(d_unit, axis=-1, keepdims=True)
-        - unit * jnp.mean(d_unit * unit, axis=-1, keepdims=True)
-    )
-    d_hidden_pre = (d_blend * update * silu_slope(hidden_pre)).astype(jnp.bfloat16)
-    d_update_pre = d_blend * (hidden - resid) * update * (1.0 - update)
-    d_direct = d_blend * (1.0 - update)
-    g_out = jnp.dot(gated.T, d_hidden_pre, preferred_element_type=jnp.float32)
-    g_bout = jnp.sum(d_hidden_pre.astype(jnp.float32), axis=0)
-    d_gated = jnp.dot(d_hidden_pre, w_out.T, preferred_element_type=jnp.float32)
-    d_reset_pre = d_gated * attended * silu_slope(reset_pre)
-    d_attended = (d_gated * reset).astype(jnp.bfloat16).reshape(blocks_n, GROUP, vwidth)
-    scores = block_scores()
-    probs = jnp.exp(scores - log_norm)
-    probs_bf = probs.astype(jnp.bfloat16)
-    d_probs = jnp.einsum("cqv,ckv->cqk", d_attended, value_blk, preferred_element_type=jnp.float32)
-    d_values = jnp.einsum(
-        "cqk,cqv->ckv", probs_bf, d_attended, preferred_element_type=jnp.float32
-    ).reshape(row_count, vwidth)
-    d_scores = (probs * (d_probs - jnp.sum(d_probs * probs, axis=-1, keepdims=True))).astype(
-        jnp.bfloat16
-    )
-    d_query = (
-        jnp.einsum("cqk,ckz->cqz", d_scores, key_blk, preferred_element_type=jnp.float32).reshape(
-            row_count, zwidth
-        )
-        * scale
-    )
-    d_key = (
-        jnp.einsum("cqk,cqz->ckz", d_scores, query_blk, preferred_element_type=jnp.float32).reshape(
-            row_count, zwidth
-        )
-        * scale
-    )
-    d_value_pre = (d_values * silu_slope(value_pre)).astype(jnp.bfloat16)
-    g_value = jnp.dot(tok_in.T, d_value_pre, preferred_element_type=jnp.float32)
-    g_bvalue = jnp.sum(d_value_pre.astype(jnp.float32), axis=0)
-    d_resid = d_direct + jnp.dot(d_value_pre, w_value.T, preferred_element_type=jnp.float32)
-    g_qscale = jnp.stack([jnp.sum(d_query * shared, axis=0), jnp.sum(d_key * shared, axis=0)])
-    g_qshift = jnp.stack([jnp.sum(d_query, axis=0), jnp.sum(d_key, axis=0)])
-    d_query_pre = (d_query * qk_scale[0] + d_key * qk_scale[1]) * silu_slope(query_pre)
-    d_mix_pre = jnp.concatenate(
-        [d_update_pre, d_query_pre, d_reset_pre, d_hidden_pre.astype(jnp.float32)], axis=1
-    ).astype(jnp.bfloat16)
-    g_mix = jnp.dot(tok_mix.T, d_mix_pre, preferred_element_type=jnp.float32)
-    g_bmix = jnp.sum(d_mix_pre.astype(jnp.float32), axis=0)
-    d_mix_in = jnp.dot(d_mix_pre, w_mix.T, preferred_element_type=jnp.float32)
-    back_mix = swap(from_rows(d_mix_in.astype(jnp.bfloat16), nseq_count, devices))
-    back_resid = swap(from_rows(d_resid.astype(jnp.bfloat16), nseq_count, devices))
-    back_mix = pad_to_lanes(back_mix.reshape(devices, columns, span), 1)
-    back_resid = pad_to_lanes(back_resid.reshape(devices, columns, span), 1)
-    pull, heads, total = ema_back(back_mix, slope, params)
+    recv_mix = folded(swap(mixed[:, :columns].reshape(devices, count, channels, span)))
+    recv_grad = folded(swap(by_block(out_grad)))
+
+    where = vectors(width, mwidth, vwidth, ff)
+    vec = jnp.concatenate([b_mix, b_value, b_out, ln_gain, ln_bias, b_up, b_down])[None]
+    x, values, vslope = value_part(recv_in, w_value, vec, where)
+    (
+        result, query, key, shared, qslope, probs, reset, turned, gated_t,
+        hslope, uslope, keep, unit, rstd, normed_t, hidden_t, fslope,
+    ) = forward_part(
+        first, seq_lengths, recv_mix, x, values, w_mix, w_out, w_up, w_down, vec, where, qk_scale, qk_shift
+    )
+    output = swap(unfolded(result, devices)).transpose(1, 2, 0, 3).reshape(inputs.shape)
+    down_kept, down_sent, up_kept, up_sent, dh, du, direct, small_ffn = back_ffn(
+        first, seq_lengths, side, recv_grad, hidden_t, fslope, normed_t, unit, rstd, vec, where,
+        hslope, uslope, keep, w_down, w_up,
+    )
+    out_kept, out_sent, dmix, dvalue, back_mix, back_resid, small_attend = back_attend(
+        side, recv_mix.shape, dh, du, direct, gated_t, reset, turned, values, vslope, probs,
+        query, key, shared, qslope, qk_scale, w_out, w_mix, w_value,
+    )
+    back_mix = swap(unfolded(back_mix, devices))
+    back_resid = swap(unfolded(back_resid, devices))
+    mix_kept, mix_sent, value_kept, value_sent = back_weights(side, recv_mix, recv_in, dmix, dvalue)
+
+    small = jnp.concatenate([small_ffn[0], small_attend[0]]).astype(low)
+    half = mix_kept.shape[1]
+    tok_size = lax.axis_size("tok")
+    lines = -(-small.size // (tok_size * half))
+    small_size = small.size
+    small = jnp.pad(small, (0, tok_size * lines * half - small_size))
+    small = small.reshape(tok_size // 2, 2, lines, half)
+
+    def pair(parts):
+        tall, wide = parts
+        return jnp.concatenate([tall, fold(wide, tall.shape[-1])], axis=-2)
+
+    def with_small(parts):
+        return jnp.concatenate(parts, axis=-2)
+
+    def spread_small(which):
+        part = lax.dynamic_index_in_dim(small, which, 1, keepdims=False)
+        return jnp.broadcast_to(part[None], (devices,) + part.shape).reshape(-1, half)
+
+    owned_ffn = reduce_rows([down_kept, up_kept], [down_sent, up_sent], pair, Y_FIRST)
+    owned_mid = reduce_rows([out_kept, value_kept], [out_sent, value_sent], pair, X_FIRST)
+    owned_mix = reduce_rows(
+        [mix_kept, spread_small(side[0])], [mix_sent, spread_small(1 - side[0])], with_small, Y_FIRST
+    )
+
+    pull, heads, total = ema_back(by_column(back_mix), slope, params)
     totals = lax.all_gather(total, "tok")
     sums, tails = ema_sums(xs, pull, entry, params)
-    input_grad, sums = ema_finish(place, pull, heads, params, omega, totals, sums, tails, back_resid)
+    input_grad, sums = ema_finish(
+        place, pull, heads, params, omega, totals, sums, tails, by_column(back_resid)
+    )
     input_grad = input_grad[:columns].reshape(inputs.shape)
-    g_up_s, g_down_s = reduce_pair(g_up, g_down, ORDER_A)
-    g_value_s, g_out_s = reduce_pair(g_value, g_out, ORDER_B)
-    g_mix_s = reduce_rows(g_mix.astype(jnp.bfloat16)[None], ORDER_A)[0]
-    ema_grads = ema_param_grads(
-        lax.psum(sums, "tok"), ema_alpha, ema_delta, ema_beta, ema_eta, nseq_count
-    )
-    summed = (g_mix_s, g_value_s, g_out_s, g_up_s, g_down_s) + ema_grads
-    smalls = lax.psum(
-        (g_bmix, g_bvalue, g_bout, g_qscale, g_qshift, g_gain, g_lnbias, g_bup, g_bdown),
-        ("ch", "tok"),
-    )
+    ema_grads = ema_param_grads(sum_tok(sums), ema_alpha, ema_delta, ema_beta, ema_eta, count)
+
+    def unpair(owned, tall_rows):
+        whole = gather_tok(owned).astype(f32)
+        cut = tall_rows // devices // (tok_size // 2)
+        whole = whole.reshape((tok_size // 2, 2) + whole.shape[1:])
+        tall, wide = whole[:, :, :cut], whole[:, :, cut:]
+        tall = tall.transpose(0, 2, 1, 3).reshape(tall_rows // devices, -1)
+        lone = width // devices // (tok_size // 2)
+        wide = wide.reshape(tok_size // 2, 2, -1, lone, wide.shape[-1])
+        wide = wide.transpose(0, 3, 1, 2, 4).reshape(width // devices, -1)
+        return tall, wide
+
+    g_down, g_up = unpair(owned_ffn, ff)
+    g_out, g_value = unpair(owned_mid, vwidth)
+    whole = gather_tok(owned_mix).astype(f32)
+    small = whole[:, -lines:].reshape(-1)[:small_size]
+    whole = whole[:, :-lines].reshape(tok_size // 2, 2, -1, half)
+    g_mix = jnp.concatenate([whole[:, 0], whole[:, 1, :, 2 * half - mwidth :]], axis=-1)
+    g_mix = g_mix.reshape(width // devices, mwidth)
+    sizes = (width, ff, width, width, width, mwidth, vwidth, qk_scale.size, qk_scale.size)
+    found, at = [], 0
+    for size in sizes:
+        found.append(small[at : at + size])
+        at += size
+    g_bdown, g_bup, g_gain, g_lnbias, g_bout, g_bmix, g_bvalue, g_qscale, g_qshift = found
+    g_qscale, g_qshift = g_qscale.reshape(qk_scale.shape), g_qshift.reshape(qk_scale.shape)
     return (
         output,
         input_grad,
-        summed[5],
-        summed[6],
-        summed[7],
-        summed[8],
-        summed[9],
-        summed[0],
-        smalls[0],
-        summed[1],
-        smalls[1],
-        summed[2],
-        smalls[2],
-        smalls[3],
-        smalls[4],
-        smalls[5],
-        smalls[6],
-        summed[3],
-        smalls[7],
-        summed[4],
-        smalls[8],
+        *ema_grads,
+        g_mix,
+        g_bmix,
+        g_value,
+        g_bvalue,
+        g_out,
+        g_bout,
+        g_qscale,
+        g_qshift,
+        g_gain,
+        g_lnbias,
+        g_up,
+        g_bup,
+        g_down,
+        g_bdown,
     )
 
 
 def solution(mesh):
-    placed = (
-        P(None, "ch", "tok"),
-        P(None, "ch", "tok"),
-        P(),
-        P("ch", None),
-        P("ch", None),
-        P("ch", None),
-        P("ch", None),
-        P("ch"),
-        P(),
-        P(),
-        P(),
-        P(),
-        P(),
-        P(),
-        P(),
-        P(),
-        P(),
-        P(),
-        P(),
-        P(),
-        P(),
-        P(),
-    )
+    by_ch = P("ch", None)
+    placed = P(None, "ch", "tok")
     return jax.shard_map(
         local,
         mesh=mesh,
-        in_specs=placed,
+        in_specs=(placed, placed, P()) + (by_ch,) * 4 + (P("ch"),) + (P(),) * 14,
         out_specs=(
-            P(None, "ch", "tok"),
-            P(None, "ch", "tok"),
-            P("ch", None),
-            P("ch", None),
-            P("ch", None),
-            P("ch", None),
-            P("ch"),
-            P("ch", None),
-            P(),
-            P("ch", None),
-            P(),
-            P("ch", None),
-            P(),
-            P(),
-            P(),
-            P(),
-            P(),
-            P("ch", None),
-            P(),
-            P("ch", None),
-            P(),
+            (placed, placed)
+            + (by_ch,) * 4
+            + (P("ch"), by_ch, P(), by_ch, P(), by_ch)
+            + (P(),) * 5
+            + (by_ch, P(), by_ch, P())
         ),
         check_vma=False,
     )

time: 477 us -> 392 us (0.82)
  blocking collectives: 122 us -> 14 us
  Pallas kernels: 37.9 us -> 120 us
  matrix products: 64.4 us -> 0 us
  waiting for transfers between devices: 85.6 us -> 133 us
  other arithmetic: 54.7 us -> 29.7 us
  local copies, waits for them, and re-layouts: 63.6 us -> 41.6 us
    psum x2 -> x0, blocking collectives: 86.6 us -> none  [the longest x1 72.8 us: local(): lax.psum((g_bmix, g_bvalue, g_bout, g_qscale, g_qshift, g_gain, g_lnbias,...]
    pallas_call x0 -> x5, Pallas kernels: none -> 73.4 us  [call(): pl.pallas_call(kernel, out_shape=tuple((jax.ShapeDtypeStruct(shape, kind)...]
    dot_general x21 -> x0, matrix products: 64.4 us -> none  [the longest x1 6.58 us: local(): jnp.dot(grad_rows, w_down.T, preferred_element_type=jnp.float32)]
    ppermute x15 -> x26, waiting for transfers between devices: 30.5 us -> 75.5 us  [exchange(): return lax.ppermute(part, axis, [(i, i ^ 1 << bit) for i in range(size)])]
    all_gather x3 -> x0, blocking collectives: 22.6 us -> none  [reduce_rows(): whole = lax.all_gather(total, 'tok', axis=1)]
    reduce_sum x9 -> x0, other arithmetic: 15.7 us -> none  [the longest x1 4.99 us: local(): g_bout = jnp.sum(d_hidden_pre.astype(jnp.float32), axis=0)]
    dynamic_slice x1 -> x8, local copies, waits for them, and re-layouts: 3.33 us -> 15.1 us  [one(): return lax.dynamic_index_in_dim(part, which, at, keepdims=False)]
    concatenate x0 -> x7, other arithmetic: none -> 8.84 us  [the longest x4 6 us: pair(): return jnp.concatenate([tall, fold(wide, tall.shape[-1])], axis=-2)]
  transfers between devices with their start and end apart: 21 -> 32, of which waited for: 9 -> 15; matrix products, arithmetic and copies ran while one was open for 17% -> 14% of each run, Pallas kernels for 8% -> 24%
where the time goes in v3:
time: 392 us; the launch traced here: 386 us
  waiting for transfers between devices  133 us (34%)
  Pallas kernels  120 us (31%)
  starting transfers between devices  46.1 us (12%)
  local copies, waits for them, and re-layouts  41.6 us (11%)
  other arithmetic  29.7 us (8%)
  blocking collectives  14 us (4%)
    ppermute x26, waiting for transfers between devices, exchange(): return lax.ppermute(part, axis, [(i, i ^ 1 << bit) for i in range(size)])  75.5 us
    pallas_call x5, Pallas kernels, call(): pl.pallas_call(kernel, out_shape=tuple((jax.ShapeDtypeStruct(shape, kind)...  73.4 us
    all_to_all x6, waiting for transfers between devices, swap(): return lax.all_to_all(parts, 'ch', split_axis=0, concat_axis=0, tiled=True)  57.7 us
    all_to_all x6, starting transfers between devices, swap(): return lax.all_to_all(parts, 'ch', split_axis=0, concat_axis=0, tiled=True)  26.9 us
    ppermute x26, starting transfers between devices, exchange(): return lax.ppermute(part, axis, [(i, i ^ 1 << bit) for i in range(size)])  19.2 us
    convert_element_type x21, other arithmetic, add(): return (left.astype(f32) + right.astype(f32)).astype(low)  16.9 us
    pallas_call x1, Pallas kernels, ema_finish(): pl.pallas_call(ema_finish_kernel, grid=(columns // LANES,), out_shape=(ja...  16.6 us
    dynamic_slice x8, local copies, waits for them, and re-layouts, one(): return lax.dynamic_index_in_dim(part, which, at, keepdims=False)  15.1 us
  transfers between devices with their start and end apart: 32, of which 15 were waited for; matrix products, arithmetic and copies ran while one was open for 14% of the time, Pallas kernels for 24%

profile of v3, /device:TPU:0, one launch (start us, length us, event | category | flops | bytes accessed | tf_op | source)
XLA Modules:
  0.0 386.3 jit_solution(13685632459892886494)
XLA Ops:
  2.3 4.9 %shard_map.373 = (f32[1024,384]{1,0:T(8,128)}, f32[128,384]{1,0:T(8,128)}, f32[16,384]{1,0:T(8,128)}) custom-call(bf16[384,1024]{1,0:T(8,128)(2,1)} %bitcast.251, f32[4,16,384]{2,1,0:T(8,128)} %tile.7.params_ref), custom_call_target="tpu_custom_call" | custom-call | flops 12582912 | bytes 2359296 | tf_op jit(solution)/shard_map/pallas_call | solution.py:88
  7.2 8.2 %all-gather = f32[64,384]{1,0:T(8,128)} all-gather(f32[16,384]{1,0:T(8,128)} %get-tuple-element.75), channel_id=2, replica_groups=mesh['ch'=8,'tok'=4] {'tok'}, dimensions={0}, use_global_device_ids=true | all-gather | bytes 122880 | tf_op jit(solution)/shard_map/all_gather | solution.py:940
  16.1 7.2 %shard_map.374 = (bf16[8,384,128]{2,1,0:T(8,128)(2,1)}, bf16[1024,384]{1,0:T(8,128)(2,1)}, f32[128,384]{1,0:T(8,128)}) custom-call(s32[1]{0:T(128)} %bitcast.1.place_ref, f32[1024,384]{1,0:T(8,128)} %get-tuple-element.73.xs_ref, f32[128,384]{1,0:T(8,128)} %get-tuple-element.74.ends_ref, f32[4,16,384]{2,1,0:T(8,128)} %tile.7.params_ref, ...), custom_call_target="tpu_custom_call" | custom-call | flops 25165824 | bytes 3932160 | tf_op jit(solution)/shard_map/pallas_call | solution.py:143
  23.3 5.9 %all-to-all-start = ((bf16[8,4,96,128]{3,2,1,0:T(8,128)(2,1)}), bf16[8,4,96,128]{3,2,1,0:T(8,128)(2,1)S(1)}, u32[]{:S(2)}, u32[]{:S(2)}) async-start(bf16[8,4,96,128]{3,2,1,0:T(8,128)(2,1)} %bitcast.267), calls=%async_computation | async-start | bytes 1572864 | tf_op jit(solution)/shard_map/all_to_all | solution.py:878
  30.2 19.6 %all-to-all-done.mixed_ref = bf16[8,4,96,128]{3,2,1,0:T(8,128)(2,1)S(1)} async-done(((bf16[8,4,96,128]{3,2,1,0:T(8,128)(2,1)}), bf16[8,4,96,128]{3,2,1,0:T(8,128)(2,1)S(1)}, u32[]{:S(2)}, u32[]{:S(2)}) %all-to-all-start) | async-done | bytes 786464 | tf_op jit(solution)/shard_map/all_to_all | solution.py:878
  49.9 3.6 all-to-all-start.1
  54.7 19.2 %all-to-all-done.1.x_ref = bf16[8,4,96,128]{3,2,1,0:T(8,128)(2,1)S(1)} async-done(((bf16[8,4,96,128]{3,2,1,0:T(8,128)(2,1)}), bf16[8,4,96,128]{3,2,1,0:T(8,128)(2,1)S(1)}, u32[]{:S(2)}, u32[]{:S(2)}) %all-to-all-start.1) | async-done | bytes 786464 | tf_op jit(solution)/shard_map/all_to_all | solution.py:878
  73.9 3.5 all-to-all-start.3
  78.3 7.0 %shard_map.375 = (bf16[512,768]{1,0:T(8,128)(2,1)}, bf16[512,1536]{1,0:T(8,128)(2,1)}, bf16[512,1536]{1,0:T(8,128)(2,1)}) custom-call(bf16[768,1536]{1,0:T(8,128)(2,1)} %wvalue_hbm.1, bf16[8,4,96,128]{3,2,1,0:T(8,128)(2,1)} %copy-done.18, f32[1,9344]{1,0:T(1,128)} %broadcast_in_dim.35.vec_ref), custom_call_target="tpu_custom_call" | custom-call | flops 1207959552 | bytes 6291456 | tf_op jit(solution)/shard_map/pallas_call | solution.py:397
  85.3 23.4 %shard_map.376 = (bf16[8,4,96,128]{3,2,1,0:T(8,128)(2,1)}, bf16[512,128]{1,0:T(8,128)(2,1)}, bf16[512,128]{1,0:T(8,128)(2,1)}, f32[512,128]{1,0:T(8,128)}, f32[5...) custom-call(s32[1]{0:T(128)} %bitcast.place_ref, ...), custom_call_target="tpu_custom_call" | custom-call | flops 6140461056 | bytes 23789568 | tf_op jit(solution)/shard_map/pallas_call | solution.py:397
  109.5 14.1 %shard_map.377 = (bf16[1536,384]{1,0:T(8,128)(2,1)}, bf16[1536,384]{1,0:T(8,128)(2,1)}, bf16[768,768]{1,0:T(8,128)(2,1)}, bf16[768,768]{1,0:T(8,128)(2,1)}, bf16...) custom-call(s32[1]{0:T(128)} %bitcast.place_ref, ...), custom_call_target="tpu_custom_call" | custom-call | flops 4831838208 | bytes 17301504 | tf_op jit(solution)/shard_map/pallas_call | solution.py:397
  124.2 20.6 %shard_map.378 = (bf16[1536,384]{1,0:T(8,128)(2,1)}, bf16[1536,384]{1,0:T(8,128)(2,1)}, bf16[512,3200]{1,0:T(8,128)(2,1)}, bf16[512,1536]{1,0:T(8,128)(2,1)}, bf...) custom-call(s32[1]{0:T(128)} %bitcast.12.side_ref, bf16[1536,768]{1,0:T(8,128)(2,1)} %wout_hbm.3, ...), custom_call_target="tpu_custom_call" | custom-call | flops 6140461056 | bytes 19857408 | tf_op jit(solution)/shard_map/pallas_call | solution.py:397
  144.8 8.3 %shard_map.382 = (bf16[768,1664]{1,0:T(8,128)(2,1)}, bf16[768,1664]{1,0:T(8,128)(2,1)}, bf16[768,768]{1,0:T(8,128)(2,1)}, bf16[768,768]{1,0:T(8,128)(2,1)}) custom-call(s32[1]{0:T(128)} %bitcast.12.side_ref, bf16[8,4,96,128]{3,2,1,0:T(8,128)(2,1)} %copy-done.17, bf16[8,4,96,128]{3,2,1,0:T(8,128)(2,1)} %copy-done.18, ...), custom_call_target="tpu_custom_call" | custom-call | flops 3724541952 | bytes 7274496 | tf_op jit(solution)/shard_map/pallas_call | solution.py:397
  154.1 6.0 %all-to-all-start.4 = ((bf16[8,4,96,128]{3,2,1,0:T(8,128)(2,1)}), bf16[8,4,96,128]{3,2,1,0:T(8,128)(2,1)S(1)}, u32[]{:S(2)}, u32[]{:S(2)}) async-start(bf16[8,4,96,128]{3,2,1,0:T(8,128)(2,1)} %get-tuple-element.100), calls=%async_computation.4 | async-start | bytes 1572864 | tf_op jit(solution)/shard_map/all_to_all | solution.py:878
  160.7 2.0 constant_dynamic-slice_fusion.17
  166.7 2.3 constant_dynamic-slice_fusion.1
  169.0 11.8 %all-to-all-done.4 = bf16[8,4,96,128]{3,2,1,0:T(8,128)(2,1)S(1)} async-done(((bf16[8,4,96,128]{3,2,1,0:T(8,128)(2,1)}), bf16[8,4,96,128]{3,2,1,0:T(8,128)(2,1)S(1)}, u32[]{:S(2)}, u32[]{:S(2)}) %all-to-all-start.4) | async-done | bytes 786464 | tf_op jit(solution)/shard_map/all_to_all | solution.py:878
  180.9 4.2 %all-to-all-start.5 = ((bf16[8,4,96,128]{3,2,1,0:T(8,128)(2,1)}), bf16[8,4,96,128]{3,2,1,0:T(8,128)(2,1)}, u32[]{:S(2)}, u32[]{:S(2)}) async-start(bf16[8,4,96,128]{3,2,1,0:T(8,128)(2,1)} %get-tuple-element.108), calls=%async_computation.5 | async-start | bytes 1572864 | tf_op jit(solution)/shard_map/all_to_all | solution.py:878
  185.1 2.8 fusion.13
  187.9 2.3 constant_dynamic-slice_fusion.3
  192.2 2.3 fusion.11
  196.1 2.0 fusion.10
  198.1 7.0 %all-to-all-done.5 = bf16[8,4,96,128]{3,2,1,0:T(8,128)(2,1)} async-done(((bf16[8,4,96,128]{3,2,1,0:T(8,128)(2,1)}), bf16[8,4,96,128]{3,2,1,0:T(8,128)(2,1)}, u32[]{:S(2)}, u32[]{:S(2)}) %all-to-all-start.5) | async-done | bytes 786464 | tf_op jit(solution)/shard_map/all_to_all | solution.py:878
  205.1 3.5 all-to-all-start.2
  208.7 2.5 pad_maximum_fusion.3
  211.2 1.9 collective-permute-start.12
  216.8 5.2 %shard_map.379 = (f32[1024,384]{1,0:T(8,128)}, f32[128,384]{1,0:T(8,128)}, f32[16,384]{1,0:T(8,128)}) custom-call(bf16[8,384,128]{2,1,0:T(8,128)(2,1)} %bitcast.252, bf16[1024,384]{1,0:T(8,128)(2,1)} %get-tuple-element.101.slope_ref, f32[4,16,384]{2,1,0:T(8,128)} %tile.7.params_ref), custom_call_target="tpu_custom_call" | custom-call | flops 12582912 | bytes 3145728 | tf_op jit(solution)/shard_map/pallas_call | solution.py:197
  222.0 12.6 %shard_map.380 = (f32[40,384]{1,0:T(8,128)}, f32[128,384]{1,0:T(8,128)}) custom-call(f32[1024,384]{1,0:T(8,128)} %get-tuple-element.73.xs_ref, f32[1024,384]{1,0:T(8,128)} %get-tuple-element.102.pull_ref, f32[128,384]{1,0:T(8,128)} %get-tuple-element.105.entry_ref, f32[4,16,384]{2,1,0:T(8,128)} %tile.7.params_ref), custom_call_target="tpu_custom_call" | custom-call | flops 50331648 | bytes 3145728 | tf_op jit(solution)/shard_map/pallas_call | solution.py:249
  234.6 5.8 %all-gather.1 = f32[64,384]{1,0:T(8,128)} all-gather(f32[16,384]{1,0:T(8,128)S(1)} %copy-done.25), channel_id=3, replica_groups=mesh['ch'=8,'tok'=4] {'tok'}, dimensions={0}, use_global_device_ids=true | all-gather | bytes 122880 | tf_op jit(solution)/shard_map/all_gather | solution.py:993
  240.4 16.6 %shard_map.381 = (f32[384,1024]{1,0:T(8,128)}, f32[40,384]{1,0:T(8,128)}) custom-call(s32[1]{0:T(128)} %bitcast.1.place_ref, f32[1024,384]{1,0:T(8,128)} %get-tuple-element.102.pull_ref, f32[128,384]{1,0:T(8,128)} %get-tuple-element.103.heads_ref, f32[4,16,384]{2,1,0:T(8,128)} %tile.7.params_ref, f32[1,384]{1,0:T(1,128)} %broadcast_in_dim_tile.3.omega_ref, ...), custom_call_target="tpu_custom_call" | custom-call | flops 25165824 | bytes 5505024 | tf_op jit(solution)/shard_map/pallas_call | solution.py:306
  260.4 2.6 collective-permute-done.1
  265.3 1.9 add_convert_fusion.5
  271.6 1.9 constant_dynamic-slice_fusion.16
  274.8 6.7 %collective-permute-done.21 = bf16[2,2,192,384]{3,2,1,0:T(8,128)(2,1)S(1)} collective-permute-done((bf16[2,2,192,384]{3,2,1,0:T(8,128)(2,1)S(1)}, bf16[2,2,192,384]{3,2,1,0:T(8,128)(2,1)S(1)}, u32[]{:S(2)}, u32[]{:S(2)}) %collective-permute-start.21) | collective-permute-done | bytes 589856 | tf_op jit(solution)/shard_map/ppermute | solution.py:817
  283.3 1.7 pad_maximum_fusion
  286.5 6.6 %collective-permute-done.22 = bf16[2,192,384]{2,1,0:T(8,128)(2,1)S(1)} collective-permute-done((bf16[2,192,384]{2,1,0:T(8,128)(2,1)S(1)}, bf16[2,192,384]{2,1,0:T(8,128)(2,1)S(1)}, u32[]{:S(2)}, u32[]{:S(2)}) %collective-permute-start.22) | collective-permute-done | bytes 294944 | tf_op jit(solution)/shard_map/ppermute | solution.py:817
  295.1 1.7 collective-permute-done.14
  296.8 2.7 collective-permute-start.15
  299.5 6.1 %collective-permute-done.23 = bf16[192,384]{1,0:T(8,128)(2,1)S(1)} collective-permute-done((bf16[192,384]{1,0:T(8,128)(2,1)S(1)}, bf16[192,384]{1,0:T(8,128)(2,1)S(1)}, u32[]{:S(2)}, u32[]{:S(2)}) %collective-permute-start.23) | collective-permute-done | bytes 147488 | tf_op jit(solution)/shard_map/ppermute | solution.py:817
  307.9 10.9 %collective-permute-done.24 = bf16[1,192,384]{2,1,0:T(8,128)(2,1)S(1)} collective-permute-done((bf16[1,192,384]{2,1,0:T(8,128)(2,1)S(1)}, bf16[1,192,384]{2,1,0:T(8,128)(2,1)S(1)}, u32[]{:S(2)}, u32[]{:S(2)}) %collective-permute-start.24) | collective-permute-done | bytes 147488 | tf_op jit(solution)/shard_map/ppermute | solution.py:817
  318.9 2.7 constant_dynamic-slice_fusion.14
  323.9 16.2 %collective-permute-done.5 = bf16[2,2,50,1664]{3,1,2,0:T(2,128)(2,1)S(1)} collective-permute-done((bf16[2,2,50,1664]{3,1,2,0:T(2,128)(2,1)S(1)}, bf16[2,2,50,1664]{3,1,2,0:T(2,128)(2,1)S(1)}, u32[]{:S(2)}, u32[]{:S(2)}) %collective-permute-start.5) | collective-permute-done | bytes 665632 | tf_op jit(solution)/shard_map/ppermute | solution.py:817
  340.0 1.6 constant_dynamic-slice_fusion.12
  342.4 9.6 %collective-permute-done.6 = bf16[2,50,1664]{2,1,0:T(8,128)(2,1)S(1)} collective-permute-done((bf16[2,50,1664]{2,1,0:T(8,128)(2,1)S(1)}, bf16[2,50,1664]{2,1,0:T(8,128)(2,1)S(1)}, u32[]{:S(2)}, u32[]{:S(2)}) %collective-permute-start.6) | collective-permute-done | bytes 332832 | tf_op jit(solution)/shard_map/ppermute | solution.py:817
  352.1 2.4 collective-permute-start.7
  354.6 7.8 %collective-permute-done.7 = bf16[50,1664]{1,0:T(8,128)(2,1)S(1)} collective-permute-done((bf16[50,1664]{1,0:T(8,128)(2,1)S(1)}, bf16[50,1664]{1,0:T(8,128)(2,1)S(1)}, u32[]{:S(2)}, u32[]{:S(2)}) %collective-permute-start.7) | collective-permute-done | bytes 166432 | tf_op jit(solution)/shard_map/ppermute | solution.py:817
  363.4 5.8 %collective-permute-done.8 = bf16[1,50,1664]{2,1,0:T(8,128)(2,1)S(1)} collective-permute-done((bf16[1,50,1664]{2,1,0:T(8,128)(2,1)S(1)}, bf16[1,50,1664]{2,1,0:T(8,128)(2,1)S(1)}, u32[]{:S(2)}, u32[]{:S(2)}) %collective-permute-start.8) | collective-permute-done | bytes 166432 | tf_op jit(solution)/shard_map/ppermute | solution.py:817
  377.5 2.0 reshape.351
  (215 shorter events, 56.9 us)
Async XLA Ops:
  0.7 52.9 %copy-start = (bf16[4,96,1024]{2,1,0:T(8,128)(2,1)S(1)}, bf16[4,96,1024]{2,1,0:T(8,128)(2,1)}, u32[]{:S(2)}) copy-start(bf16[4,96,1024]{2,1,0:T(8,128)(2,1)} %param.23) | copy-start | bytes 2359300
  0.7 14.8 %copy-start.35 = (f32[96]{0:T(128)S(1)}, f32[96]{0:T(128)}, u32[]{:S(2)}) copy-start(f32[96]{0:T(128)} %param.29) | copy-start | bytes 1156
  23.3 26.6 %all-to-all-start = ((bf16[8,4,96,128]{3,2,1,0:T(8,128)(2,1)}), bf16[8,4,96,128]{3,2,1,0:T(8,128)(2,1)S(1)}, u32[]{:S(2)}, u32[]{:S(2)}) async-start(bf16[8,4,96,128]{3,2,1,0:T(8,128)(2,1)} %bitcast.267), calls=%async_computation | async-start | bytes 1572864 | tf_op jit(solution)/shard_map/all_to_all | solution.py:878
  49.9 24.0 %all-to-all-start.1 = ((bf16[8,4,96,128]{3,2,1,0:T(8,128)(2,1)}), bf16[8,4,96,128]{3,2,1,0:T(8,128)(2,1)S(1)}, u32[]{:S(2)}, u32[]{:S(2)}) async-start(bf16[8,4,96,128]{3,2,1,0:T(8,128)(2,1)} %bitcast_bitcast_fusion.1), calls=%async_computation.1 | async-start | bytes 1572864 | tf_op jit(solution)/shard_map/all_to_all | solution.py:878
  53.5 23.9 %copy-start.27 = (f32[3200]{0:T(1024)S(1)}, f32[3200]{0:T(1024)}, u32[]{:S(2)}) copy-start(f32[3200]{0:T(1024)} %param.31) | copy-start | bytes 38404
  53.5 24.0 %copy-start.29 = (f32[1536]{0:T(1024)S(1)}, f32[1536]{0:T(1024)}, u32[]{:S(2)}) copy-start(f32[1536]{0:T(1024)} %param.33) | copy-start | bytes 18436
  53.5 24.0 %copy-start.31 = (f32[768]{0:T(1024)S(1)}, f32[768]{0:T(1024)}, u32[]{:S(2)}) copy-start(f32[768]{0:T(1024)} %param.35) | copy-start | bytes 9220
  53.6 24.0 %copy-start.32 = (f32[768]{0:T(1024)S(1)}, f32[768]{0:T(1024)}, u32[]{:S(2)}) copy-start(f32[768]{0:T(1024)} %param.38) | copy-start | bytes 9220
  53.6 24.0 %copy-start.33 = (f32[768]{0:T(1024)S(1)}, f32[768]{0:T(1024)}, u32[]{:S(2)}) copy-start(f32[768]{0:T(1024)} %param.39) | copy-start | bytes 9220
  53.6 24.0 %copy-start.30 = (f32[1536]{0:T(1024)S(1)}, f32[1536]{0:T(1024)}, u32[]{:S(2)}) copy-start(f32[1536]{0:T(1024)} %param.41) | copy-start | bytes 18436
  53.6 24.0 %copy-start.34 = (f32[768]{0:T(1024)S(1)}, f32[768]{0:T(1024)}, u32[]{:S(2)}) copy-start(f32[768]{0:T(1024)} %param.43) | copy-start | bytes 9220
  73.9 34.8 %all-to-all-start.3 = ((bf16[8,4,96,128]{3,2,1,0:T(8,128)(2,1)}), bf16[8,4,96,128]{3,2,1,0:T(8,128)(2,1)S(1)}, u32[]{:S(2)}, u32[]{:S(2)}) async-start(bf16[8,4,96,128]{3,2,1,0:T(8,128)(2,1)} %bitcast_bitcast_fusion), calls=%async_computation.3 | async-start | bytes 1572864 | tf_op jit(solution)/shard_map/all_to_all | solution.py:878
  123.6 43.0 %collective-permute-start.19 = (bf16[768,768]{1,0:T(8,128)(2,1)}, bf16[768,768]{1,0:T(8,128)(2,1)}, u32[]{:S(2)}, u32[]{:S(2)}) collective-permute-start(bf16[768,768]{1,0:T(8,128)(2,1)} %get-tuple-element.124), channel_id=1, source_target_pairs={{0,1},{1,0},{2,3},{3,2},{4,5},{5,4},{6,7},{7,6},{8,9},{9,8},{10,11... | collective-permute-start | bytes 3538952 | tf_op jit(solution)/shard_map/ppermute | solution.py:817
  123.7 64.2 %collective-permute-start.18 = (bf16[1536,384]{1,0:T(8,128)(2,1)}, bf16[1536,384]{1,0:T(8,128)(2,1)}, u32[]{:S(2)}, u32[]{:S(2)}) collective-permute-start(bf16[1536,384]{1,0:T(8,128)(2,1)} %get-tuple-element.122), channel_id=1, source_target_pairs={{0,1},{1,0},{2,3},{3,2},{4,5},{5,4},{6,7},{7,6},{8,9},{9,8},{10,11... | collective-permute-start | bytes 3538952 | tf_op jit(solution)/shard_map/ppermute | solution.py:817
  144.8 8.9 %copy-start.26 = (f32[1,6016]{1,0:T(1,128)S(1)}, f32[1,6016]{1,0:T(1,128)}, u32[]{:S(2)}) copy-start(f32[1,6016]{1,0:T(1,128)} %get-tuple-element.116) | copy-start | bytes 72196
  144.8 8.9 %copy-start.28 = (f32[1,3840]{1,0:T(1,128)S(1)}, f32[1,3840]{1,0:T(1,128)}, u32[]{:S(2)}) copy-start(f32[1,3840]{1,0:T(1,128)} %get-tuple-element.115) | copy-start | bytes 46084
  153.2 39.1 %collective-permute-start.11 = (bf16[768,768]{1,0:T(8,128)(2,1)}, bf16[768,768]{1,0:T(8,128)(2,1)}, u32[]{:S(2)}, u32[]{:S(2)}) collective-permute-start(bf16[768,768]{1,0:T(8,128)(2,1)} %get-tuple-element.120), channel_id=1, source_target_pairs={{0,1},{1,0},{2,3},{3,2},{4,5},{5,4},{6,7},{7,6},{8,9},{9,8},{10,11... | collective-permute-start | bytes 3538952 | tf_op jit(solution)/shard_map/ppermute | solution.py:817
  153.2 42.2 %collective-permute-start.10 = (bf16[1536,384]{1,0:T(8,128)(2,1)}, bf16[1536,384]{1,0:T(8,128)(2,1)}, u32[]{:S(2)}, u32[]{:S(2)}) collective-permute-start(bf16[1536,384]{1,0:T(8,128)(2,1)} %get-tuple-element.118), channel_id=1, source_target_pairs={{0,1},{1,0},{2,3},{3,2},{4,5},{5,4},{6,7},{7,6},{8,9},{9,8},{10,11... | collective-permute-start | bytes 3538952 | tf_op jit(solution)/shard_map/ppermute | solution.py:817
  154.0 11.6 %collective-permute-start.3 = (bf16[32,1664]{1,0:T(8,128)(2,1)S(1)}, bf16[32,1664]{1,0:T(8,128)(2,1)S(1)}, u32[]{:S(2)}, u32[]{:S(2)}) collective-permute-start(bf16[32,1664]{1,0:T(8,128)(2,1)S(1)} %reshape.348), channel_id=1, source_target_pairs={{0,1},{1,0},{2,3},{3,2},{4,5},{5,4},{6,7},{7,6},{8,9},{9,8},{10,11... | collective-permute-start | bytes 319496 | tf_op jit(solution)/shard_map/ppermute | solution.py:817
  154.1 26.7 %all-to-all-start.4 = ((bf16[8,4,96,128]{3,2,1,0:T(8,128)(2,1)}), bf16[8,4,96,128]{3,2,1,0:T(8,128)(2,1)S(1)}, u32[]{:S(2)}, u32[]{:S(2)}) async-start(bf16[8,4,96,128]{3,2,1,0:T(8,128)(2,1)} %get-tuple-element.100), calls=%async_computation.4 | async-start | bytes 1572864 | tf_op jit(solution)/shard_map/all_to_all | solution.py:878
  165.6 106.0 %collective-permute-start.2 = (bf16[768,1664]{1,0:T(8,128)(2,1)}, bf16[768,1664]{1,0:T(8,128)(2,1)}, u32[]{:S(2)}, u32[]{:S(2)}) collective-permute-start(bf16[768,1664]{1,0:T(8,128)(2,1)} %get-tuple-element.114), channel_id=1, source_target_pairs={{0,1},{1,0},{2,3},{3,2},{4,5},{5,4},{6,7},{7,6},{8,9},{9,8},{10,11... | collective-permute-start | bytes 7667720 | tf_op jit(solution)/shard_map/ppermute | solution.py:817
  180.9 7.0 %copy-start.5 = (bf16[8,4,96,128]{3,2,1,0:T(8,128)(2,1)}, bf16[8,4,96,128]{3,2,1,0:T(8,128)(2,1)S(1)}, u32[]{:S(2)}) copy-start(bf16[8,4,96,128]{3,2,1,0:T(8,128)(2,1)S(1)} %all-to-all-done.4) | copy-start | bytes 2359300
  180.9 24.2 %all-to-all-start.5 = ((bf16[8,4,96,128]{3,2,1,0:T(8,128)(2,1)}), bf16[8,4,96,128]{3,2,1,0:T(8,128)(2,1)}, u32[]{:S(2)}, u32[]{:S(2)}) async-start(bf16[8,4,96,128]{3,2,1,0:T(8,128)(2,1)} %get-tuple-element.108), calls=%async_computation.5 | async-start | bytes 1572864 | tf_op jit(solution)/shard_map/all_to_all | solution.py:878
  191.5 73.7 %collective-permute-start.20 = (bf16[2,2,2,192,384]{4,3,0,2,1:T(8,128)(2,1)}, bf16[2,2,2,192,384]{4,3,0,2,1:T(8,128)(2,1)}, u32[]{:S(2)}, u32[]{:S(2)}) collective-permute-start(bf16[2,2,2,192,384]{4,3,0,2,1:T(8,128)(2,1)} %pad_maximum_fusion.5), channel_id=1, source_target_pairs={{0,2},{1,3},{2,0},{3,1},{4,6},{5,7},{6,4},{7,5},{8,10},{9,11},{10,... | collective-permute-start | bytes 3538952 | tf_op jit(solution)/shard_map/ppermute | solution.py:817
  205.1 54.3 %all-to-all-start.2 = ((bf16[8,4,96,128]{3,2,1,0:T(8,128)(2,1)}), bf16[8,4,96,128]{3,2,1,0:T(8,128)(2,1)S(1)}, u32[]{:S(2)}, u32[]{:S(2)}) async-start(bf16[8,4,96,128]{3,2,1,0:T(8,128)(2,1)} %get-tuple-element.79), calls=%async_computation.2 | async-start | bytes 1572864 | tf_op jit(solution)/shard_map/all_to_all | solution.py:878
  211.2 56.5 %collective-permute-start.12 = (bf16[2,2,2,192,384]{4,3,2,1,0:T(8,128)(2,1)}, bf16[2,2,2,192,384]{4,3,2,1,0:T(8,128)(2,1)}, u32[]{:S(2)}, u32[]{:S(2)}) collective-permute-start(bf16[2,2,2,192,384]{4,3,2,1,0:T(8,128)(2,1)} %pad_maximum_fusion.3), channel_id=1, source_target_pairs={{0,4},{4,0},{8,12},{12,8},{16,20},{20,16},{24,28},{28,24},{1,5},{5... | collective-permute-start | bytes 3538952 | tf_op jit(solution)/shard_map/ppermute | solution.py:817
  222.0 12.6 %copy-start.25 = (f32[16,384]{1,0:T(8,128)S(1)}, f32[16,384]{1,0:T(8,128)}, u32[]{:S(2)}) copy-start(f32[16,384]{1,0:T(8,128)} %get-tuple-element.104) | copy-start | bytes 73732
  257.0 1.6 collective-permute-start
  258.6 6.0 %copy-start.22 = (f32[96,16]{0,1:T(8,128)S(1)}, f32[96,16]{0,1:T(8,128)}, u32[]{:S(2)}) copy-start(f32[96,16]{0,1:T(8,128)} %param.27) | copy-start | bytes 18436
  258.6 6.0 %copy-start.23 = (f32[96,16]{0,1:T(8,128)S(1)}, f32[96,16]{0,1:T(8,128)}, u32[]{:S(2)}) copy-start(f32[96,16]{0,1:T(8,128)} %param.26) | copy-start | bytes 18436
  258.6 6.0 %copy-start.24 = (f32[96,16]{0,1:T(8,128)S(1)}, f32[96,16]{0,1:T(8,128)}, u32[]{:S(2)}) copy-start(f32[96,16]{0,1:T(8,128)} %param.25) | copy-start | bytes 18436
  258.7 4.4 %collective-permute-start.1 = (f32[40,384]{1,0:T(8,128)S(1)}, f32[40,384]{1,0:T(8,128)}, u32[]{:S(2)}, u32[]{:S(2)}) collective-permute-start(f32[40,384]{1,0:T(8,128)S(1)} %add.254), channel_id=1, source_target_pairs={{0,2},{1,3},{2,0},{3,1},{4,6},{5,7},{6,4},{7,5},{8,10},{9,11},{10,... | collective-permute-start | bytes 184328 | tf_op jit(solution)/shard_map/ppermute | solution.py:817
  267.2 14.4 %collective-permute-start.21 = (bf16[2,2,192,384]{3,2,1,0:T(8,128)(2,1)S(1)}, bf16[2,2,192,384]{3,2,1,0:T(8,128)(2,1)S(1)}, u32[]{:S(2)}, u32[]{:S(2)}) collective-permute-start(bf16[2,2,192,384]{3,2,1,0:T(8,128)(2,1)S(1)} %copy.185), channel_id=1, source_target_pairs={{0,4},{4,0},{8,12},{12,8},{16,20},{20,16},{24,28},{28,24},{1,5},{5... | collective-permute-start | bytes 1769480 | tf_op jit(solution)/shard_map/ppermute | solution.py:817
  269.6 16.1 %collective-permute-start.13 = (bf16[2,2,192,384]{3,2,1,0:T(8,128)(2,1)S(1)}, bf16[2,2,192,384]{3,2,1,0:T(8,128)(2,1)S(1)}, u32[]{:S(2)}, u32[]{:S(2)}) collective-permute-start(bf16[2,2,192,384]{3,2,1,0:T(8,128)(2,1)S(1)} %fusion.17), channel_id=1, source_target_pairs={{0,2},{1,3},{2,0},{3,1},{4,6},{5,7},{6,4},{7,5},{8,10},{9,11},{10,... | collective-permute-start | bytes 1769480 | tf_op jit(solution)/shard_map/ppermute | solution.py:817
  281.7 11.4 %collective-permute-start.22 = (bf16[2,192,384]{2,1,0:T(8,128)(2,1)S(1)}, bf16[2,192,384]{2,1,0:T(8,128)(2,1)S(1)}, u32[]{:S(2)}, u32[]{:S(2)}) collective-permute-start(bf16[2,192,384]{2,1,0:T(8,128)(2,1)S(1)} %get-tuple-element.140), channel_id=1, source_target_pairs={{0,8},{4,12},{8,0},{12,4},{16,24},{20,28},{24,16},{28,20},{1,9},{5... | collective-permute-start | bytes 884744 | tf_op jit(solution)/shard_map/ppermute | solution.py:817
  285.0 33.9 %collective-permute-start.4 = (bf16[2,2,2,50,1664]{4,2,3,1,0:T(2,128)(2,1)S(1)}, bf16[2,2,2,50,1664]{4,2,3,1,0:T(2,128)(2,1)S(1)}, u32[]{:S(2)}, u32[]{:S(2)}) collective-permute-start(bf16[2,2,2,50,1664]{4,2,3,1,0:T(2,128)(2,1)S(1)} %pad_maximum_fusion), channel_id=1, source_target_pairs={{0,2},{1,3},{2,0},{3,1},{4,6},{5,7},{6,4},{7,5},{8,10},{9,11},{10,... | collective-permute-start | bytes 3993608 | tf_op jit(solution)/shard_map/ppermute | solution.py:817
  285.9 10.8 %collective-permute-start.14 = (bf16[2,192,384]{2,1,0:T(8,128)(2,1)S(1)}, bf16[2,192,384]{2,1,0:T(8,128)(2,1)S(1)}, u32[]{:S(2)}, u32[]{:S(2)}) collective-permute-start(bf16[2,192,384]{2,1,0:T(8,128)(2,1)S(1)} %get-tuple-element.152), channel_id=1, source_target_pairs={{0,8},{4,12},{8,0},{12,4},{16,24},{20,28},{24,16},{28,20},{1,9},{5... | collective-permute-start | bytes 884744 | tf_op jit(solution)/shard_map/ppermute | solution.py:817
  293.2 12.4 %collective-permute-start.23 = (bf16[192,384]{1,0:T(8,128)(2,1)S(1)}, bf16[192,384]{1,0:T(8,128)(2,1)S(1)}, u32[]{:S(2)}, u32[]{:S(2)}) collective-permute-start(bf16[192,384]{1,0:T(8,128)(2,1)S(1)} %fusion.42), channel_id=1, source_target_pairs={{0,16},{4,20},{8,24},{12,28},{16,0},{20,4},{24,8},{28,12},{1,17},{... | collective-permute-start | bytes 442376 | tf_op jit(solution)/shard_map/ppermute | solution.py:817
  296.8 10.4 %collective-permute-start.15 = (bf16[192,384]{1,0:T(8,128)(2,1)S(1)}, bf16[192,384]{1,0:T(8,128)(2,1)S(1)}, u32[]{:S(2)}, u32[]{:S(2)}) collective-permute-start(bf16[192,384]{1,0:T(8,128)(2,1)S(1)} %fusion.39), channel_id=1, source_target_pairs={{0,16},{4,20},{8,24},{12,28},{16,0},{20,4},{24,8},{28,12},{1,17},{... | collective-permute-start | bytes 442376 | tf_op jit(solution)/shard_map/ppermute | solution.py:817
  305.7 13.1 %collective-permute-start.24 = (bf16[1,192,384]{2,1,0:T(8,128)(2,1)S(1)}, bf16[1,192,384]{2,1,0:T(8,128)(2,1)S(1)}, u32[]{:S(2)}, u32[]{:S(2)}) collective-permute-start(bf16[1,192,384]{2,1,0:T(8,128)(2,1)S(1)} %fusion.41), channel_id=1, source_target_pairs={{0,2},{1,3},{2,0},{3,1},{4,6},{5,7},{6,4},{7,5},{8,10},{9,11},{10,... | collective-permute-start | bytes 442376 | tf_op jit(solution)/shard_map/ppermute | solution.py:817
  307.3 16.1 %collective-permute-start.16 = (bf16[1,192,384]{2,1,0:T(8,128)(2,1)S(1)}, bf16[1,192,384]{2,1,0:T(8,128)(2,1)S(1)}, u32[]{:S(2)}, u32[]{:S(2)}) collective-permute-start(bf16[1,192,384]{2,1,0:T(8,128)(2,1)S(1)} %fusion.38), channel_id=1, source_target_pairs={{0,2},{1,3},{2,0},{3,1},{4,6},{5,7},{6,4},{7,5},{8,10},{9,11},{10,... | collective-permute-start | bytes 442376 | tf_op jit(solution)/shard_map/ppermute | solution.py:817
  318.9 4.8 %collective-permute-start.25 = (bf16[2,192,384]{2,1,0:T(8,128)(2,1)S(1)}, bf16[2,192,384]{2,1,0:T(8,128)(2,1)S(1)}, u32[]{:S(2)}, u32[]{:S(2)}) collective-permute-start(bf16[2,192,384]{2,1,0:T(8,128)(2,1)S(1)} %maximum_bitcast_fusion.2), channel_id=1, source_target_pairs={{0,1},{1,0},{2,3},{3,2},{4,5},{5,4},{6,7},{7,6},{8,9},{9,8},{10,11... | collective-permute-start | bytes 884744 | tf_op jit(solution)/shard_map/ppermute | solution.py:817
  322.6 17.4 %collective-permute-start.5 = (bf16[2,2,50,1664]{3,1,2,0:T(2,128)(2,1)S(1)}, bf16[2,2,50,1664]{3,1,2,0:T(2,128)(2,1)S(1)}, u32[]{:S(2)}, u32[]{:S(2)}) collective-permute-start(bf16[2,2,50,1664]{3,1,2,0:T(2,128)(2,1)S(1)} %copy.158), channel_id=1, source_target_pairs={{0,4},{4,0},{8,12},{12,8},{16,20},{20,16},{24,28},{28,24},{1,5},{5... | collective-permute-start | bytes 1996808 | tf_op jit(solution)/shard_map/ppermute | solution.py:817
  323.4 39.9 %collective-permute-start.17 = (bf16[2,192,384]{2,1,0:T(8,128)(2,1)S(1)}, bf16[2,192,384]{2,1,0:T(8,128)(2,1)S(1)}, u32[]{:S(2)}, u32[]{:S(2)}) collective-permute-start(bf16[2,192,384]{2,1,0:T(8,128)(2,1)S(1)} %maximum_bitcast_fusion.1), channel_id=1, source_target_pairs={{0,1},{1,0},{2,3},{3,2},{4,5},{5,4},{6,7},{7,6},{8,9},{9,8},{10,11... | collective-permute-start | bytes 884744 | tf_op jit(solution)/shard_map/ppermute | solution.py:817
  341.7 10.3 %collective-permute-start.6 = (bf16[2,50,1664]{2,1,0:T(8,128)(2,1)S(1)}, bf16[2,50,1664]{2,1,0:T(8,128)(2,1)S(1)}, u32[]{:S(2)}, u32[]{:S(2)}) collective-permute-start(bf16[2,50,1664]{2,1,0:T(8,128)(2,1)S(1)} %fusion.22), channel_id=1, source_target_pairs={{0,8},{4,12},{8,0},{12,4},{16,24},{20,28},{24,16},{28,20},{1,9},{5... | collective-permute-start | bytes 998408 | tf_op jit(solution)/shard_map/ppermute | solution.py:817
  352.1 10.3 %collective-permute-start.7 = (bf16[50,1664]{1,0:T(8,128)(2,1)S(1)}, bf16[50,1664]{1,0:T(8,128)(2,1)S(1)}, u32[]{:S(2)}, u32[]{:S(2)}) collective-permute-start(bf16[50,1664]{1,0:T(8,128)(2,1)S(1)} %fusion.36), channel_id=1, source_target_pairs={{0,16},{4,20},{8,24},{12,28},{16,0},{20,4},{24,8},{28,12},{1,17},{... | collective-permute-start | bytes 499208 | tf_op jit(solution)/shard_map/ppermute | solution.py:817
  362.5 6.6 %collective-permute-start.8 = (bf16[1,50,1664]{2,1,0:T(8,128)(2,1)S(1)}, bf16[1,50,1664]{2,1,0:T(8,128)(2,1)S(1)}, u32[]{:S(2)}, u32[]{:S(2)}) collective-permute-start(bf16[1,50,1664]{2,1,0:T(8,128)(2,1)S(1)} %fusion.35), channel_id=1, source_target_pairs={{0,2},{1,3},{2,0},{3,1},{4,6},{5,7},{6,4},{7,5},{8,10},{9,11},{10,... | collective-permute-start | bytes 499208 | tf_op jit(solution)/shard_map/ppermute | solution.py:817
  369.2 6.1 %collective-permute-start.9 = (bf16[2,50,1664]{2,1,0:T(8,128)(2,1)S(1)}, bf16[2,50,1664]{2,1,0:T(8,128)(2,1)S(1)}, u32[]{:S(2)}, u32[]{:S(2)}) collective-permute-start(bf16[2,50,1664]{2,1,0:T(8,128)(2,1)S(1)} %maximum_bitcast_fusion), channel_id=1, source_target_pairs={{0,1},{1,0},{2,3},{3,2},{4,5},{5,4},{6,7},{7,6},{8,9},{9,8},{10,11... | collective-permute-start | bytes 998408 | tf_op jit(solution)/shard_map/ppermute | solution.py:817
  (21 other events, 58.6 us)
